TPU v7x, 256 devices: a whole 4x4x8 slice. The times are simulated.
256 devices in a mesh: rep: 32 (over z, y), fsdp: 8 (over x, core).
Axes of the slice: x: 4, y: 4, z: 8, core: 2. Of those that a mesh axis runs over, the one named last changes fastest.
Arguments:
- local_params: bfloat16 [32, 256, 8192], P('rep', 'fsdp'), may hold values from -120 to 120
- base_params: bfloat16 [256, 8192], P('fsdp'), may hold values from -4 to 4
- momentum: float32 [256, 8192], P('fsdp'), may hold values from -4 to 4
Outputs:
- new_base: bfloat16 [256, 8192], replicated
- new_momentum: float32 [256, 8192], P('fsdp')
All inputs are finite; a program needn't handle non-finite values.
Results may differ from a plain program's by a relative error of at most 0.015.
Values may be sent and summed in bfloat16 or wider, within the bound.
No kernel may reach another device: no remote copies, remote signals or barrier semaphores. Data moves between devices by JAX's collectives and lax.ppermute only.
A program may use at most 64 MiB of HBM per device.

v0:
```python
import jax
import jax.numpy as jnp
from jax import lax
from jax.sharding import PartitionSpec as P

BLOCK = 32


floor_value = 0.5
spread_ratio = 3.0
code_peak = 6.0
outer_rate = 0.7
momentum_coef = 0.9


def encode(local_rows, base_rows):
    pseudo_grad = base_rows.astype(jnp.float32) - local_rows.astype(jnp.float32)
    blocks = pseudo_grad.reshape(pseudo_grad.shape[0], pseudo_grad.shape[1] // BLOCK, BLOCK)
    mean_square = jnp.mean(blocks * blocks, axis=2)
    block_scale = lax.optimization_barrier(
        (jnp.maximum(jnp.sqrt(mean_square), floor_value) / spread_ratio).astype(jnp.bfloat16)
    )
    ratios = blocks / block_scale.astype(jnp.float32)[:, :, None]
    quant_codes = lax.optimization_barrier(
        jnp.clip(ratios, -code_peak, code_peak).astype(jnp.bfloat16)
    )
    return (quant_codes, block_scale)


def dequantize(quant_codes, block_scale):
    values = quant_codes.astype(jnp.float32) * block_scale.astype(jnp.float32)[:, :, None]
    return values.reshape(values.shape[0], values.shape[1] * values.shape[2])


def outer_update(average, momentum, base_rows):
    new_momentum = momentum_coef * momentum + average
    new_base = (
        base_rows.astype(jnp.float32) - outer_rate * (average + momentum_coef * new_momentum)
    ).astype(jnp.bfloat16)
    return (new_base, new_momentum)


def shards(local_params, base_params, momentum):
    quant_codes, block_scale = encode(local_params[0], base_params)
    replicas = lax.axis_size("rep")
    summed = lax.psum(dequantize(quant_codes, block_scale).astype(jnp.bfloat16), "rep").astype(
        jnp.float32
    )
    new_base, new_momentum = outer_update(summed / replicas, momentum, base_params)
    gathered = lax.all_gather(new_base, "fsdp", axis=0, tiled=True)
    return (gathered, new_momentum)


def solution(mesh):
    in_specs = (P("rep", "fsdp", None), P("fsdp", None), P("fsdp", None))
    out_specs = (P(), P("fsdp", None))
    return jax.shard_map(shards, mesh=mesh, in_specs=in_specs, out_specs=out_specs, check_vma=False)
```

profile of v0, /device:TPU:1, one launch (start us, length us, event | category | flops | bytes accessed | tf_op | source)
XLA Modules:
  0.0 218.6 jit_solution(9770064229030968245)
XLA Ops:
  7.2 0.0 all-reduce.2.cloned.1.call-start
  7.2 1.3 convert_subtract_fusion.1
  8.5 2.7 %reshape.12 = f32[32,256,32]{2,1,0:T(8,128)} reshape(f32[32,8192]{1,0:T(8,128)S(1)} %convert_subtract_fusion.1) | data formatting | bytes 2097152 | tf_op jit(solution)/shard_map/reshape | solution.py:18
  11.2 0.0 copy-start
  11.2 3.5 %multiply_reduce_fusion = f32[32,256]{1,0:T(8,128)S(1)} fusion(f32[32,256,32]{2,1,0:T(8,128)} %reshape.12), kind=kLoop, calls=%fused_computation.2 | loop fusion | flops 516096 | bytes 1081344 | tf_op jit(solution)/shard_map/reduce_sum | solution.py:19
  14.8 0.0 copy-done
  14.8 1.4 clamp_convert_fusion
  16.2 0.0 copy-start.1
  16.2 1.4 multiply_convert_fusion
  17.6 3.0 %convert_element_type.43 = bf16[32,8192]{1,0:T(8,128)(2,1)} reshape(bf16[32,256,32]{2,1,0:T(8,128)(2,1)S(1)} %multiply_convert_fusion) | data formatting | bytes 1048576 | tf_op jit(solution)/shard_map/convert_element_type | solution.py:46
  20.6 0.0 all-reduce.2.cloned.1.call-update
  20.6 0.0 all-gather.2.cloned.1.call-start
  20.7 146.9 %all-reduce.2.cloned.1.call-done = bf16[32,8192]{1,0:T(8,128)(2,1)} async-done(((bf16[32,8192]{1,0:T(8,128)(2,1)}), bf16[32,8192]{1,0:T(8,128)(2,1)}) %all-reduce.2.cloned.1.call-update) | async-done | bytes 524304 | tf_op jit(solution)/shard_map/psum | solution.py:46
  167.6 0.0 copy-done.1
  167.6 2.8 %fusion = (bf16[32,8192]{1,0:T(8,128)(2,1)}, f32[32,8192]{1,0:T(8,128)}) fusion(bf16[32,8192]{1,0:T(8,128)(2,1)S(1)} %copy-done.1, bf16[32,8192]{1,0:T(8,128)(2,1)} %all-reduce.2.cloned.1.call-done, f32[32,8192]{1,0:T(8,128)} %param.5), kind=kLoop, calls=%fused_computation.5 | loop fusion | flops 2621440 | bytes 3670016 | tf_op jit(solution)/shard_map/convert_element_type | solution.py:39
  170.4 0.0 all-gather.2.cloned.1.call-update
  170.5 36.7 %all-gather.2.cloned.1.call-done = bf16[256,8192]{1,0:T(8,128)(2,1)} async-done(((bf16[32,8192]{1,0:T(8,128)(2,1)}), bf16[256,8192]{1,0:T(8,128)(2,1)}) %all-gather.2.cloned.1.call-update) | async-done | bytes 4194320 | tf_op jit(solution)/shard_map/all_gather | solution.py:50
  207.1 4.6 %copy.7 = bf16[256,8192]{1,0:T(8,128)(2,1)} copy(bf16[256,8192]{1,0:T(8,128)(2,1)} %all-gather.2.cloned.1.call-done) | data formatting | bytes 8388608
  (2 shorter events, 0.0 us)
Async XLA Ops:
  7.2 160.4 %all-reduce.2.cloned.1.call-start = ((), (), s32[]{:S(2)}) async-start(), calls=%async_computation | async-start | bytes 1048576 | tf_op jit(solution)/shard_map/psum | solution.py:46
  11.2 3.5 %copy-start = (f32[32,256,32]{2,1,0:T(8,128)S(1)}, f32[32,256,32]{2,1,0:T(8,128)}, u32[]{:S(2)}) copy-start(f32[32,256,32]{2,1,0:T(8,128)} %reshape.12) | copy-start | bytes 3145732
  16.2 151.4 %copy-start.1 = (bf16[32,8192]{1,0:T(8,128)(2,1)S(1)}, bf16[32,8192]{1,0:T(8,128)(2,1)}, u32[]{:S(2)}) copy-start(bf16[32,8192]{1,0:T(8,128)(2,1)} %param.4) | copy-start | bytes 1572868
  20.6 186.5 %all-gather.2.cloned.1.call-start = ((), (), s32[]{:S(2)}) async-start(), calls=%async_computation.1 | async-start | bytes 4718592 | tf_op jit(solution)/shard_map/all_gather | solution.py:50
Sparse Core Ops, SparseCore 0:
  20.8 146.7 all-reduce.1
  170.6 36.5 all-gather.1
where the time goes:
time: 219 us
  waiting for transfers between devices  184 us (84%)
  between operations  14.1 us (6%)
  other arithmetic  10.5 us (5%)
  local copies, waits for them, and re-layouts  10.3 us (5%)
    psum x1, waiting for transfers between devices, shards(): lax.psum(dequantize(quant_codes, block_scale).astype(jnp.bfloat16), 'rep')  147 us
    all_gather x1, waiting for transfers between devices, shards(): gathered = lax.all_gather(new_base, 'fsdp', axis=0, tiled=True)  36.7 us
    unnamed x5, local copies, waits for them, and re-layouts  4.65 us
  transfers between devices with their start and end apart: 2, of which 2 were waited for; matrix products, arithmetic and copies ran while one was open for 0% of the time, Pallas kernels for 0%

commit v1 on v0

v1 whole, which is shorter than its diff:
```python
import jax
import jax.numpy as jnp
from jax import lax
from jax.experimental import pallas as pl
from jax.experimental.pallas import tpu as pltpu
from jax.sharding import Mesh, PartitionSpec as P

BLOCK = 32

floor_value = 0.5
spread_ratio = 3.0
code_peak = 6.0
outer_rate = 0.7
momentum_coef = 0.9

ROWS = 32
HALF = 16
COLS = 8192
PIECES = 4
WIDE = COLS // PIECES
LANES = 128


def encode_kernel(local_ref, base_ref, out_ref):
    lane = lax.broadcasted_iota(jnp.int32, (LANES, LANES), 0) // BLOCK
    lane_t = lax.broadcasted_iota(jnp.int32, (LANES, LANES), 1) // BLOCK
    same_block = jnp.where(lane == lane_t, 1.0 / BLOCK, 0.0).astype(jnp.float32)
    for half in range(2):
        for piece in range(PIECES):
            rows = pl.ds(half * HALF, HALF)
            cols = pl.ds(piece * WIDE, WIDE)
            grad = base_ref[rows, cols].astype(jnp.float32) - local_ref[0, rows, cols].astype(
                jnp.float32
            )
            tall = jnp.concatenate(
                [grad[:, k * LANES : (k + 1) * LANES] for k in range(WIDE // LANES)], axis=0
            )
            mean_square = jnp.dot(
                tall * tall,
                same_block,
                precision=lax.Precision.HIGHEST,
                preferred_element_type=jnp.float32,
            )
            scale = (jnp.maximum(jnp.sqrt(mean_square), floor_value) / spread_ratio).astype(
                jnp.bfloat16
            )
            limit = code_peak * scale.astype(jnp.float32)
            decoded = jnp.clip(tall, -limit, limit).astype(jnp.bfloat16)
            for k in range(WIDE // LANES):
                out_ref[half * PIECES + piece, :, k * LANES : (k + 1) * LANES] = decoded[
                    k * HALF : (k + 1) * HALF
                ]


def encode(local_params, base_rows):
    return pl.pallas_call(
        encode_kernel,
        out_shape=jax.ShapeDtypeStruct((2 * PIECES, HALF, WIDE), jnp.bfloat16),
        name="encode",
    )(local_params, base_rows)


def update_kernel(average_ref, base_ref, momentum_ref, first_ref, second_ref, new_momentum_ref):
    for half, new_base_ref in ((0, first_ref), (1, second_ref)):
        for piece in range(PIECES):
            rows = pl.ds(half * HALF, HALF)
            cols = pl.ds(piece * WIDE, WIDE)
            average = average_ref[half * PIECES + piece].astype(jnp.float32)
            new_momentum = momentum_coef * momentum_ref[rows, cols] + average
            new_momentum_ref[rows, cols] = new_momentum
            new_base_ref[:, cols] = (
                base_ref[rows, cols].astype(jnp.float32)
                - outer_rate * (average + momentum_coef * new_momentum)
            ).astype(jnp.bfloat16)


def outer_update(average, base_rows, momentum):
    part = jax.ShapeDtypeStruct((HALF, COLS), jnp.bfloat16)
    return pl.pallas_call(
        update_kernel,
        out_shape=(part, part, jax.ShapeDtypeStruct((ROWS, COLS), jnp.float32)),
        name="outer_update",
    )(average, base_rows, momentum)


def assemble_kernel(place_ref, *refs):
    parts, out_ref, sems = refs[:16], refs[16], refs[17]
    copies = []
    for k in range(16):
        start = pl.multiple_of(place_ref[k] * HALF, HALF)
        copies.append(
            pltpu.make_async_copy(parts[k], out_ref.at[pl.ds(start, HALF), :], sems.at[k])
        )
    for copy in copies:
        copy.start()
    for copy in copies:
        copy.wait()


def assemble(places, parts):
    return pl.pallas_call(
        assemble_kernel,
        out_shape=jax.ShapeDtypeStruct((16 * HALF, COLS), jnp.bfloat16),
        in_specs=[pl.BlockSpec(memory_space=pltpu.SMEM)]
        + [pl.BlockSpec(memory_space=pl.ANY)] * 16,
        out_specs=pl.BlockSpec(memory_space=pl.ANY),
        scratch_shapes=[pltpu.SemaphoreType.DMA((16,))],
        name="assemble",
    )(places, *parts)


def ring(n, step):
    return [(i, (i + step) % n) for i in range(n)]


def shards(local_params, base_params, momentum):
    decoded = encode(local_params, base_params)

    near = ("zl", "y")
    received = lax.all_to_all(decoded, near, 0, 0, tiled=True)
    partial = jnp.sum(received.astype(jnp.float32), axis=0).astype(jnp.bfloat16)

    others = [lax.ppermute(partial, "zh", ring(4, k)) for k in (1, 2, 3)]
    one, two, three = [value.astype(jnp.float32) for value in others]
    total = (partial.astype(jnp.float32) + two) + (one + three)
    average = (total / 32).astype(jnp.bfloat16)

    gathered = lax.all_to_all(
        jnp.broadcast_to(average[None], (8,) + average.shape), near, 0, 0, tiled=True
    )

    first, second, new_momentum = outer_update(gathered, base_params, momentum)

    left = [lax.ppermute(half, "x", ring(4, 1)) for half in (first, second)]
    right = [lax.ppermute(half, "x", ring(4, 3)) for half in (second, first)]
    far = [lax.ppermute(left[0], "x", ring(4, 1)), lax.ppermute(right[0], "x", ring(4, 3))]
    mine = [first, second, left[0], left[1], right[1], right[0], far[0], far[1]]
    theirs = [lax.ppermute(part, "core", ring(2, 1)) for part in mine]

    x, core = lax.axis_index("x"), lax.axis_index("core")
    at = [x, x, (x + 3) % 4, (x + 3) % 4, (x + 1) % 4, (x + 1) % 4, (x + 2) % 4, (x + 2) % 4]
    places = [(at[k] * 2 + c) * 2 + k % 2 for c in (core, 1 - core) for k in range(8)]
    new_base = assemble(jnp.stack(places).astype(jnp.int32), mine + theirs)
    return (new_base, new_momentum)


def solution(mesh):
    fine = Mesh(mesh.devices.reshape(4, 2, 4, 4, 2), ("zh", "zl", "y", "x", "core"))
    rep, fsdp = ("zh", "zl", "y"), ("x", "core")
    in_specs = (P(rep, fsdp, None), P(fsdp, None), P(fsdp, None))
    out_specs = (P(), P(fsdp, None))
    return jax.shard_map(shards, mesh=fine, in_specs=in_specs, out_specs=out_specs, check_vma=False)
```

time: 219 us -> 205 us (0.936)
  waiting for transfers between devices: 184 us -> 15.4 us
  Pallas kernels: 0 us -> 135 us
  starting transfers between devices: 0.08 us -> 27.3 us
  blocking collectives: 0 us -> 25.6 us
  between operations: 14.1 us -> 0.77 us
  other arithmetic: 10.5 us -> 0.12 us
  local copies, waits for them, and re-layouts: 10.3 us -> 0.81 us
    psum x1 -> x0, waiting for transfers between devices: 147 us -> none  [shards(): lax.psum(dequantize(quant_codes, block_scale).astype(jnp.bfloat16), 'rep')]
    pallas_call x0 -> x3, Pallas kernels: none -> 135 us  [the longest x1 129 us: assemble(): pl.pallas_call(assemble_kernel, out_shape=jax.ShapeDtypeStruct((16 * HALF...]
    all_gather x1 -> x0, waiting for transfers between devices: 36.7 us -> none  [shards(): gathered = lax.all_gather(new_base, 'fsdp', axis=0, tiled=True)]
    ppermute x0 -> x17, starting transfers between devices: none -> 27.3 us  [the longest x8 10.4 us: shards(): theirs = [lax.ppermute(part, 'core', ring(2, 1)) for part in mine]]
    all_to_all x0 -> x2, blocking collectives: none -> 25.6 us  [the longest x1 15 us: shards(): received = lax.all_to_all(decoded, near, 0, 0, tiled=True)]
    ppermute x0 -> x17, waiting for transfers between devices: none -> 15.4 us  [the longest x2 5.14 us: shards(): right = [lax.ppermute(half, 'x', ring(4, 3)) for half in (second, first)]]
    convert_element_type x5 -> x1, other arithmetic: 5.7 us -> 0.04 us  [shards(): average = (total / 32).astype(jnp.bfloat16)]
    unnamed x5 -> x26, local copies, waits for them, and re-layouts: 4.65 us -> 0.13 us
  transfers between devices with their start and end apart: 2 -> 17, of which waited for: 2 -> 8; matrix products, arithmetic and copies ran while one was open for 0% -> 0% of each run, Pallas kernels for 0% -> 0%
where the time goes in v1:
time: 205 us
  Pallas kernels  135 us (66%)
  starting transfers between devices  27.3 us (13%)
  blocking collectives  25.6 us (12%)
  waiting for transfers between devices  15.4 us (8%)
    pallas_call x1, Pallas kernels, assemble(): pl.pallas_call(assemble_kernel, out_shape=jax.ShapeDtypeStruct((16 * HALF...  129 us
    all_to_all x1, blocking collectives, shards(): received = lax.all_to_all(decoded, near, 0, 0, tiled=True)  15 us
    all_to_all x1, blocking collectives, shards(): lax.all_to_all(jnp.broadcast_to(average[None], (8,) + average.shape), nea...  10.6 us
    ppermute x8, starting transfers between devices, shards(): theirs = [lax.ppermute(part, 'core', ring(2, 1)) for part in mine]  10.4 us
    ppermute x3, starting transfers between devices, shards(): others = [lax.ppermute(partial, 'zh', ring(4, k)) for k in (1, 2, 3)]  8.45 us
    ppermute x2, starting transfers between devices, shards(): right = [lax.ppermute(half, 'x', ring(4, 3)) for half in (second, first)]  5.15 us
    ppermute x2, waiting for transfers between devices, shards(): right = [lax.ppermute(half, 'x', ring(4, 3)) for half in (second, first)]  5.14 us
  transfers between devices with their start and end apart: 17, of which 8 were waited for; matrix products, arithmetic and copies ran while one was open for 0% of the time, Pallas kernels for 0%

profile of v1, /device:TPU:1, one launch (start us, length us, event | category | flops | bytes accessed | tf_op | source)
XLA Modules:
  0.0 205.0 jit_solution(12484069674173810320)
XLA Ops:
  0.6 3.2 %encode.1 = bf16[8,16,2048]{2,1,0:T(8,128)(2,1)} custom-call(bf16[1,32,8192]{2,1,0:T(8,128)(2,1)} %local_ref.1, bf16[32,8192]{1,0:T(8,128)(2,1)} %base_ref.3), custom_call_target="tpu_custom_call" | custom-call | tf_op jit(solution)/shard_map/encode/pallas_call | solution.py:56
  3.8 15.0 %all_to_all.10 = bf16[8,16,2048]{2,1,0:T(8,128)(2,1)S(1)} all-to-all(bf16[8,16,2048]{2,1,0:T(8,128)(2,1)} %encode.1), channel_id=1, replica_groups=mesh['zh'=4,'zl'=2,'y'=4,'x'=4,'core'=2] {'zl','y'}, dimensions={0} | all-to-all | bytes 1048576 | tf_op jit(solution)/shard_map/all_to_all | solution.py:120
  18.8 0.1 reduce_sum.12
  18.9 5.2 %collective-permute-start.2 = (bf16[16,2048]{1,0:T(8,128)(2,1)S(1)}, bf16[16,2048]{1,0:T(8,128)(2,1)S(1)}, u32[]{:S(2)}, u32[]{:S(2)}) collective-permute-start(bf16[16,2048]{1,0:T(8,128)(2,1)S(1)} %reduce_sum.12), channel_id=1, source_target_pairs={{0,192},{64,0},{128,64},{192,128},{1,193},{65,1},{129,65},{193,129... | collective-permute-start | bytes 196616 | tf_op jit(solution)/shard_map/ppermute | solution.py:123
  24.1 3.3 %collective-permute-start = (bf16[16,2048]{1,0:T(8,128)(2,1)S(1)}, bf16[16,2048]{1,0:T(8,128)(2,1)S(1)}, u32[]{:S(2)}, u32[]{:S(2)}) collective-permute-start(bf16[16,2048]{1,0:T(8,128)(2,1)S(1)} %reduce_sum.12), channel_id=1, source_target_pairs={{0,128},{64,192},{128,0},{192,64},{1,129},{65,193},{129,1},{193,65... | collective-permute-start | bytes 196616 | tf_op jit(solution)/shard_map/ppermute | solution.py:123
  27.4 2.2 %collective-permute-done.1 = bf16[16,2048]{1,0:T(8,128)(2,1)S(1)} collective-permute-done((bf16[16,2048]{1,0:T(8,128)(2,1)S(1)}, bf16[16,2048]{1,0:T(8,128)(2,1)S(1)}, u32[]{:S(2)}, u32[]{:S(2)}) %collective-permute-start.1) | collective-permute-done | bytes 65568 | tf_op jit(solution)/shard_map/ppermute | solution.py:123
  29.5 1.7 collective-permute-done
  31.3 10.6 %all_to_all.11.average_ref = bf16[8,16,2048]{2,1,0:T(8,128)(2,1)} all-to-all(bf16[8,16,2048]{2,1,0:T(8,128)(2,1)S(1)} %broadcast_in_dim.2), channel_id=1, replica_groups=mesh['zh'=4,'zl'=2,'y'=4,'x'=4,'core'=2] {'zl','y'}, dimensions={0} | all-to-all | bytes 1048576 | tf_op jit(solution)/shard_map/all_to_all | solution.py:128
  41.9 2.9 %outer_update.1 = (bf16[16,8192]{1,0:T(8,128)(2,1)}, bf16[16,8192]{1,0:T(8,128)(2,1)}, f32[32,8192]{1,0:T(8,128)}) custom-call(bf16[8,16,2048]{2,1,0:T(8,128)(2,1)} %all_to_all.11.average_ref, bf16[32,8192]{1,0:T(8,128)(2,1)} %base_ref.3, f32[32,8192]{1,0:T(8,128)} %momentum_ref.1), custom_call_target="tpu_custom_call" | custom-call | tf_op jit(solution)/shard_map/outer_update/pallas_call | solution.py:79
  44.8 5.6 %collective-permute-start.9 = (bf16[16,8192]{1,0:T(8,128)(2,1)}, bf16[16,8192]{1,0:T(8,128)(2,1)S(1)}, u32[]{:S(2)}, u32[]{:S(2)}) collective-permute-start(bf16[16,8192]{1,0:T(8,128)(2,1)} %get-tuple-element.5.refs_0_), channel_id=1, source_target_pairs={{0,1},{1,0},{2,3},{3,2},{4,5},{5,4},{6,7},{7,6},{8,9},{9,8},{10,11... | collective-permute-start | bytes 786440 | tf_op jit(solution)/shard_map/ppermute | solution.py:138
  50.3 2.5 %collective-permute-start.5 = (bf16[16,8192]{1,0:T(8,128)(2,1)}, bf16[16,8192]{1,0:T(8,128)(2,1)S(1)}, u32[]{:S(2)}, u32[]{:S(2)}) collective-permute-start(bf16[16,8192]{1,0:T(8,128)(2,1)} %get-tuple-element.5.refs_0_), channel_id=1, source_target_pairs={{0,6},{2,0},{4,2},{6,4},{1,7},{3,1},{5,3},{7,5},{8,14},{10,8},{12,... | collective-permute-start | bytes 786440 | tf_op jit(solution)/shard_map/ppermute | solution.py:135
  52.8 2.7 %collective-permute-start.6 = (bf16[16,8192]{1,0:T(8,128)(2,1)}, bf16[16,8192]{1,0:T(8,128)(2,1)S(1)}, u32[]{:S(2)}, u32[]{:S(2)}) collective-permute-start(bf16[16,8192]{1,0:T(8,128)(2,1)} %get-tuple-element.6.refs_1_), channel_id=1, source_target_pairs={{0,6},{2,0},{4,2},{6,4},{1,7},{3,1},{5,3},{7,5},{8,14},{10,8},{12,... | collective-permute-start | bytes 786440 | tf_op jit(solution)/shard_map/ppermute | solution.py:135
  55.5 0.8 collective-permute-start.10
  56.3 0.0 collective-permute-done.9.refs_8_
  56.4 2.5 %collective-permute-done.5.refs_4_ = bf16[16,8192]{1,0:T(8,128)(2,1)S(1)} collective-permute-done((bf16[16,8192]{1,0:T(8,128)(2,1)}, bf16[16,8192]{1,0:T(8,128)(2,1)S(1)}, u32[]{:S(2)}, u32[]{:S(2)}) %collective-permute-start.5) | collective-permute-done | bytes 262176 | tf_op jit(solution)/shard_map/ppermute | solution.py:135
  58.9 1.2 collective-permute-start.13
  60.1 1.8 collective-permute-done.3.refs_2_
  61.9 0.0 collective-permute-start.7
  61.9 2.6 %collective-permute-done.6.refs_5_ = bf16[16,8192]{1,0:T(8,128)(2,1)S(1)} collective-permute-done((bf16[16,8192]{1,0:T(8,128)(2,1)}, bf16[16,8192]{1,0:T(8,128)(2,1)S(1)}, u32[]{:S(2)}, u32[]{:S(2)}) %collective-permute-start.6) | collective-permute-done | bytes 262176 | tf_op jit(solution)/shard_map/ppermute | solution.py:135
  64.5 3.3 %collective-permute-start.8 = (bf16[16,8192]{1,0:T(8,128)(2,1)S(1)}, bf16[16,8192]{1,0:T(8,128)(2,1)S(1)}, u32[]{:S(2)}, u32[]{:S(2)}) collective-permute-start(bf16[16,8192]{1,0:T(8,128)(2,1)S(1)} %collective-permute-done.6.refs_5_), channel_id=1, source_target_pairs={{0,6},{2,0},{4,2},{6,4},{1,7},{3,1},{5,3},{7,5},{8,14},{10,8},{12,... | collective-permute-start | bytes 786440 | tf_op jit(solution)/shard_map/ppermute | solution.py:136
  67.8 1.1 collective-permute-start.11
  68.9 0.0 collective-permute-done.4.refs_3_
  68.9 0.4 collective-permute-start.14
  69.3 0.1 collective-permute-start.12
  69.4 3.7 %collective-permute-done.7.refs_6_ = bf16[16,8192]{1,0:T(8,128)(2,1)S(1)} collective-permute-done((bf16[16,8192]{1,0:T(8,128)(2,1)S(1)}, bf16[16,8192]{1,0:T(8,128)(2,1)S(1)}, u32[]{:S(2)}, u32[]{:S(2)}) %collective-permute-start.7) | collective-permute-done | bytes 262176 | tf_op jit(solution)/shard_map/ppermute | solution.py:136
  73.1 1.1 collective-permute-start.15
  74.2 0.1 collective-permute-start.16
  74.3 0.6 stack.67.place_ref
  75.0 0.4 collective-permute-done.15.refs_14_
  75.4 0.5 collective-permute-done.16.refs_15_
  76.0 0.1 copy-done.12
  76.1 129.0 %assemble.1 = bf16[256,8192]{1,0:T(8,128)(2,1)} custom-call(s32[16]{0:T(128)} %stack.67.place_ref, bf16[16,8192]{1,0:T(8,128)(2,1)} %get-tuple-element.5.refs_0_, bf16[16,8192]{1,0:T(8,128)(2,1)} %get-tuple-element.6.refs_1_, bf16[16,8192]{1,0:T(8,128)(2,1)} %copy-done.2, bf16[16,8192]{1,0:T(8,128)(2,1)} %copy-done.5, bf16[16,8192]{1,0:T(8,128)(2,1)} %copy-done.1, ...), custom_call_target="tpu_custom_call" | custom-call | tf_op jit(solution)/shard_map/assemble/pallas_call | solution.py:101
  (37 shorter events, 0.2 us)
Async XLA Ops:
  18.9 8.5 %collective-permute-start.2 = (bf16[16,2048]{1,0:T(8,128)(2,1)S(1)}, bf16[16,2048]{1,0:T(8,128)(2,1)S(1)}, u32[]{:S(2)}, u32[]{:S(2)}) collective-permute-start(bf16[16,2048]{1,0:T(8,128)(2,1)S(1)} %reduce_sum.12), channel_id=1, source_target_pairs={{0,192},{64,0},{128,64},{192,128},{1,193},{65,1},{129,65},{193,129... | collective-permute-start | bytes 196616 | tf_op jit(solution)/shard_map/ppermute | solution.py:123
  24.1 5.4 %collective-permute-start.1 = (bf16[16,2048]{1,0:T(8,128)(2,1)S(1)}, bf16[16,2048]{1,0:T(8,128)(2,1)S(1)}, u32[]{:S(2)}, u32[]{:S(2)}) collective-permute-start(bf16[16,2048]{1,0:T(8,128)(2,1)S(1)} %reduce_sum.12), channel_id=1, source_target_pairs={{0,64},{64,128},{128,192},{192,0},{1,65},{65,129},{129,193},{193,1... | collective-permute-start | bytes 196616 | tf_op jit(solution)/shard_map/ppermute | solution.py:123
  24.1 7.1 %collective-permute-start = (bf16[16,2048]{1,0:T(8,128)(2,1)S(1)}, bf16[16,2048]{1,0:T(8,128)(2,1)S(1)}, u32[]{:S(2)}, u32[]{:S(2)}) collective-permute-start(bf16[16,2048]{1,0:T(8,128)(2,1)S(1)} %reduce_sum.12), channel_id=1, source_target_pairs={{0,128},{64,192},{128,0},{192,64},{1,129},{65,193},{129,1},{193,65... | collective-permute-start | bytes 196616 | tf_op jit(solution)/shard_map/ppermute | solution.py:123
  44.8 11.6 %collective-permute-start.9 = (bf16[16,8192]{1,0:T(8,128)(2,1)}, bf16[16,8192]{1,0:T(8,128)(2,1)S(1)}, u32[]{:S(2)}, u32[]{:S(2)}) collective-permute-start(bf16[16,8192]{1,0:T(8,128)(2,1)} %get-tuple-element.5.refs_0_), channel_id=1, source_target_pairs={{0,1},{1,0},{2,3},{3,2},{4,5},{5,4},{6,7},{7,6},{8,9},{9,8},{10,11... | collective-permute-start | bytes 786440 | tf_op jit(solution)/shard_map/ppermute | solution.py:138
  50.3 8.5 %collective-permute-start.5 = (bf16[16,8192]{1,0:T(8,128)(2,1)}, bf16[16,8192]{1,0:T(8,128)(2,1)S(1)}, u32[]{:S(2)}, u32[]{:S(2)}) collective-permute-start(bf16[16,8192]{1,0:T(8,128)(2,1)} %get-tuple-element.5.refs_0_), channel_id=1, source_target_pairs={{0,6},{2,0},{4,2},{6,4},{1,7},{3,1},{5,3},{7,5},{8,14},{10,8},{12,... | collective-permute-start | bytes 786440 | tf_op jit(solution)/shard_map/ppermute | solution.py:135
  52.8 9.0 %collective-permute-start.3 = (bf16[16,8192]{1,0:T(8,128)(2,1)}, bf16[16,8192]{1,0:T(8,128)(2,1)S(1)}, u32[]{:S(2)}, u32[]{:S(2)}) collective-permute-start(bf16[16,8192]{1,0:T(8,128)(2,1)} %get-tuple-element.5.refs_0_), channel_id=1, source_target_pairs={{0,2},{2,4},{4,6},{6,0},{1,3},{3,5},{5,7},{7,1},{8,10},{10,12},{12... | collective-permute-start | bytes 786440 | tf_op jit(solution)/shard_map/ppermute | solution.py:134
  52.8 11.7 %collective-permute-start.6 = (bf16[16,8192]{1,0:T(8,128)(2,1)}, bf16[16,8192]{1,0:T(8,128)(2,1)S(1)}, u32[]{:S(2)}, u32[]{:S(2)}) collective-permute-start(bf16[16,8192]{1,0:T(8,128)(2,1)} %get-tuple-element.6.refs_1_), channel_id=1, source_target_pairs={{0,6},{2,0},{4,2},{6,4},{1,7},{3,1},{5,3},{7,5},{8,14},{10,8},{12,... | collective-permute-start | bytes 786440 | tf_op jit(solution)/shard_map/ppermute | solution.py:135
  55.5 12.3 %collective-permute-start.10 = (bf16[16,8192]{1,0:T(8,128)(2,1)}, bf16[16,8192]{1,0:T(8,128)(2,1)S(1)}, u32[]{:S(2)}, u32[]{:S(2)}) collective-permute-start(bf16[16,8192]{1,0:T(8,128)(2,1)} %get-tuple-element.6.refs_1_), channel_id=1, source_target_pairs={{0,1},{1,0},{2,3},{3,2},{4,5},{5,4},{6,7},{7,6},{8,9},{9,8},{10,11... | collective-permute-start | bytes 786440 | tf_op jit(solution)/shard_map/ppermute | solution.py:138
  56.4 19.5 %copy-start = (bf16[16,8192]{1,0:T(8,128)(2,1)}, bf16[16,8192]{1,0:T(8,128)(2,1)S(1)}, u32[]{:S(2)}) copy-start(bf16[16,8192]{1,0:T(8,128)(2,1)S(1)} %collective-permute-done.9.refs_8_) | copy-start | bytes 786436
  56.4 12.5 %collective-permute-start.4 = (bf16[16,8192]{1,0:T(8,128)(2,1)}, bf16[16,8192]{1,0:T(8,128)(2,1)S(1)}, u32[]{:S(2)}, u32[]{:S(2)}) collective-permute-start(bf16[16,8192]{1,0:T(8,128)(2,1)} %get-tuple-element.6.refs_1_), channel_id=1, source_target_pairs={{0,2},{2,4},{4,6},{6,0},{1,3},{3,5},{5,7},{7,1},{8,10},{10,12},{12... | collective-permute-start | bytes 786440 | tf_op jit(solution)/shard_map/ppermute | solution.py:134
  58.9 17.0 %copy-start.1 = (bf16[16,8192]{1,0:T(8,128)(2,1)}, bf16[16,8192]{1,0:T(8,128)(2,1)S(1)}, u32[]{:S(2)}) copy-start(bf16[16,8192]{1,0:T(8,128)(2,1)S(1)} %collective-permute-done.5.refs_4_) | copy-start | bytes 786436
  58.9 10.4 %collective-permute-start.13 = (bf16[16,8192]{1,0:T(8,128)(2,1)S(1)}, bf16[16,8192]{1,0:T(8,128)(2,1)S(1)}, u32[]{:S(2)}, u32[]{:S(2)}) collective-permute-start(bf16[16,8192]{1,0:T(8,128)(2,1)S(1)} %collective-permute-done.5.refs_4_), channel_id=1, source_target_pairs={{0,1},{1,0},{2,3},{3,2},{4,5},{5,4},{6,7},{7,6},{8,9},{9,8},{10,11... | collective-permute-start | bytes 786440 | tf_op jit(solution)/shard_map/ppermute | solution.py:138
  61.9 14.0 %copy-start.2 = (bf16[16,8192]{1,0:T(8,128)(2,1)}, bf16[16,8192]{1,0:T(8,128)(2,1)S(1)}, u32[]{:S(2)}) copy-start(bf16[16,8192]{1,0:T(8,128)(2,1)S(1)} %collective-permute-done.3.refs_2_) | copy-start | bytes 786436
  61.9 11.2 %collective-permute-start.7 = (bf16[16,8192]{1,0:T(8,128)(2,1)S(1)}, bf16[16,8192]{1,0:T(8,128)(2,1)S(1)}, u32[]{:S(2)}, u32[]{:S(2)}) collective-permute-start(bf16[16,8192]{1,0:T(8,128)(2,1)S(1)} %collective-permute-done.3.refs_2_), channel_id=1, source_target_pairs={{0,2},{2,4},{4,6},{6,0},{1,3},{3,5},{5,7},{7,1},{8,10},{10,12},{12... | collective-permute-start | bytes 786440 | tf_op jit(solution)/shard_map/ppermute | solution.py:136
  64.5 11.4 %copy-start.3 = (bf16[16,8192]{1,0:T(8,128)(2,1)}, bf16[16,8192]{1,0:T(8,128)(2,1)S(1)}, u32[]{:S(2)}) copy-start(bf16[16,8192]{1,0:T(8,128)(2,1)S(1)} %collective-permute-done.6.refs_5_) | copy-start | bytes 786436
  64.5 9.7 %collective-permute-start.8 = (bf16[16,8192]{1,0:T(8,128)(2,1)S(1)}, bf16[16,8192]{1,0:T(8,128)(2,1)S(1)}, u32[]{:S(2)}, u32[]{:S(2)}) collective-permute-start(bf16[16,8192]{1,0:T(8,128)(2,1)S(1)} %collective-permute-done.6.refs_5_), channel_id=1, source_target_pairs={{0,6},{2,0},{4,2},{6,4},{1,7},{3,1},{5,3},{7,5},{8,14},{10,8},{12,... | collective-permute-start | bytes 786440 | tf_op jit(solution)/shard_map/ppermute | solution.py:136
  67.8 8.1 %copy-start.4 = (bf16[16,8192]{1,0:T(8,128)(2,1)}, bf16[16,8192]{1,0:T(8,128)(2,1)S(1)}, u32[]{:S(2)}) copy-start(bf16[16,8192]{1,0:T(8,128)(2,1)S(1)} %collective-permute-done.10.refs_9_) | copy-start | bytes 786436
  67.8 7.2 %collective-permute-start.11 = (bf16[16,8192]{1,0:T(8,128)(2,1)S(1)}, bf16[16,8192]{1,0:T(8,128)(2,1)S(1)}, u32[]{:S(2)}, u32[]{:S(2)}) collective-permute-start(bf16[16,8192]{1,0:T(8,128)(2,1)S(1)} %collective-permute-done.3.refs_2_), channel_id=1, source_target_pairs={{0,1},{1,0},{2,3},{3,2},{4,5},{5,4},{6,7},{7,6},{8,9},{9,8},{10,11... | collective-permute-start | bytes 786440 | tf_op jit(solution)/shard_map/ppermute | solution.py:138
  68.9 7.0 %copy-start.5 = (bf16[16,8192]{1,0:T(8,128)(2,1)}, bf16[16,8192]{1,0:T(8,128)(2,1)S(1)}, u32[]{:S(2)}) copy-start(bf16[16,8192]{1,0:T(8,128)(2,1)S(1)} %collective-permute-done.4.refs_3_) | copy-start | bytes 786436
  68.9 6.1 %collective-permute-start.14 = (bf16[16,8192]{1,0:T(8,128)(2,1)S(1)}, bf16[16,8192]{1,0:T(8,128)(2,1)S(1)}, u32[]{:S(2)}, u32[]{:S(2)}) collective-permute-start(bf16[16,8192]{1,0:T(8,128)(2,1)S(1)} %collective-permute-done.6.refs_5_), channel_id=1, source_target_pairs={{0,1},{1,0},{2,3},{3,2},{4,5},{5,4},{6,7},{7,6},{8,9},{9,8},{10,11... | collective-permute-start | bytes 786440 | tf_op jit(solution)/shard_map/ppermute | solution.py:138
  69.3 6.6 %copy-start.6 = (bf16[16,8192]{1,0:T(8,128)(2,1)}, bf16[16,8192]{1,0:T(8,128)(2,1)S(1)}, u32[]{:S(2)}) copy-start(bf16[16,8192]{1,0:T(8,128)(2,1)S(1)} %collective-permute-done.13.refs_12_) | copy-start | bytes 786436
  69.3 5.7 %collective-permute-start.12 = (bf16[16,8192]{1,0:T(8,128)(2,1)S(1)}, bf16[16,8192]{1,0:T(8,128)(2,1)S(1)}, u32[]{:S(2)}, u32[]{:S(2)}) collective-permute-start(bf16[16,8192]{1,0:T(8,128)(2,1)S(1)} %collective-permute-done.4.refs_3_), channel_id=1, source_target_pairs={{0,1},{1,0},{2,3},{3,2},{4,5},{5,4},{6,7},{7,6},{8,9},{9,8},{10,11... | collective-permute-start | bytes 786440 | tf_op jit(solution)/shard_map/ppermute | solution.py:138
  73.1 2.8 %copy-start.7 = (bf16[16,8192]{1,0:T(8,128)(2,1)}, bf16[16,8192]{1,0:T(8,128)(2,1)S(1)}, u32[]{:S(2)}) copy-start(bf16[16,8192]{1,0:T(8,128)(2,1)S(1)} %collective-permute-done.7.refs_6_) | copy-start | bytes 786436
  73.1 2.3 %collective-permute-start.15 = (bf16[16,8192]{1,0:T(8,128)(2,1)S(1)}, bf16[16,8192]{1,0:T(8,128)(2,1)S(1)}, u32[]{:S(2)}, u32[]{:S(2)}) collective-permute-start(bf16[16,8192]{1,0:T(8,128)(2,1)S(1)} %collective-permute-done.7.refs_6_), channel_id=1, source_target_pairs={{0,1},{1,0},{2,3},{3,2},{4,5},{5,4},{6,7},{7,6},{8,9},{9,8},{10,11... | collective-permute-start | bytes 786440 | tf_op jit(solution)/shard_map/ppermute | solution.py:138
  74.2 1.7 copy-start.8
  74.2 1.7 collective-permute-start.16
  75.0 1.0 copy-start.9
  75.0 1.0 copy-start.10
  75.0 1.0 copy-start.11
  75.4 0.7 copy-start.12

commit v2 on v1

--- a/solution.py
+++ b/solution.py
@@ -19,6 +19,8 @@
 PIECES = 4
 WIDE = COLS // PIECES
 LANES = 128
+
+SMALL = pltpu.CompilerParams(vmem_limit_bytes=16 << 20)
 
 
 def encode_kernel(local_ref, base_ref, out_ref):
@@ -52,10 +54,15 @@
                 ]
 
 
+def in_vmem(value):
+    return pltpu.with_memory_space_constraint(value, pltpu.VMEM)
+
+
 def encode(local_params, base_rows):
     return pl.pallas_call(
         encode_kernel,
-        out_shape=jax.ShapeDtypeStruct((2 * PIECES, HALF, WIDE), jnp.bfloat16),
+        out_shape=pltpu.VMEM((2 * PIECES, HALF, WIDE), jnp.bfloat16),
+        compiler_params=SMALL,
         name="encode",
     )(local_params, base_rows)
 
@@ -75,12 +82,13 @@
 
 
 def outer_update(average, base_rows, momentum):
-    part = jax.ShapeDtypeStruct((HALF, COLS), jnp.bfloat16)
+    part = pltpu.VMEM((HALF, COLS), jnp.bfloat16)
     return pl.pallas_call(
         update_kernel,
         out_shape=(part, part, jax.ShapeDtypeStruct((ROWS, COLS), jnp.float32)),
+        compiler_params=SMALL,
         name="outer_update",
-    )(average, base_rows, momentum)
+    )(in_vmem(average), base_rows, momentum)
 
 
 def assemble_kernel(place_ref, *refs):
@@ -102,11 +110,12 @@
         assemble_kernel,
         out_shape=jax.ShapeDtypeStruct((16 * HALF, COLS), jnp.bfloat16),
         in_specs=[pl.BlockSpec(memory_space=pltpu.SMEM)]
-        + [pl.BlockSpec(memory_space=pl.ANY)] * 16,
+        + [pl.BlockSpec(memory_space=pltpu.VMEM)] * 16,
         out_specs=pl.BlockSpec(memory_space=pl.ANY),
         scratch_shapes=[pltpu.SemaphoreType.DMA((16,))],
+        compiler_params=SMALL,
         name="assemble",
-    )(places, *parts)
+    )(places, *[in_vmem(part) for part in parts])
 
 
 def ring(n, step):

time: 205 us -> 76.9 us (0.38)
  Pallas kernels: 135 us -> 5.58 us
    pallas_call x1, Pallas kernels: 129 us -> 3.25 us  [assemble(): pl.pallas_call(assemble_kernel, out_shape=jax.ShapeDtypeStruct((16 * HALF...]
where the time goes in v2:
time: 76.9 us; the launch traced here: 76.7 us
  starting transfers between devices  27.2 us (35%)
  blocking collectives  25.1 us (33%)
  waiting for transfers between devices  15.7 us (20%)
  Pallas kernels  5.58 us (7%)
  local copies, waits for them, and re-layouts  2.22 us (3%)
    all_to_all x1, blocking collectives, shards(): received = lax.all_to_all(decoded, near, 0, 0, tiled=True)  14.8 us
    all_to_all x1, blocking collectives, shards(): lax.all_to_all(jnp.broadcast_to(average[None], (8,) + average.shape), nea...  10.3 us
    ppermute x8, starting transfers between devices, shards(): theirs = [lax.ppermute(part, 'core', ring(2, 1)) for part in mine]  10.2 us
    ppermute x3, starting transfers between devices, shards(): others = [lax.ppermute(partial, 'zh', ring(4, k)) for k in (1, 2, 3)]  8.45 us
    ppermute x2, starting transfers between devices, shards(): right = [lax.ppermute(half, 'x', ring(4, 3)) for half in (second, first)]  5.15 us
    ppermute x2, waiting for transfers between devices, shards(): right = [lax.ppermute(half, 'x', ring(4, 3)) for half in (second, first)]  4.73 us
    ppermute x3, waiting for transfers between devices, shards(): others = [lax.ppermute(partial, 'zh', ring(4, k)) for k in (1, 2, 3)]  3.89 us
    ppermute x1, waiting for transfers between devices, shards(): lax.ppermute(left[0], 'x', ring(4, 1))  3.71 us
  transfers between devices with their start and end apart: 17, of which 8 were waited for; matrix products, arithmetic and copies ran while one was open for 0% of the time, Pallas kernels for 0%

profile of v2, /device:TPU:1, one launch (start us, length us, event | category | flops | bytes accessed | tf_op | source)
XLA Modules:
  0.0 76.7 jit_solution(11864726990296739962)
XLA Ops:
  0.6 1.0 %copy-done = bf16[32,8192]{1,0:T(8,128)(2,1)S(1)} copy-done((bf16[32,8192]{1,0:T(8,128)(2,1)S(1)}, bf16[32,8192]{1,0:T(8,128)(2,1)}, u32[]{:S(2)}) %copy-start) | copy-done | bytes 524312
  1.7 1.0 %copy-done.3 = bf16[1,32,8192]{2,1,0:T(8,128)(2,1)S(1)} copy-done((bf16[1,32,8192]{2,1,0:T(8,128)(2,1)S(1)}, bf16[1,32,8192]{2,1,0:T(8,128)(2,1)}, u32[]{:S(2)}) %copy-start.3) | copy-done | bytes 524312
  2.7 1.2 %encode.1 = bf16[8,16,2048]{2,1,0:T(8,128)(2,1)S(1)} custom-call(bf16[1,32,8192]{2,1,0:T(8,128)(2,1)S(1)} %copy-done.3, bf16[32,8192]{1,0:T(8,128)(2,1)S(1)} %copy-done), custom_call_target="tpu_custom_call" | custom-call | tf_op jit(solution)/shard_map/encode/pallas_call | solution.py:62
  3.9 14.8 %all_to_all.10 = bf16[8,16,2048]{2,1,0:T(8,128)(2,1)S(1)} all-to-all(bf16[8,16,2048]{2,1,0:T(8,128)(2,1)S(1)} %encode.1), channel_id=1, replica_groups=mesh['zh'=4,'zl'=2,'y'=4,'x'=4,'core'=2] {'zl','y'}, dimensions={0} | all-to-all | bytes 1048576 | tf_op jit(solution)/shard_map/all_to_all | solution.py:129
  18.7 0.1 reduce_sum.12
  18.8 5.2 %collective-permute-start.2 = (bf16[16,2048]{1,0:T(8,128)(2,1)S(1)}, bf16[16,2048]{1,0:T(8,128)(2,1)S(1)}, u32[]{:S(2)}, u32[]{:S(2)}) collective-permute-start(bf16[16,2048]{1,0:T(8,128)(2,1)S(1)} %reduce_sum.12), channel_id=1, source_target_pairs={{0,192},{64,0},{128,64},{192,128},{1,193},{65,1},{129,65},{193,129... | collective-permute-start | bytes 196616 | tf_op jit(solution)/shard_map/ppermute | solution.py:132
  24.0 3.3 %collective-permute-start = (bf16[16,2048]{1,0:T(8,128)(2,1)S(1)}, bf16[16,2048]{1,0:T(8,128)(2,1)S(1)}, u32[]{:S(2)}, u32[]{:S(2)}) collective-permute-start(bf16[16,2048]{1,0:T(8,128)(2,1)S(1)} %reduce_sum.12), channel_id=1, source_target_pairs={{0,128},{64,192},{128,0},{192,64},{1,129},{65,193},{129,1},{193,65... | collective-permute-start | bytes 196616 | tf_op jit(solution)/shard_map/ppermute | solution.py:132
  27.2 0.0 collective-permute-done.2
  27.3 2.2 %collective-permute-done.1 = bf16[16,2048]{1,0:T(8,128)(2,1)S(1)} collective-permute-done((bf16[16,2048]{1,0:T(8,128)(2,1)S(1)}, bf16[16,2048]{1,0:T(8,128)(2,1)S(1)}, u32[]{:S(2)}, u32[]{:S(2)}) %collective-permute-start.1) | collective-permute-done | bytes 65568 | tf_op jit(solution)/shard_map/ppermute | solution.py:132
  29.4 1.7 %collective-permute-done = bf16[16,2048]{1,0:T(8,128)(2,1)S(1)} collective-permute-done((bf16[16,2048]{1,0:T(8,128)(2,1)S(1)}, bf16[16,2048]{1,0:T(8,128)(2,1)S(1)}, u32[]{:S(2)}, u32[]{:S(2)}) %collective-permute-start) | collective-permute-done | bytes 65568 | tf_op jit(solution)/shard_map/ppermute | solution.py:132
  31.2 10.3 %all_to_all.11.average_ref = bf16[8,16,2048]{2,1,0:T(8,128)(2,1)S(1)} all-to-all(bf16[8,16,2048]{2,1,0:T(8,128)(2,1)S(1)} %broadcast_in_dim.2), channel_id=1, replica_groups=mesh['zh'=4,'zl'=2,'y'=4,'x'=4,'core'=2] {'zl','y'}, dimensions={0} | all-to-all | bytes 1048576 | tf_op jit(solution)/shard_map/all_to_all | solution.py:137
  41.6 1.1 %outer_update.1 = (bf16[16,8192]{1,0:T(8,128)(2,1)S(1)}, bf16[16,8192]{1,0:T(8,128)(2,1)S(1)}, f32[32,8192]{1,0:T(8,128)}) custom-call(bf16[8,16,2048]{2,1,0:T(8,128)(2,1)S(1)} %all_to_all.11.average_ref, bf16[32,8192]{1,0:T(8,128)(2,1)S(1)} %copy-done.1, f32[32,8192]{1,0:T(8,128)S(1)} %copy-done.2), custom_call_target="tpu_custom_call" | custom-call | tf_op jit(solution)/shard_map/outer_update/pallas_call | solution.py:86
  42.7 5.4 %collective-permute-start.9 = (bf16[16,8192]{1,0:T(8,128)(2,1)S(1)}, bf16[16,8192]{1,0:T(8,128)(2,1)S(1)}, u32[]{:S(2)}, u32[]{:S(2)}) collective-permute-start(bf16[16,8192]{1,0:T(8,128)(2,1)S(1)} %get-tuple-element.5.refs_0_), channel_id=1, source_target_pairs={{0,1},{1,0},{2,3},{3,2},{4,5},{5,4},{6,7},{7,6},{8,9},{9,8},{10,11... | collective-permute-start | bytes 786440 | tf_op jit(solution)/shard_map/ppermute | solution.py:147
  48.1 2.5 %collective-permute-start.5 = (bf16[16,8192]{1,0:T(8,128)(2,1)S(1)}, bf16[16,8192]{1,0:T(8,128)(2,1)S(1)}, u32[]{:S(2)}, u32[]{:S(2)}) collective-permute-start(bf16[16,8192]{1,0:T(8,128)(2,1)S(1)} %get-tuple-element.5.refs_0_), channel_id=1, source_target_pairs={{0,6},{2,0},{4,2},{6,4},{1,7},{3,1},{5,3},{7,5},{8,14},{10,8},{12,... | collective-permute-start | bytes 786440 | tf_op jit(solution)/shard_map/ppermute | solution.py:144
  50.6 0.0 collective-permute-start.3
  50.6 2.7 %collective-permute-start.6 = (bf16[16,8192]{1,0:T(8,128)(2,1)S(1)}, bf16[16,8192]{1,0:T(8,128)(2,1)S(1)}, u32[]{:S(2)}, u32[]{:S(2)}) collective-permute-start(bf16[16,8192]{1,0:T(8,128)(2,1)S(1)} %get-tuple-element.6.refs_1_), channel_id=1, source_target_pairs={{0,6},{2,0},{4,2},{6,4},{1,7},{3,1},{5,3},{7,5},{8,14},{10,8},{12,... | collective-permute-start | bytes 786440 | tf_op jit(solution)/shard_map/ppermute | solution.py:144
  53.2 0.8 %collective-permute-start.10 = (bf16[16,8192]{1,0:T(8,128)(2,1)S(1)}, bf16[16,8192]{1,0:T(8,128)(2,1)S(1)}, u32[]{:S(2)}, u32[]{:S(2)}) collective-permute-start(bf16[16,8192]{1,0:T(8,128)(2,1)S(1)} %get-tuple-element.6.refs_1_), channel_id=1, source_target_pairs={{0,1},{1,0},{2,3},{3,2},{4,5},{5,4},{6,7},{7,6},{8,9},{9,8},{10,11... | collective-permute-start | bytes 786440 | tf_op jit(solution)/shard_map/ppermute | solution.py:147
  54.1 2.2 %collective-permute-done.5.refs_4_ = bf16[16,8192]{1,0:T(8,128)(2,1)S(1)} collective-permute-done((bf16[16,8192]{1,0:T(8,128)(2,1)S(1)}, bf16[16,8192]{1,0:T(8,128)(2,1)S(1)}, u32[]{:S(2)}, u32[]{:S(2)}) %collective-permute-start.5) | collective-permute-done | bytes 262176 | tf_op jit(solution)/shard_map/ppermute | solution.py:144
  56.3 1.2 %collective-permute-start.13 = (bf16[16,8192]{1,0:T(8,128)(2,1)S(1)}, bf16[16,8192]{1,0:T(8,128)(2,1)S(1)}, u32[]{:S(2)}, u32[]{:S(2)}) collective-permute-start(bf16[16,8192]{1,0:T(8,128)(2,1)S(1)} %collective-permute-done.5.refs_4_), channel_id=1, source_target_pairs={{0,1},{1,0},{2,3},{3,2},{4,5},{5,4},{6,7},{7,6},{8,9},{9,8},{10,11... | collective-permute-start | bytes 786440 | tf_op jit(solution)/shard_map/ppermute | solution.py:147
  57.5 1.9 %collective-permute-done.3.refs_2_ = bf16[16,8192]{1,0:T(8,128)(2,1)S(1)} collective-permute-done((bf16[16,8192]{1,0:T(8,128)(2,1)S(1)}, bf16[16,8192]{1,0:T(8,128)(2,1)S(1)}, u32[]{:S(2)}, u32[]{:S(2)}) %collective-permute-start.3) | collective-permute-done | bytes 262176 | tf_op jit(solution)/shard_map/ppermute | solution.py:143
  59.4 2.5 %collective-permute-done.6.refs_5_ = bf16[16,8192]{1,0:T(8,128)(2,1)S(1)} collective-permute-done((bf16[16,8192]{1,0:T(8,128)(2,1)S(1)}, bf16[16,8192]{1,0:T(8,128)(2,1)S(1)}, u32[]{:S(2)}, u32[]{:S(2)}) %collective-permute-start.6) | collective-permute-done | bytes 262176 | tf_op jit(solution)/shard_map/ppermute | solution.py:144
  61.9 3.4 %collective-permute-start.8 = (bf16[16,8192]{1,0:T(8,128)(2,1)S(1)}, bf16[16,8192]{1,0:T(8,128)(2,1)S(1)}, u32[]{:S(2)}, u32[]{:S(2)}) collective-permute-start(bf16[16,8192]{1,0:T(8,128)(2,1)S(1)} %collective-permute-done.6.refs_5_), channel_id=1, source_target_pairs={{0,6},{2,0},{4,2},{6,4},{1,7},{3,1},{5,3},{7,5},{8,14},{10,8},{12,... | collective-permute-start | bytes 786440 | tf_op jit(solution)/shard_map/ppermute | solution.py:145
  65.3 1.1 %collective-permute-start.11 = (bf16[16,8192]{1,0:T(8,128)(2,1)S(1)}, bf16[16,8192]{1,0:T(8,128)(2,1)S(1)}, u32[]{:S(2)}, u32[]{:S(2)}) collective-permute-start(bf16[16,8192]{1,0:T(8,128)(2,1)S(1)} %collective-permute-done.3.refs_2_), channel_id=1, source_target_pairs={{0,1},{1,0},{2,3},{3,2},{4,5},{5,4},{6,7},{7,6},{8,9},{9,8},{10,11... | collective-permute-start | bytes 786440 | tf_op jit(solution)/shard_map/ppermute | solution.py:147
  66.4 0.4 collective-permute-start.14
  66.8 0.1 collective-permute-start.12
  66.9 3.7 %collective-permute-done.7.refs_6_ = bf16[16,8192]{1,0:T(8,128)(2,1)S(1)} collective-permute-done((bf16[16,8192]{1,0:T(8,128)(2,1)S(1)}, bf16[16,8192]{1,0:T(8,128)(2,1)S(1)}, u32[]{:S(2)}, u32[]{:S(2)}) %collective-permute-start.7) | collective-permute-done | bytes 262176 | tf_op jit(solution)/shard_map/ppermute | solution.py:145
  70.6 1.1 %collective-permute-start.15 = (bf16[16,8192]{1,0:T(8,128)(2,1)S(1)}, bf16[16,8192]{1,0:T(8,128)(2,1)}, u32[]{:S(2)}, u32[]{:S(2)}) collective-permute-start(bf16[16,8192]{1,0:T(8,128)(2,1)S(1)} %collective-permute-done.7.refs_6_), channel_id=1, source_target_pairs={{0,1},{1,0},{2,3},{3,2},{4,5},{5,4},{6,7},{7,6},{8,9},{9,8},{10,11... | collective-permute-start | bytes 786440 | tf_op jit(solution)/shard_map/ppermute | solution.py:147
  71.7 0.1 collective-permute-start.16
  71.9 0.1 stack.67.place_ref
  72.0 1.1 %collective-permute-done.15.refs_14_ = bf16[16,8192]{1,0:T(8,128)(2,1)} collective-permute-done((bf16[16,8192]{1,0:T(8,128)(2,1)S(1)}, bf16[16,8192]{1,0:T(8,128)(2,1)}, u32[]{:S(2)}, u32[]{:S(2)}) %collective-permute-start.15) | collective-permute-done | bytes 262176 | tf_op jit(solution)/shard_map/ppermute | solution.py:147
  73.0 0.4 collective-permute-done.16.refs_15_
  73.4 3.3 %assemble.1 = bf16[256,8192]{1,0:T(8,128)(2,1)} custom-call(s32[16]{0:T(128)S(1)} %stack.67.place_ref, bf16[16,8192]{1,0:T(8,128)(2,1)S(1)} %get-tuple-element.5.refs_0_, bf16[16,8192]{1,0:T(8,128)(2,1)S(1)} %get-tuple-element.6.refs_1_, bf16[16,8192]{1,0:T(8,128)(2,1)S(1)} %collective-permute-done.3.refs_2_, ...), custom_call_target="tpu_custom_call" | custom-call | tf_op jit(solution)/shard_map/assemble/pallas_call | solution.py:109
  (19 shorter events, 0.1 us)
Async XLA Ops:
  0.6 1.0 %copy-start = (bf16[32,8192]{1,0:T(8,128)(2,1)S(1)}, bf16[32,8192]{1,0:T(8,128)(2,1)}, u32[]{:S(2)}) copy-start(bf16[32,8192]{1,0:T(8,128)(2,1)} %base_ref.3) | copy-start | bytes 1572868
  1.7 1.0 %copy-start.3 = (bf16[1,32,8192]{2,1,0:T(8,128)(2,1)S(1)}, bf16[1,32,8192]{2,1,0:T(8,128)(2,1)}, u32[]{:S(2)}) copy-start(bf16[1,32,8192]{2,1,0:T(8,128)(2,1)} %local_ref.1) | copy-start | bytes 1572868
  2.7 38.9 %copy-start.1 = (bf16[32,8192]{1,0:T(8,128)(2,1)S(1)}, bf16[32,8192]{1,0:T(8,128)(2,1)}, u32[]{:S(2)}) copy-start(bf16[32,8192]{1,0:T(8,128)(2,1)} %base_ref.3) | copy-start | bytes 1572868
  2.7 38.9 %copy-start.2 = (f32[32,8192]{1,0:T(8,128)S(1)}, f32[32,8192]{1,0:T(8,128)}, u32[]{:S(2)}) copy-start(f32[32,8192]{1,0:T(8,128)} %momentum_ref.1) | copy-start | bytes 3145732
  18.8 8.5 %collective-permute-start.2 = (bf16[16,2048]{1,0:T(8,128)(2,1)S(1)}, bf16[16,2048]{1,0:T(8,128)(2,1)S(1)}, u32[]{:S(2)}, u32[]{:S(2)}) collective-permute-start(bf16[16,2048]{1,0:T(8,128)(2,1)S(1)} %reduce_sum.12), channel_id=1, source_target_pairs={{0,192},{64,0},{128,64},{192,128},{1,193},{65,1},{129,65},{193,129... | collective-permute-start | bytes 196616 | tf_op jit(solution)/shard_map/ppermute | solution.py:132
  24.0 5.4 %collective-permute-start.1 = (bf16[16,2048]{1,0:T(8,128)(2,1)S(1)}, bf16[16,2048]{1,0:T(8,128)(2,1)S(1)}, u32[]{:S(2)}, u32[]{:S(2)}) collective-permute-start(bf16[16,2048]{1,0:T(8,128)(2,1)S(1)} %reduce_sum.12), channel_id=1, source_target_pairs={{0,64},{64,128},{128,192},{192,0},{1,65},{65,129},{129,193},{193,1... | collective-permute-start | bytes 196616 | tf_op jit(solution)/shard_map/ppermute | solution.py:132
  24.0 7.1 %collective-permute-start = (bf16[16,2048]{1,0:T(8,128)(2,1)S(1)}, bf16[16,2048]{1,0:T(8,128)(2,1)S(1)}, u32[]{:S(2)}, u32[]{:S(2)}) collective-permute-start(bf16[16,2048]{1,0:T(8,128)(2,1)S(1)} %reduce_sum.12), channel_id=1, source_target_pairs={{0,128},{64,192},{128,0},{192,64},{1,129},{65,193},{129,1},{193,65... | collective-permute-start | bytes 196616 | tf_op jit(solution)/shard_map/ppermute | solution.py:132
  42.7 11.4 %collective-permute-start.9 = (bf16[16,8192]{1,0:T(8,128)(2,1)S(1)}, bf16[16,8192]{1,0:T(8,128)(2,1)S(1)}, u32[]{:S(2)}, u32[]{:S(2)}) collective-permute-start(bf16[16,8192]{1,0:T(8,128)(2,1)S(1)} %get-tuple-element.5.refs_0_), channel_id=1, source_target_pairs={{0,1},{1,0},{2,3},{3,2},{4,5},{5,4},{6,7},{7,6},{8,9},{9,8},{10,11... | collective-permute-start | bytes 786440 | tf_op jit(solution)/shard_map/ppermute | solution.py:147
  48.1 8.2 %collective-permute-start.5 = (bf16[16,8192]{1,0:T(8,128)(2,1)S(1)}, bf16[16,8192]{1,0:T(8,128)(2,1)S(1)}, u32[]{:S(2)}, u32[]{:S(2)}) collective-permute-start(bf16[16,8192]{1,0:T(8,128)(2,1)S(1)} %get-tuple-element.5.refs_0_), channel_id=1, source_target_pairs={{0,6},{2,0},{4,2},{6,4},{1,7},{3,1},{5,3},{7,5},{8,14},{10,8},{12,... | collective-permute-start | bytes 786440 | tf_op jit(solution)/shard_map/ppermute | solution.py:144
  50.6 8.8 %collective-permute-start.3 = (bf16[16,8192]{1,0:T(8,128)(2,1)S(1)}, bf16[16,8192]{1,0:T(8,128)(2,1)S(1)}, u32[]{:S(2)}, u32[]{:S(2)}) collective-permute-start(bf16[16,8192]{1,0:T(8,128)(2,1)S(1)} %get-tuple-element.5.refs_0_), channel_id=1, source_target_pairs={{0,2},{2,4},{4,6},{6,0},{1,3},{3,5},{5,7},{7,1},{8,10},{10,12},{12... | collective-permute-start | bytes 786440 | tf_op jit(solution)/shard_map/ppermute | solution.py:143
  50.6 11.4 %collective-permute-start.6 = (bf16[16,8192]{1,0:T(8,128)(2,1)S(1)}, bf16[16,8192]{1,0:T(8,128)(2,1)S(1)}, u32[]{:S(2)}, u32[]{:S(2)}) collective-permute-start(bf16[16,8192]{1,0:T(8,128)(2,1)S(1)} %get-tuple-element.6.refs_1_), channel_id=1, source_target_pairs={{0,6},{2,0},{4,2},{6,4},{1,7},{3,1},{5,3},{7,5},{8,14},{10,8},{12,... | collective-permute-start | bytes 786440 | tf_op jit(solution)/shard_map/ppermute | solution.py:144
  53.2 12.1 %collective-permute-start.10 = (bf16[16,8192]{1,0:T(8,128)(2,1)S(1)}, bf16[16,8192]{1,0:T(8,128)(2,1)S(1)}, u32[]{:S(2)}, u32[]{:S(2)}) collective-permute-start(bf16[16,8192]{1,0:T(8,128)(2,1)S(1)} %get-tuple-element.6.refs_1_), channel_id=1, source_target_pairs={{0,1},{1,0},{2,3},{3,2},{4,5},{5,4},{6,7},{7,6},{8,9},{9,8},{10,11... | collective-permute-start | bytes 786440 | tf_op jit(solution)/shard_map/ppermute | solution.py:147
  54.1 12.3 %collective-permute-start.4 = (bf16[16,8192]{1,0:T(8,128)(2,1)S(1)}, bf16[16,8192]{1,0:T(8,128)(2,1)S(1)}, u32[]{:S(2)}, u32[]{:S(2)}) collective-permute-start(bf16[16,8192]{1,0:T(8,128)(2,1)S(1)} %get-tuple-element.6.refs_1_), channel_id=1, source_target_pairs={{0,2},{2,4},{4,6},{6,0},{1,3},{3,5},{5,7},{7,1},{8,10},{10,12},{12... | collective-permute-start | bytes 786440 | tf_op jit(solution)/shard_map/ppermute | solution.py:143
  56.3 10.5 %collective-permute-start.13 = (bf16[16,8192]{1,0:T(8,128)(2,1)S(1)}, bf16[16,8192]{1,0:T(8,128)(2,1)S(1)}, u32[]{:S(2)}, u32[]{:S(2)}) collective-permute-start(bf16[16,8192]{1,0:T(8,128)(2,1)S(1)} %collective-permute-done.5.refs_4_), channel_id=1, source_target_pairs={{0,1},{1,0},{2,3},{3,2},{4,5},{5,4},{6,7},{7,6},{8,9},{9,8},{10,11... | collective-permute-start | bytes 786440 | tf_op jit(solution)/shard_map/ppermute | solution.py:147
  59.4 11.2 %collective-permute-start.7 = (bf16[16,8192]{1,0:T(8,128)(2,1)S(1)}, bf16[16,8192]{1,0:T(8,128)(2,1)S(1)}, u32[]{:S(2)}, u32[]{:S(2)}) collective-permute-start(bf16[16,8192]{1,0:T(8,128)(2,1)S(1)} %collective-permute-done.3.refs_2_), channel_id=1, source_target_pairs={{0,2},{2,4},{4,6},{6,0},{1,3},{3,5},{5,7},{7,1},{8,10},{10,12},{12... | collective-permute-start | bytes 786440 | tf_op jit(solution)/shard_map/ppermute | solution.py:145
  61.9 9.8 %collective-permute-start.8 = (bf16[16,8192]{1,0:T(8,128)(2,1)S(1)}, bf16[16,8192]{1,0:T(8,128)(2,1)S(1)}, u32[]{:S(2)}, u32[]{:S(2)}) collective-permute-start(bf16[16,8192]{1,0:T(8,128)(2,1)S(1)} %collective-permute-done.6.refs_5_), channel_id=1, source_target_pairs={{0,6},{2,0},{4,2},{6,4},{1,7},{3,1},{5,3},{7,5},{8,14},{10,8},{12,... | collective-permute-start | bytes 786440 | tf_op jit(solution)/shard_map/ppermute | solution.py:145
  65.3 6.6 %collective-permute-start.11 = (bf16[16,8192]{1,0:T(8,128)(2,1)S(1)}, bf16[16,8192]{1,0:T(8,128)(2,1)S(1)}, u32[]{:S(2)}, u32[]{:S(2)}) collective-permute-start(bf16[16,8192]{1,0:T(8,128)(2,1)S(1)} %collective-permute-done.3.refs_2_), channel_id=1, source_target_pairs={{0,1},{1,0},{2,3},{3,2},{4,5},{5,4},{6,7},{7,6},{8,9},{9,8},{10,11... | collective-permute-start | bytes 786440 | tf_op jit(solution)/shard_map/ppermute | solution.py:147
  66.4 5.6 %collective-permute-start.14 = (bf16[16,8192]{1,0:T(8,128)(2,1)S(1)}, bf16[16,8192]{1,0:T(8,128)(2,1)S(1)}, u32[]{:S(2)}, u32[]{:S(2)}) collective-permute-start(bf16[16,8192]{1,0:T(8,128)(2,1)S(1)} %collective-permute-done.6.refs_5_), channel_id=1, source_target_pairs={{0,1},{1,0},{2,3},{3,2},{4,5},{5,4},{6,7},{7,6},{8,9},{9,8},{10,11... | collective-permute-start | bytes 786440 | tf_op jit(solution)/shard_map/ppermute | solution.py:147
  66.8 5.1 %collective-permute-start.12 = (bf16[16,8192]{1,0:T(8,128)(2,1)S(1)}, bf16[16,8192]{1,0:T(8,128)(2,1)}, u32[]{:S(2)}, u32[]{:S(2)}) collective-permute-start(bf16[16,8192]{1,0:T(8,128)(2,1)S(1)} %collective-permute-done.4.refs_3_), channel_id=1, source_target_pairs={{0,1},{1,0},{2,3},{3,2},{4,5},{5,4},{6,7},{7,6},{8,9},{9,8},{10,11... | collective-permute-start | bytes 786440 | tf_op jit(solution)/shard_map/ppermute | solution.py:147
  70.6 2.4 %collective-permute-start.15 = (bf16[16,8192]{1,0:T(8,128)(2,1)S(1)}, bf16[16,8192]{1,0:T(8,128)(2,1)}, u32[]{:S(2)}, u32[]{:S(2)}) collective-permute-start(bf16[16,8192]{1,0:T(8,128)(2,1)S(1)} %collective-permute-done.7.refs_6_), channel_id=1, source_target_pairs={{0,1},{1,0},{2,3},{3,2},{4,5},{5,4},{6,7},{7,6},{8,9},{9,8},{10,11... | collective-permute-start | bytes 786440 | tf_op jit(solution)/shard_map/ppermute | solution.py:147
  71.7 1.7 %collective-permute-start.16 = (bf16[16,8192]{1,0:T(8,128)(2,1)S(1)}, bf16[16,8192]{1,0:T(8,128)(2,1)}, u32[]{:S(2)}, u32[]{:S(2)}) collective-permute-start(bf16[16,8192]{1,0:T(8,128)(2,1)S(1)} %collective-permute-done.8.refs_7_), channel_id=1, source_target_pairs={{0,1},{1,0},{2,3},{3,2},{4,5},{5,4},{6,7},{7,6},{8,9},{9,8},{10,11... | collective-permute-start | bytes 786440 | tf_op jit(solution)/shard_map/ppermute | solution.py:147

commit v3 on v2

v3 whole, which is shorter than its diff:
```python
import functools

import jax
import jax.numpy as jnp
from jax import lax
from jax.experimental import pallas as pl
from jax.experimental.pallas import tpu as pltpu
from jax.sharding import Mesh, PartitionSpec as P

BLOCK = 32

floor_value = 0.5
spread_ratio = 3.0
code_peak = 6.0
outer_rate = 0.7
momentum_coef = 0.9

ROWS = 32
HALF = 16
COLS = 8192
PIECES = 4
WIDE = COLS // PIECES
LANES = 128

SMALL = pltpu.CompilerParams(vmem_limit_bytes=16 << 20)


def encode_kernel(local_hbm, base_hbm, out_ref, local_ref, base_ref, sems):
    copies = []
    for half in range(2):
        rows = pl.ds(half * HALF, HALF)
        copies.append(
            (
                pltpu.make_async_copy(
                    local_hbm.at[0, rows, :], local_ref.at[half], sems.at[0, half]
                ),
                pltpu.make_async_copy(base_hbm.at[rows, :], base_ref.at[half], sems.at[1, half]),
            )
        )
    for pair in copies:
        for copy in pair:
            copy.start()
    block = lax.broadcasted_iota(jnp.int32, (LANES, LANES), 0) // BLOCK
    block_t = lax.broadcasted_iota(jnp.int32, (LANES, LANES), 1) // BLOCK
    same_block = jnp.where(block == block_t, 1.0 / BLOCK, 0.0).astype(jnp.float32)
    for k in range(2 * PIECES):
        half, piece = k // PIECES, k % PIECES
        if piece == 0:
            for copy in copies[half]:
                copy.wait()
        cols = pl.ds(piece * WIDE, WIDE)
        grad = base_ref[half, :, cols].astype(jnp.float32) - local_ref[half, :, cols].astype(
            jnp.float32
        )
        tall = jnp.concatenate(
            [grad[:, i * LANES : (i + 1) * LANES] for i in range(WIDE // LANES)], axis=0
        )
        mean_square = jnp.dot(
            tall * tall,
            same_block,
            precision=lax.Precision.HIGHEST,
            preferred_element_type=jnp.float32,
        )
        scale = (jnp.maximum(jnp.sqrt(mean_square), floor_value) / spread_ratio).astype(
            jnp.bfloat16
        )
        limit = code_peak * scale.astype(jnp.float32)
        decoded = jnp.clip(tall, -limit, limit).astype(jnp.bfloat16)
        for i in range(WIDE // LANES):
            out_ref[k, :, i * LANES : (i + 1) * LANES] = decoded[i * HALF : (i + 1) * HALF]


def in_vmem(value):
    return pltpu.with_memory_space_constraint(value, pltpu.VMEM)


def in_hbm(value):
    return pltpu.with_memory_space_constraint(value, pltpu.HBM)


def encode(local_params, base_rows):
    halves = (2, HALF, COLS)
    return pl.pallas_call(
        encode_kernel,
        out_shape=pltpu.VMEM((2 * PIECES, HALF, WIDE), jnp.bfloat16),
        in_specs=[pl.BlockSpec(memory_space=pltpu.HBM)] * 2,
        scratch_shapes=[
            pltpu.VMEM(halves, jnp.bfloat16),
            pltpu.VMEM(halves, jnp.bfloat16),
            pltpu.SemaphoreType.DMA((2, 2)),
        ],
        compiler_params=SMALL,
        name="encode",
    )(in_hbm(local_params), in_hbm(base_rows))


def update_kernel(
    average_ref, base_ref, momentum_ref, first_ref, second_ref, own_ref, new_momentum_ref
):
    for half, new_base_ref in ((0, first_ref), (1, second_ref)):
        for piece in range(PIECES):
            rows = pl.ds(half * HALF, HALF)
            cols = pl.ds(piece * WIDE, WIDE)
            average = average_ref[half * PIECES + piece].astype(jnp.float32)
            new_momentum = momentum_coef * momentum_ref[rows, cols] + average
            new_momentum_ref[rows, cols] = new_momentum
            new_base = (
                base_ref[rows, cols].astype(jnp.float32)
                - outer_rate * (average + momentum_coef * new_momentum)
            ).astype(jnp.bfloat16)
            new_base_ref[:, cols] = new_base
            own_ref[rows, cols] = new_base


def outer_update(average, base_rows, momentum):
    part = pltpu.VMEM((HALF, COLS), jnp.bfloat16)
    own = pltpu.VMEM((ROWS, COLS), jnp.bfloat16)
    return pl.pallas_call(
        update_kernel,
        out_shape=(part, part, own, jax.ShapeDtypeStruct((ROWS, COLS), jnp.float32)),
        compiler_params=SMALL,
        name="outer_update",
    )(in_vmem(average), base_rows, momentum)


def join_kernel(one_ref, two_ref, out_ref):
    out_ref[pl.ds(0, HALF), :] = one_ref[...]
    out_ref[pl.ds(HALF, HALF), :] = two_ref[...]


def join(one, two):
    return pl.pallas_call(
        join_kernel,
        out_shape=pltpu.VMEM((ROWS, COLS), jnp.bfloat16),
        compiler_params=SMALL,
        name="join",
    )(in_vmem(one), in_vmem(two))


def place_kernel(count, place_ref, *refs):
    parts, out_ref, sems = refs[:count], refs[-2], refs[-1]
    copies = []
    for ref in parts:
        for k in range(ref.shape[0] // HALF):
            start = pl.multiple_of(place_ref[len(copies)] * HALF, HALF)
            copies.append(
                pltpu.make_async_copy(
                    ref.at[pl.ds(k * HALF, HALF), :],
                    out_ref.at[pl.ds(start, HALF), :],
                    sems.at[len(copies)],
                )
            )
    for copy in copies:
        copy.start()
    for copy in copies:
        copy.wait()


def place(rows, parts, whole=None):
    count = len(parts)
    total = sum(part.shape[0] for part in parts) // HALF
    keep = [] if whole is None else [whole]
    hbm = pl.BlockSpec(memory_space=pltpu.HBM)
    return pl.pallas_call(
        functools.partial(place_kernel, count),
        out_shape=pltpu.HBM((16 * HALF, COLS), jnp.bfloat16),
        in_specs=[pl.BlockSpec(memory_space=pltpu.SMEM)]
        + [pl.BlockSpec(memory_space=pltpu.VMEM)] * count
        + [hbm] * len(keep),
        out_specs=hbm,
        scratch_shapes=[pltpu.SemaphoreType.DMA((total,))],
        input_output_aliases={count + 1: 0} if keep else {},
        compiler_params=SMALL,
        cost_estimate=pl.CostEstimate(
            flops=0, transcendentals=0, bytes_accessed=total * HALF * COLS * 4
        ),
        name="place",
    )(
        jnp.stack(rows).astype(jnp.int32),
        *[in_vmem(part) for part in parts],
        *[in_hbm(w) for w in keep],
    )


def ring(n, step):
    return [(i, (i + step) % n) for i in range(n)]


def shards(local_params, base_params, momentum):
    decoded = encode(local_params, base_params)

    near = ("zl", "y")
    received = lax.all_to_all(decoded, near, 0, 0, tiled=True)
    partial = jnp.sum(received.astype(jnp.float32), axis=0).astype(jnp.bfloat16)

    others = [lax.ppermute(partial, "zh", ring(4, k)) for k in (1, 2, 3)]
    one, two, three = [value.astype(jnp.float32) for value in others]
    total = (partial.astype(jnp.float32) + two) + (one + three)
    average = (total / 32).astype(jnp.bfloat16)

    gathered = lax.all_to_all(
        jnp.broadcast_to(average[None], (8,) + average.shape), near, 0, 0, tiled=True
    )

    first, second, own, new_momentum = outer_update(gathered, base_params, momentum)

    def swap(part):
        return lax.ppermute(part, "core", ring(2, 1))

    x, core = lax.axis_index("x"), lax.axis_index("core")

    def rows(step, c):
        return [(((x + step) % 4) * 2 + c) * 2 + half for half in range(2)]

    left = [lax.ppermute(half, "x", ring(4, 1)) for half in (first, second)]
    right = [lax.ppermute(half, "x", ring(4, 3)) for half in (second, first)]
    far = [lax.ppermute(left[0], "x", ring(4, 1)), lax.ppermute(right[0], "x", ring(4, 3))]

    from_left = join(left[0], left[1])
    from_right = join(right[1], right[0])
    from_far = join(far[0], far[1])
    near = [own, from_left, from_right]
    near_steps, far_step = (0, 3, 1), 2
    new_base = place(
        [r for step in near_steps for r in rows(step, core)]
        + [r for step in near_steps for r in rows(step, 1 - core)]
        + rows(far_step, core),
        near + [swap(part) for part in near] + [from_far],
    )
    new_base = place(rows(far_step, 1 - core), [swap(from_far)], new_base)
    return (new_base, new_momentum)


def solution(mesh):
    fine = Mesh(mesh.devices.reshape(4, 2, 4, 4, 2), ("zh", "zl", "y", "x", "core"))
    rep, fsdp = ("zh", "zl", "y"), ("x", "core")
    in_specs = (P(rep, fsdp, None), P(fsdp, None), P(fsdp, None))
    out_specs = (P(), P(fsdp, None))
    return jax.shard_map(shards, mesh=fine, in_specs=in_specs, out_specs=out_specs, check_vma=False)
```

time: 76.9 us -> 70.9 us (0.922)
  waiting for transfers between devices: 15.7 us -> 6.2 us
  Pallas kernels: 5.58 us -> 8.69 us
  starting transfers between devices: 27.2 us -> 29.6 us
  local copies, waits for them, and re-layouts: 2.22 us -> 0.14 us
    ppermute x2, waiting for transfers between devices: 4.73 us -> 0.01 us  [shards(): right = [lax.ppermute(half, 'x', ring(4, 3)) for half in (second, first)]]
    ppermute x8 -> x4, starting transfers between devices: 10.2 us -> 14.3 us  [swap(): return lax.ppermute(part, 'core', ring(2, 1))]
    ppermute x1, waiting for transfers between devices: 3.71 us -> 0.01 us  [shards(): lax.ppermute(left[0], 'x', ring(4, 1))]
    ppermute x2, starting transfers between devices: 5.15 us -> 2.73 us  [shards(): right = [lax.ppermute(half, 'x', ring(4, 3)) for half in (second, first)]]
    unnamed x8 -> x4, local copies, waits for them, and re-layouts: 2.08 us -> 0.01 us
    pallas_call x2 -> x6, Pallas kernels: 4.39 us -> 6.11 us  [the longest x2 4.87 us: place(): pl.pallas_call(functools.partial(place_kernel, count), out_shape=pltpu.HB...]
    ppermute x8 -> x4, waiting for transfers between devices: 1.44 us -> 0.01 us  [swap(): return lax.ppermute(part, 'core', ring(2, 1))]
    ppermute x2, starting transfers between devices: 0.01 us -> 1.42 us  [shards(): left = [lax.ppermute(half, 'x', ring(4, 1)) for half in (first, second)]]
  transfers between devices with their start and end apart: 17 -> 13, of which waited for: 8 -> 3; matrix products, arithmetic and copies ran while one was open for 0% -> 0% of each run, Pallas kernels for 0% -> 4%
where the time goes in v3:
time: 70.9 us; the launch traced here: 70.7 us
  starting transfers between devices  29.6 us (42%)
  blocking collectives  25.1 us (35%)
  Pallas kernels  8.69 us (12%)
  waiting for transfers between devices  6.2 us (9%)
  between operations  0.74 us (1%)
    all_to_all x1, blocking collectives, shards(): received = lax.all_to_all(decoded, near, 0, 0, tiled=True)  14.8 us
    ppermute x4, starting transfers between devices, swap(): return lax.ppermute(part, 'core', ring(2, 1))  14.3 us
    all_to_all x1, blocking collectives, shards(): lax.all_to_all(jnp.broadcast_to(average[None], (8,) + average.shape), nea...  10.3 us
    ppermute x3, starting transfers between devices, shards(): others = [lax.ppermute(partial, 'zh', ring(4, k)) for k in (1, 2, 3)]  8.45 us
    pallas_call x2, Pallas kernels, place(): pl.pallas_call(functools.partial(place_kernel, count), out_shape=pltpu.HB...  4.87 us
    ppermute x3, waiting for transfers between devices, shards(): others = [lax.ppermute(partial, 'zh', ring(4, k)) for k in (1, 2, 3)]  3.89 us
    ppermute x2, starting transfers between devices, shards(): right = [lax.ppermute(half, 'x', ring(4, 3)) for half in (second, first)]  2.73 us
    ppermute x1, starting transfers between devices, shards(): lax.ppermute(right[0], 'x', ring(4, 3))  2.67 us
  transfers between devices with their start and end apart: 13, of which 3 were waited for; matrix products, arithmetic and copies ran while one was open for 0% of the time, Pallas kernels for 4%

profile of v3, /device:TPU:1, one launch (start us, length us, event | category | flops | bytes accessed | tf_op | source)
XLA Modules:
  0.0 70.7 jit_solution(14248181379587752766)
XLA Ops:
  0.6 2.6 %encode.1 = bf16[8,16,2048]{2,1,0:T(8,128)(2,1)S(1)} custom-call(bf16[1,32,8192]{2,1,0:T(8,128)(2,1)} %local_hbm.1, bf16[32,8192]{1,0:T(8,128)(2,1)} %base_ref.1), custom_call_target="tpu_custom_call" | custom-call | tf_op jit(solution)/shard_map/encode/pallas_call | solution.py:83
  3.2 14.8 %all_to_all.10 = bf16[8,16,2048]{2,1,0:T(8,128)(2,1)S(1)} all-to-all(bf16[8,16,2048]{2,1,0:T(8,128)(2,1)S(1)} %encode.1), channel_id=1, replica_groups=mesh['zh'=4,'zl'=2,'y'=4,'x'=4,'core'=2] {'zl','y'}, dimensions={0} | all-to-all | bytes 1048576 | tf_op jit(solution)/shard_map/all_to_all | solution.py:193
  18.0 0.1 reduce_sum.12
  18.1 5.2 %collective-permute-start.2 = (bf16[16,2048]{1,0:T(8,128)(2,1)S(1)}, bf16[16,2048]{1,0:T(8,128)(2,1)S(1)}, u32[]{:S(2)}, u32[]{:S(2)}) collective-permute-start(bf16[16,2048]{1,0:T(8,128)(2,1)S(1)} %reduce_sum.12), channel_id=1, source_target_pairs={{0,192},{64,0},{128,64},{192,128},{1,193},{65,1},{129,65},{193,129... | collective-permute-start | bytes 196616 | tf_op jit(solution)/shard_map/ppermute | solution.py:196
  23.3 3.2 %collective-permute-start = (bf16[16,2048]{1,0:T(8,128)(2,1)S(1)}, bf16[16,2048]{1,0:T(8,128)(2,1)S(1)}, u32[]{:S(2)}, u32[]{:S(2)}) collective-permute-start(bf16[16,2048]{1,0:T(8,128)(2,1)S(1)} %reduce_sum.12), channel_id=1, source_target_pairs={{0,128},{64,192},{128,0},{192,64},{1,129},{65,193},{129,1},{193,65... | collective-permute-start | bytes 196616 | tf_op jit(solution)/shard_map/ppermute | solution.py:196
  26.6 0.0 collective-permute-done.2
  26.6 2.2 %collective-permute-done.1 = bf16[16,2048]{1,0:T(8,128)(2,1)S(1)} collective-permute-done((bf16[16,2048]{1,0:T(8,128)(2,1)S(1)}, bf16[16,2048]{1,0:T(8,128)(2,1)S(1)}, u32[]{:S(2)}, u32[]{:S(2)}) %collective-permute-start.1) | collective-permute-done | bytes 65568 | tf_op jit(solution)/shard_map/ppermute | solution.py:196
  28.8 1.7 %collective-permute-done = bf16[16,2048]{1,0:T(8,128)(2,1)S(1)} collective-permute-done((bf16[16,2048]{1,0:T(8,128)(2,1)S(1)}, bf16[16,2048]{1,0:T(8,128)(2,1)S(1)}, u32[]{:S(2)}, u32[]{:S(2)}) %collective-permute-start) | collective-permute-done | bytes 65568 | tf_op jit(solution)/shard_map/ppermute | solution.py:196
  30.5 10.3 %all_to_all.11.average_ref = bf16[8,16,2048]{2,1,0:T(8,128)(2,1)S(1)} all-to-all(bf16[8,16,2048]{2,1,0:T(8,128)(2,1)S(1)} %broadcast_in_dim.2), channel_id=1, replica_groups=mesh['zh'=4,'zl'=2,'y'=4,'x'=4,'core'=2] {'zl','y'}, dimensions={0} | all-to-all | bytes 1048576 | tf_op jit(solution)/shard_map/all_to_all | solution.py:201
  40.9 1.1 %outer_update.1 = (bf16[16,8192]{1,0:T(8,128)(2,1)S(1)}, bf16[16,8192]{1,0:T(8,128)(2,1)S(1)}, bf16[32,8192]{1,0:T(8,128)(2,1)S(1)}, f32[32,8192]{1,0:T(8,128)}) custom-call(bf16[8,16,2048]{2,1,0:T(8,128)(2,1)S(1)} %all_to_all.11.average_ref, bf16[32,8192]{1,0:T(8,128)(2,1)S(1)} %copy-done, f32[32,8192]{1,0:T(8,128)S(1)} %copy-done.1), custom_call_target="tpu_custom_call" | custom-call | tf_op jit(solution)/shard_map/outer_update/pallas_call | solution.py:118
  42.0 1.2 %collective-permute-start.3 = (bf16[16,8192]{1,0:T(8,128)(2,1)S(1)}, bf16[16,8192]{1,0:T(8,128)(2,1)S(1)}, u32[]{:S(2)}, u32[]{:S(2)}) collective-permute-start(bf16[16,8192]{1,0:T(8,128)(2,1)S(1)} %get-tuple-element.6), channel_id=1, source_target_pairs={{0,2},{2,4},{4,6},{6,0},{1,3},{3,5},{5,7},{7,1},{8,10},{10,12},{12... | collective-permute-start | bytes 786440 | tf_op jit(solution)/shard_map/ppermute | solution.py:215
  43.2 1.5 %collective-permute-start.5 = (bf16[16,8192]{1,0:T(8,128)(2,1)S(1)}, bf16[16,8192]{1,0:T(8,128)(2,1)S(1)}, u32[]{:S(2)}, u32[]{:S(2)}) collective-permute-start(bf16[16,8192]{1,0:T(8,128)(2,1)S(1)} %get-tuple-element.7), channel_id=1, source_target_pairs={{0,6},{2,0},{4,2},{6,4},{1,7},{3,1},{5,3},{7,5},{8,14},{10,8},{12,... | collective-permute-start | bytes 786440 | tf_op jit(solution)/shard_map/ppermute | solution.py:216
  44.7 1.3 %collective-permute-start.9 = (bf16[16,8192]{1,0:T(8,128)(2,1)S(1)}, bf16[16,8192]{1,0:T(8,128)(2,1)S(1)}, u32[]{:S(2)}, u32[]{:S(2)}) collective-permute-start(bf16[16,8192]{1,0:T(8,128)(2,1)S(1)} %get-tuple-element.6), channel_id=1, source_target_pairs={{0,6},{2,0},{4,2},{6,4},{1,7},{3,1},{5,3},{7,5},{8,14},{10,8},{12,... | collective-permute-start | bytes 786440 | tf_op jit(solution)/shard_map/ppermute | solution.py:216
  46.0 0.2 collective-permute-start.8
  46.2 2.3 %collective-permute-done.3.one_ref = bf16[16,8192]{1,0:T(8,128)(2,1)S(1)} collective-permute-done((bf16[16,8192]{1,0:T(8,128)(2,1)S(1)}, bf16[16,8192]{1,0:T(8,128)(2,1)S(1)}, u32[]{:S(2)}, u32[]{:S(2)}) %collective-permute-start.3) | collective-permute-done | bytes 262176 | tf_op jit(solution)/shard_map/ppermute | solution.py:215
  48.5 0.0 collective-permute-start.4
  48.5 0.0 collective-permute-done.5.two_ref
  48.5 2.7 %collective-permute-start.6 = (bf16[16,8192]{1,0:T(8,128)(2,1)S(1)}, bf16[16,8192]{1,0:T(8,128)(2,1)S(1)}, u32[]{:S(2)}, u32[]{:S(2)}) collective-permute-start(bf16[16,8192]{1,0:T(8,128)(2,1)S(1)} %collective-permute-done.5.two_ref), channel_id=1, source_target_pairs={{0,6},{2,0},{4,2},{6,4},{1,7},{3,1},{5,3},{7,5},{8,14},{10,8},{12,... | collective-permute-start | bytes 786440 | tf_op jit(solution)/shard_map/ppermute | solution.py:217
  51.1 10.0 %collective-permute-start.10 = (bf16[32,8192]{1,0:T(8,128)(2,1)S(1)}, bf16[32,8192]{1,0:T(8,128)(2,1)S(1)}, u32[]{:S(2)}, u32[]{:S(2)}) collective-permute-start(bf16[32,8192]{1,0:T(8,128)(2,1)S(1)} %get-tuple-element.8.refs_0_), channel_id=1, source_target_pairs={{0,1},{1,0},{2,3},{3,2},{4,5},{5,4},{6,7},{7,6},{8,9},{9,8},{10,11... | collective-permute-start | bytes 1572872 | tf_op jit(solution)/shard_map/ppermute | solution.py:208
  61.1 0.0 collective-permute-done.9.one_ref
  61.2 0.1 collective-permute-start.12
  61.3 0.6 collective-permute-start.11
  61.9 0.0 collective-permute-done.4.one_ref
  61.9 0.0 collective-permute-done.6.two_ref
  61.9 3.7 %collective-permute-start.7 = (bf16[32,8192]{1,0:T(8,128)(2,1)S(1)}, bf16[32,8192]{1,0:T(8,128)(2,1)}, u32[]{:S(2)}, u32[]{:S(2)}) collective-permute-start(bf16[32,8192]{1,0:T(8,128)(2,1)S(1)} %join.3.refs_6_), channel_id=1, source_target_pairs={{0,1},{1,0},{2,3},{3,2},{4,5},{5,4},{6,7},{7,6},{8,9},{9,8},{10,11... | collective-permute-start | bytes 1572872 | tf_op jit(solution)/shard_map/ppermute | solution.py:208
  65.6 0.1 stack.71.place_ref
  65.7 0.1 pad_add_fusion.place_ref
  65.8 0.0 collective-permute-done.12.refs_5_
  65.8 0.0 collective-permute-done.11.refs_4_
  65.8 3.0 %place.2.refs_1_ = bf16[256,8192]{1,0:T(8,128)(2,1)} custom-call(s32[14]{0:T(128)S(1)} %stack.71.place_ref, bf16[32,8192]{1,0:T(8,128)(2,1)S(1)} %get-tuple-element.8.refs_0_, bf16[32,8192]{1,0:T(8,128)(2,1)S(1)} %join.4.refs_1_, bf16[32,8192]{1,0:T(8,128)(2,1)S(1)} %join.5.refs_2_, bf16[32,8192]{1,0:T(8,128)(2,1)S(1)} %collective-permute-done.10.refs_3_, ...), custom_call_target="tpu_custom_call" | custom-call | bytes 7340032 | tf_op jit(solution)/shard_map/place/pallas_call | solution.py:164
  68.8 0.0 collective-permute-done.7.refs_0_
  68.8 1.9 %place.3 = bf16[256,8192]{1,0:T(8,128)(2,1)} custom-call(s32[2]{0:T(128)S(1)} %pad_add_fusion.place_ref, bf16[32,8192]{1,0:T(8,128)(2,1)} %collective-permute-done.7.refs_0_, bf16[256,8192]{1,0:T(8,128)(2,1)} %place.2.refs_1_), custom_call_target="tpu_custom_call", output_to_operand_aliasing={{}: (2, {})} | custom-call | bytes 1048576 | tf_op jit(solution)/shard_map/place/pallas_call | solution.py:164
  (12 shorter events, 0.2 us)
Async XLA Ops:
  0.6 40.3 %copy-start = (bf16[32,8192]{1,0:T(8,128)(2,1)S(1)}, bf16[32,8192]{1,0:T(8,128)(2,1)}, u32[]{:S(2)}) copy-start(bf16[32,8192]{1,0:T(8,128)(2,1)} %base_ref.1) | copy-start | bytes 1572868
  0.6 40.2 %copy-start.1 = (f32[32,8192]{1,0:T(8,128)S(1)}, f32[32,8192]{1,0:T(8,128)}, u32[]{:S(2)}) copy-start(f32[32,8192]{1,0:T(8,128)} %momentum_ref.1) | copy-start | bytes 3145732
  18.1 8.5 %collective-permute-start.2 = (bf16[16,2048]{1,0:T(8,128)(2,1)S(1)}, bf16[16,2048]{1,0:T(8,128)(2,1)S(1)}, u32[]{:S(2)}, u32[]{:S(2)}) collective-permute-start(bf16[16,2048]{1,0:T(8,128)(2,1)S(1)} %reduce_sum.12), channel_id=1, source_target_pairs={{0,192},{64,0},{128,64},{192,128},{1,193},{65,1},{129,65},{193,129... | collective-permute-start | bytes 196616 | tf_op jit(solution)/shard_map/ppermute | solution.py:196
  23.3 5.4 %collective-permute-start.1 = (bf16[16,2048]{1,0:T(8,128)(2,1)S(1)}, bf16[16,2048]{1,0:T(8,128)(2,1)S(1)}, u32[]{:S(2)}, u32[]{:S(2)}) collective-permute-start(bf16[16,2048]{1,0:T(8,128)(2,1)S(1)} %reduce_sum.12), channel_id=1, source_target_pairs={{0,64},{64,128},{128,192},{192,0},{1,65},{65,129},{129,193},{193,1... | collective-permute-start | bytes 196616 | tf_op jit(solution)/shard_map/ppermute | solution.py:196
  23.3 7.1 %collective-permute-start = (bf16[16,2048]{1,0:T(8,128)(2,1)S(1)}, bf16[16,2048]{1,0:T(8,128)(2,1)S(1)}, u32[]{:S(2)}, u32[]{:S(2)}) collective-permute-start(bf16[16,2048]{1,0:T(8,128)(2,1)S(1)} %reduce_sum.12), channel_id=1, source_target_pairs={{0,128},{64,192},{128,0},{192,64},{1,129},{65,193},{129,1},{193,65... | collective-permute-start | bytes 196616 | tf_op jit(solution)/shard_map/ppermute | solution.py:196
  42.0 6.4 %collective-permute-start.3 = (bf16[16,8192]{1,0:T(8,128)(2,1)S(1)}, bf16[16,8192]{1,0:T(8,128)(2,1)S(1)}, u32[]{:S(2)}, u32[]{:S(2)}) collective-permute-start(bf16[16,8192]{1,0:T(8,128)(2,1)S(1)} %get-tuple-element.6), channel_id=1, source_target_pairs={{0,2},{2,4},{4,6},{6,0},{1,3},{3,5},{5,7},{7,1},{8,10},{10,12},{12... | collective-permute-start | bytes 786440 | tf_op jit(solution)/shard_map/ppermute | solution.py:215
  43.2 5.2 %collective-permute-start.5 = (bf16[16,8192]{1,0:T(8,128)(2,1)S(1)}, bf16[16,8192]{1,0:T(8,128)(2,1)S(1)}, u32[]{:S(2)}, u32[]{:S(2)}) collective-permute-start(bf16[16,8192]{1,0:T(8,128)(2,1)S(1)} %get-tuple-element.7), channel_id=1, source_target_pairs={{0,6},{2,0},{4,2},{6,4},{1,7},{3,1},{5,3},{7,5},{8,14},{10,8},{12,... | collective-permute-start | bytes 786440 | tf_op jit(solution)/shard_map/ppermute | solution.py:216
  44.7 16.4 %collective-permute-start.9 = (bf16[16,8192]{1,0:T(8,128)(2,1)S(1)}, bf16[16,8192]{1,0:T(8,128)(2,1)S(1)}, u32[]{:S(2)}, u32[]{:S(2)}) collective-permute-start(bf16[16,8192]{1,0:T(8,128)(2,1)S(1)} %get-tuple-element.6), channel_id=1, source_target_pairs={{0,6},{2,0},{4,2},{6,4},{1,7},{3,1},{5,3},{7,5},{8,14},{10,8},{12,... | collective-permute-start | bytes 786440 | tf_op jit(solution)/shard_map/ppermute | solution.py:216
  46.0 15.3 %collective-permute-start.8 = (bf16[16,8192]{1,0:T(8,128)(2,1)S(1)}, bf16[16,8192]{1,0:T(8,128)(2,1)S(1)}, u32[]{:S(2)}, u32[]{:S(2)}) collective-permute-start(bf16[16,8192]{1,0:T(8,128)(2,1)S(1)} %get-tuple-element.7), channel_id=1, source_target_pairs={{0,2},{2,4},{4,6},{6,0},{1,3},{3,5},{5,7},{7,1},{8,10},{10,12},{12... | collective-permute-start | bytes 786440 | tf_op jit(solution)/shard_map/ppermute | solution.py:215
  48.5 13.4 %collective-permute-start.4 = (bf16[16,8192]{1,0:T(8,128)(2,1)S(1)}, bf16[16,8192]{1,0:T(8,128)(2,1)S(1)}, u32[]{:S(2)}, u32[]{:S(2)}) collective-permute-start(bf16[16,8192]{1,0:T(8,128)(2,1)S(1)} %collective-permute-done.3.one_ref), channel_id=1, source_target_pairs={{0,2},{2,4},{4,6},{6,0},{1,3},{3,5},{5,7},{7,1},{8,10},{10,12},{12... | collective-permute-start | bytes 786440 | tf_op jit(solution)/shard_map/ppermute | solution.py:217
  48.5 13.4 %collective-permute-start.6 = (bf16[16,8192]{1,0:T(8,128)(2,1)S(1)}, bf16[16,8192]{1,0:T(8,128)(2,1)S(1)}, u32[]{:S(2)}, u32[]{:S(2)}) collective-permute-start(bf16[16,8192]{1,0:T(8,128)(2,1)S(1)} %collective-permute-done.5.two_ref), channel_id=1, source_target_pairs={{0,6},{2,0},{4,2},{6,4},{1,7},{3,1},{5,3},{7,5},{8,14},{10,8},{12,... | collective-permute-start | bytes 786440 | tf_op jit(solution)/shard_map/ppermute | solution.py:217
  51.1 14.6 %collective-permute-start.10 = (bf16[32,8192]{1,0:T(8,128)(2,1)S(1)}, bf16[32,8192]{1,0:T(8,128)(2,1)S(1)}, u32[]{:S(2)}, u32[]{:S(2)}) collective-permute-start(bf16[32,8192]{1,0:T(8,128)(2,1)S(1)} %get-tuple-element.8.refs_0_), channel_id=1, source_target_pairs={{0,1},{1,0},{2,3},{3,2},{4,5},{5,4},{6,7},{7,6},{8,9},{9,8},{10,11... | collective-permute-start | bytes 1572872 | tf_op jit(solution)/shard_map/ppermute | solution.py:208
  61.2 4.6 %collective-permute-start.12 = (bf16[32,8192]{1,0:T(8,128)(2,1)S(1)}, bf16[32,8192]{1,0:T(8,128)(2,1)S(1)}, u32[]{:S(2)}, u32[]{:S(2)}) collective-permute-start(bf16[32,8192]{1,0:T(8,128)(2,1)S(1)} %join.5.refs_2_), channel_id=1, source_target_pairs={{0,1},{1,0},{2,3},{3,2},{4,5},{5,4},{6,7},{7,6},{8,9},{9,8},{10,11... | collective-permute-start | bytes 1572872 | tf_op jit(solution)/shard_map/ppermute | solution.py:208
  61.3 4.5 %collective-permute-start.11 = (bf16[32,8192]{1,0:T(8,128)(2,1)S(1)}, bf16[32,8192]{1,0:T(8,128)(2,1)}, u32[]{:S(2)}, u32[]{:S(2)}) collective-permute-start(bf16[32,8192]{1,0:T(8,128)(2,1)S(1)} %join.4.refs_1_), channel_id=1, source_target_pairs={{0,1},{1,0},{2,3},{3,2},{4,5},{5,4},{6,7},{7,6},{8,9},{9,8},{10,11... | collective-permute-start | bytes 1572872 | tf_op jit(solution)/shard_map/ppermute | solution.py:208
  61.9 6.8 %collective-permute-start.7 = (bf16[32,8192]{1,0:T(8,128)(2,1)S(1)}, bf16[32,8192]{1,0:T(8,128)(2,1)}, u32[]{:S(2)}, u32[]{:S(2)}) collective-permute-start(bf16[32,8192]{1,0:T(8,128)(2,1)S(1)} %join.3.refs_6_), channel_id=1, source_target_pairs={{0,1},{1,0},{2,3},{3,2},{4,5},{5,4},{6,7},{7,6},{8,9},{9,8},{10,11... | collective-permute-start | bytes 1572872 | tf_op jit(solution)/shard_map/ppermute | solution.py:208

commit v4 on v3

v4 whole, which is shorter than its diff:
```python
import functools

import jax
import jax.numpy as jnp
from jax import lax
from jax.experimental import pallas as pl
from jax.experimental.pallas import tpu as pltpu
from jax.sharding import Mesh, PartitionSpec as P

BLOCK = 32

floor_value = 0.5
spread_ratio = 3.0
code_peak = 6.0
outer_rate = 0.7
momentum_coef = 0.9

ROWS = 32
HALF = 16
COLS = 8192
PIECES = 4
WIDE = COLS // PIECES
LANES = 128

SMALL = pltpu.CompilerParams(vmem_limit_bytes=8 << 20)
TINY = pltpu.CompilerParams(vmem_limit_bytes=4 << 20)


def encode_kernel(local_hbm, base_hbm, out_ref, local_ref, base_ref, sems):
    copies = []
    for half in range(2):
        rows = pl.ds(half * HALF, HALF)
        copies.append(
            (
                pltpu.make_async_copy(
                    local_hbm.at[0, rows, :], local_ref.at[half], sems.at[0, half]
                ),
                pltpu.make_async_copy(base_hbm.at[rows, :], base_ref.at[half], sems.at[1, half]),
            )
        )
    for pair in copies:
        for copy in pair:
            copy.start()
    block = lax.broadcasted_iota(jnp.int32, (LANES, LANES), 0) // BLOCK
    block_t = lax.broadcasted_iota(jnp.int32, (LANES, LANES), 1) // BLOCK
    same_block = jnp.where(block == block_t, 1.0 / BLOCK, 0.0).astype(jnp.float32)
    for k in range(2 * PIECES):
        half, piece = k // PIECES, k % PIECES
        if piece == 0:
            for copy in copies[half]:
                copy.wait()
        cols = pl.ds(piece * WIDE, WIDE)
        grad = base_ref[half, :, cols].astype(jnp.float32) - local_ref[half, :, cols].astype(
            jnp.float32
        )
        tall = jnp.concatenate(
            [grad[:, i * LANES : (i + 1) * LANES] for i in range(WIDE // LANES)], axis=0
        )
        mean_square = jnp.dot(
            tall * tall,
            same_block,
            precision=lax.Precision.HIGHEST,
            preferred_element_type=jnp.float32,
        )
        floored = jnp.maximum(mean_square, floor_value * floor_value)
        scale = (floored * lax.rsqrt(floored) * (1.0 / spread_ratio)).astype(jnp.bfloat16)
        limit = code_peak * scale.astype(jnp.float32)
        decoded = jnp.clip(tall, -limit, limit).astype(jnp.bfloat16)
        for i in range(WIDE // LANES):
            out_ref[k, :, i * LANES : (i + 1) * LANES] = decoded[i * HALF : (i + 1) * HALF]


def in_vmem(value):
    return pltpu.with_memory_space_constraint(value, pltpu.VMEM)


def in_hbm(value):
    return pltpu.with_memory_space_constraint(value, pltpu.HBM)


def encode(local_params, base_rows):
    halves = (2, HALF, COLS)
    return pl.pallas_call(
        encode_kernel,
        out_shape=pltpu.VMEM((2 * PIECES, HALF, WIDE), jnp.bfloat16),
        in_specs=[pl.BlockSpec(memory_space=pltpu.HBM)] * 2,
        scratch_shapes=[
            pltpu.VMEM(halves, jnp.bfloat16),
            pltpu.VMEM(halves, jnp.bfloat16),
            pltpu.SemaphoreType.DMA((2, 2)),
        ],
        compiler_params=SMALL,
        name="encode",
    )(in_hbm(local_params), in_hbm(base_rows))


def pieces():
    for half in range(2):
        for piece in range(PIECES):
            rows, cols = pl.ds(half * HALF, HALF), pl.ds(piece * WIDE, WIDE)
            yield half, half * PIECES + piece, rows, cols


def step_momentum(average, momentum):
    return momentum_coef * momentum + average


def base_kernel(average_ref, base_ref, momentum_ref, *new_base_refs):
    for half, k, rows, cols in pieces():
        average = average_ref[k].astype(jnp.float32)
        new_momentum = step_momentum(average, momentum_ref[rows, cols])
        new_base_refs[half][:, cols] = (
            base_ref[rows, cols].astype(jnp.float32)
            - outer_rate * (average + momentum_coef * new_momentum)
        ).astype(jnp.bfloat16)


def update_base(average, base_rows, momentum):
    part = pltpu.VMEM((HALF, COLS), jnp.bfloat16)
    return pl.pallas_call(
        base_kernel,
        out_shape=(part, part),
        compiler_params=SMALL,
        name="update_base",
    )(in_vmem(average), base_rows, momentum)


def momentum_kernel(average_ref, momentum_hbm, new_hbm, momentum_ref, new_ref, sems):
    reads, writes = [], []
    for half in range(2):
        rows = pl.ds(half * HALF, HALF)
        reads.append(
            pltpu.make_async_copy(momentum_hbm.at[rows, :], momentum_ref.at[half], sems.at[0, half])
        )
        writes.append(pltpu.make_async_copy(new_ref.at[half], new_hbm.at[rows, :], sems.at[1, half]))
    for copy in reads:
        copy.start()
    for half in range(2):
        reads[half].wait()
        for piece in range(PIECES):
            cols = pl.ds(piece * WIDE, WIDE)
            new_ref[half, :, cols] = step_momentum(
                average_ref[half * PIECES + piece].astype(jnp.float32), momentum_ref[half, :, cols]
            )
        writes[half].start()
    for copy in writes:
        copy.wait()


def update_momentum(average, momentum):
    hbm = pl.BlockSpec(memory_space=pltpu.HBM)
    return pl.pallas_call(
        momentum_kernel,
        out_shape=pltpu.HBM((ROWS, COLS), jnp.float32),
        in_specs=[pl.BlockSpec(memory_space=pltpu.VMEM), hbm],
        out_specs=hbm,
        scratch_shapes=[
            pltpu.VMEM((2, HALF, COLS), jnp.float32),
            pltpu.VMEM((2, HALF, COLS), jnp.float32),
            pltpu.SemaphoreType.DMA((2, 2)),
        ],
        compiler_params=SMALL,
        name="update_momentum",
    )(in_vmem(average), in_hbm(momentum))


def after_kernel(*refs):
    pass


def after(part, ready):
    vmem, hbm = pl.BlockSpec(memory_space=pltpu.VMEM), pl.BlockSpec(memory_space=pltpu.HBM)
    return pl.pallas_call(
        after_kernel,
        out_shape=(pltpu.VMEM(part.shape, part.dtype), pltpu.HBM(ready.shape, ready.dtype)),
        in_specs=[vmem, hbm],
        out_specs=(vmem, hbm),
        input_output_aliases={0: 0, 1: 1},
        compiler_params=TINY,
        name="after",
    )(in_vmem(part), in_hbm(ready))


def join_kernel(one_ref, two_ref, out_ref):
    out_ref[pl.ds(0, HALF), :] = one_ref[...]
    out_ref[pl.ds(HALF, HALF), :] = two_ref[...]


def join(one, two):
    return pl.pallas_call(
        join_kernel,
        out_shape=pltpu.VMEM((ROWS, COLS), jnp.bfloat16),
        compiler_params=TINY,
        name="join",
    )(in_vmem(one), in_vmem(two))


def join_after_kernel(one_ref, two_ref, *refs):
    join_kernel(one_ref, two_ref, refs[len(refs) // 2])


def join_after(one, two, *ready):
    vmem, hbm = pl.BlockSpec(memory_space=pltpu.VMEM), pl.BlockSpec(memory_space=pltpu.HBM)
    count = len(ready)
    return pl.pallas_call(
        join_after_kernel,
        out_shape=(pltpu.VMEM((ROWS, COLS), jnp.bfloat16),)
        + tuple(pltpu.HBM(array.shape, array.dtype) for array in ready),
        in_specs=[vmem, vmem] + [hbm] * count,
        out_specs=(vmem,) + (hbm,) * count,
        input_output_aliases={2 + k: 1 + k for k in range(count)},
        compiler_params=TINY,
        name="join_after",
    )(in_vmem(one), in_vmem(two), *[in_hbm(array) for array in ready])


def place_kernel(steps, spot_ref, *refs):
    parts, out_ref, sems = refs[: len(steps)], refs[-2], refs[-1]
    copies = []
    for k, (ref, (step, other, half)) in enumerate(zip(parts, steps)):
        x, core = lax.rem(spot_ref[0] + step, 4), lax.rem(spot_ref[1] + other, 2)
        start = pl.multiple_of((x * 2 + core) * ROWS + half * HALF, HALF)
        copies.append(
            pltpu.make_async_copy(ref, out_ref.at[pl.ds(start, ref.shape[0]), :], sems.at[k])
        )
    for copy in copies:
        copy.start()
    for copy in copies:
        copy.wait()


def place(spot, parts, whole=None):
    steps, count = tuple(parts), len(parts)
    keep = [] if whole is None else [whole]
    hbm = pl.BlockSpec(memory_space=pltpu.HBM)
    return pl.pallas_call(
        functools.partial(place_kernel, steps),
        out_shape=pltpu.HBM((8 * ROWS, COLS), jnp.bfloat16),
        in_specs=[pl.BlockSpec(memory_space=pltpu.SMEM)]
        + [pl.BlockSpec(memory_space=pltpu.VMEM)] * count
        + [hbm] * len(keep),
        out_specs=hbm,
        scratch_shapes=[pltpu.SemaphoreType.DMA((count,))],
        input_output_aliases={count + 1: 0} if keep else {},
        compiler_params=TINY,
        cost_estimate=pl.CostEstimate(
            flops=0, transcendentals=0, bytes_accessed=sum(part.size for part in parts.values()) * 4
        ),
        name="place",
    )(spot, *[in_vmem(part) for part in parts.values()], *[in_hbm(w) for w in keep])


def ring(n, step):
    return [(i, (i + step) % n) for i in range(n)]


def shards(local_params, base_params, momentum):
    decoded = encode(local_params, base_params)

    near = ("zl", "y")
    received = lax.all_to_all(decoded, near, 0, 0, tiled=True)
    partial = jnp.sum(received.astype(jnp.float32), axis=0).astype(jnp.bfloat16)

    one, two, three = [
        lax.ppermute(partial, "zh", [(i, i ^ k) for i in range(4)]).astype(jnp.float32)
        for k in (1, 2, 3)
    ]
    total = (partial.astype(jnp.float32) + one) + (two + three)
    average = (total / 32).astype(jnp.bfloat16)

    gathered = lax.all_to_all(
        jnp.broadcast_to(average[None], (8,) + average.shape), near, 0, 0, tiled=True
    )

    first, second = update_base(gathered, base_params, momentum)
    new_momentum = update_momentum(gathered, momentum)

    def swap(part):
        return lax.ppermute(part, "core", ring(2, 1))

    spot = jnp.stack([lax.axis_index("x"), lax.axis_index("core")]).astype(jnp.int32)
    left = [lax.ppermute(half, "x", ring(4, 1)) for half in (first, second)]
    right = [lax.ppermute(half, "x", ring(4, 3)) for half in (second, first)]
    left[0], new_momentum = after(left[0], new_momentum)
    far = [lax.ppermute(left[0], "x", ring(4, 1)), lax.ppermute(right[0], "x", ring(4, 3))]
    from_left = join(left[0], left[1])
    from_right = join(right[1], right[0])
    new_base = place(
        spot,
        {
            (0, 0, 0): first,
            (0, 0, 1): second,
            (0, 1, 0): swap(first),
            (0, 1, 1): swap(second),
            (3, 0, 0): from_left,
            (1, 0, 0): from_right,
        },
    )
    from_far, new_base = join_after(far[0], far[1], new_base)
    new_base = place(
        spot,
        {
            (3, 1, 0): swap(from_left),
            (1, 1, 0): swap(from_right),
            (2, 0, 0): from_far,
        },
        new_base,
    )
    new_base = place(spot, {(2, 1, 0): swap(from_far)}, new_base)
    return (new_base, new_momentum)


def solution(mesh):
    fine = Mesh(mesh.devices.reshape(4, 2, 4, 4, 2), ("zh", "zl", "y", "x", "core"))
    rep, fsdp = ("zh", "zl", "y"), ("x", "core")
    in_specs = (P(rep, fsdp, None), P(fsdp, None), P(fsdp, None))
    out_specs = (P(), P(fsdp, None))
    return jax.shard_map(shards, mesh=fine, in_specs=in_specs, out_specs=out_specs, check_vma=False)
```

time: 70.9 us -> 69.3 us (0.977)
  starting transfers between devices: 29.6 us -> 24.1 us
  waiting for transfers between devices: 6.2 us -> 9.32 us
  Pallas kernels: 8.69 us -> 9.98 us
    ppermute x4 -> x5, starting transfers between devices: 14.3 us -> 9.69 us  [swap(): return lax.ppermute(part, 'core', ring(2, 1))]
    ppermute x1, waiting for transfers between devices: 0.01 us -> 2.61 us  [shards(): lax.ppermute(right[0], 'x', ring(4, 3))]
    ppermute x2, waiting for transfers between devices: 2.29 us -> 0.01 us  [shards(): left = [lax.ppermute(half, 'x', ring(4, 1)) for half in (first, second)]]
    ppermute x3, waiting for transfers between devices: 3.89 us -> 6.08 us  [shards(): lax.ppermute(partial, 'zh', [(i, i ^ k) for i in range(4)])]
    ppermute x1, starting transfers between devices: 2.67 us -> 0.83 us  [shards(): lax.ppermute(right[0], 'x', ring(4, 3))]
    ppermute x2, starting transfers between devices: 2.73 us -> 4.14 us  [shards(): right = [lax.ppermute(half, 'x', ring(4, 3)) for half in (second, first)]]
    pallas_call x3 -> x7, Pallas kernels: 6.01 us -> 7.4 us  [the longest x3 4.98 us: place(): pl.pallas_call(functools.partial(place_kernel, steps), out_shape=pltpu.HB...]
    ppermute x3, starting transfers between devices: 8.45 us -> 7.39 us  [shards(): lax.ppermute(partial, 'zh', [(i, i ^ k) for i in range(4)])]
  transfers between devices with their start and end apart: 13 -> 14, of which waited for: 3 -> 3; matrix products, arithmetic and copies ran while one was open for 0% -> 0% of each run, Pallas kernels for 4% -> 8%
where the time goes in v4:
time: 69.3 us; the launch traced here: 69.1 us
  blocking collectives  24.7 us (36%)
  starting transfers between devices  24.1 us (35%)
  Pallas kernels  9.98 us (14%)
  waiting for transfers between devices  9.32 us (13%)
  between operations  0.77 us (1%)
    all_to_all x1, blocking collectives, shards(): received = lax.all_to_all(decoded, near, 0, 0, tiled=True)  14.8 us
    all_to_all x1, blocking collectives, shards(): lax.all_to_all(jnp.broadcast_to(average[None], (8,) + average.shape), nea...  9.89 us
    ppermute x5, starting transfers between devices, swap(): return lax.ppermute(part, 'core', ring(2, 1))  9.69 us
    ppermute x3, starting transfers between devices, shards(): lax.ppermute(partial, 'zh', [(i, i ^ k) for i in range(4)])  7.39 us
    ppermute x3, waiting for transfers between devices, shards(): lax.ppermute(partial, 'zh', [(i, i ^ k) for i in range(4)])  6.08 us
    pallas_call x3, Pallas kernels, place(): pl.pallas_call(functools.partial(place_kernel, steps), out_shape=pltpu.HB...  4.98 us
    ppermute x2, starting transfers between devices, shards(): right = [lax.ppermute(half, 'x', ring(4, 3)) for half in (second, first)]  4.14 us
    ppermute x1, waiting for transfers between devices, shards(): lax.ppermute(right[0], 'x', ring(4, 3))  2.61 us
  transfers between devices with their start and end apart: 14, of which 3 were waited for; matrix products, arithmetic and copies ran while one was open for 0% of the time, Pallas kernels for 8%

profile of v4, /device:TPU:1, one launch (start us, length us, event | category | flops | bytes accessed | tf_op | source)
XLA Modules:
  0.0 69.1 jit_solution(9927368005730971471)
XLA Ops:
  0.6 0.0 copy-start
  0.7 2.5 %encode.1 = bf16[8,16,2048]{2,1,0:T(8,128)(2,1)S(1)} custom-call(bf16[1,32,8192]{2,1,0:T(8,128)(2,1)} %local_hbm.1, bf16[32,8192]{1,0:T(8,128)(2,1)} %base_ref.1), custom_call_target="tpu_custom_call" | custom-call | tf_op jit(solution)/shard_map/encode/pallas_call | solution.py:83
  3.2 14.8 %all_to_all.10 = bf16[8,16,2048]{2,1,0:T(8,128)(2,1)S(1)} all-to-all(bf16[8,16,2048]{2,1,0:T(8,128)(2,1)S(1)} %encode.1), channel_id=1, replica_groups=mesh['zh'=4,'zl'=2,'y'=4,'x'=4,'core'=2] {'zl','y'}, dimensions={0} | all-to-all | bytes 1048576 | tf_op jit(solution)/shard_map/all_to_all | solution.py:261
  18.0 0.1 reduce_sum.12
  18.0 5.2 %collective-permute-start.2 = (bf16[16,2048]{1,0:T(8,128)(2,1)S(1)}, bf16[16,2048]{1,0:T(8,128)(2,1)S(1)}, u32[]{:S(2)}, u32[]{:S(2)}) collective-permute-start(bf16[16,2048]{1,0:T(8,128)(2,1)S(1)} %reduce_sum.12), channel_id=1, source_target_pairs={{0,192},{64,128},{128,64},{192,0},{1,193},{65,129},{129,65},{193,1... | collective-permute-start | bytes 196616 | tf_op jit(solution)/shard_map/ppermute | solution.py:265
  23.3 1.2 %collective-permute-start.1 = (bf16[16,2048]{1,0:T(8,128)(2,1)S(1)}, bf16[16,2048]{1,0:T(8,128)(2,1)S(1)}, u32[]{:S(2)}, u32[]{:S(2)}) collective-permute-start(bf16[16,2048]{1,0:T(8,128)(2,1)S(1)} %reduce_sum.12), channel_id=1, source_target_pairs={{0,128},{64,192},{128,0},{192,64},{1,129},{65,193},{129,1},{193,65... | collective-permute-start | bytes 196616 | tf_op jit(solution)/shard_map/ppermute | solution.py:265
  24.4 1.0 %collective-permute-start = (bf16[16,2048]{1,0:T(8,128)(2,1)S(1)}, bf16[16,2048]{1,0:T(8,128)(2,1)S(1)}, u32[]{:S(2)}, u32[]{:S(2)}) collective-permute-start(bf16[16,2048]{1,0:T(8,128)(2,1)S(1)} %reduce_sum.12), channel_id=1, source_target_pairs={{0,64},{64,0},{128,192},{192,128},{1,65},{65,1},{129,193},{193,129... | collective-permute-start | bytes 196616 | tf_op jit(solution)/shard_map/ppermute | solution.py:265
  25.4 0.0 collective-permute-done.2
  25.4 6.1 %collective-permute-done.1 = bf16[16,2048]{1,0:T(8,128)(2,1)S(1)} collective-permute-done((bf16[16,2048]{1,0:T(8,128)(2,1)S(1)}, bf16[16,2048]{1,0:T(8,128)(2,1)S(1)}, u32[]{:S(2)}, u32[]{:S(2)}) %collective-permute-start.1) | collective-permute-done | bytes 65568 | tf_op jit(solution)/shard_map/ppermute | solution.py:265
  31.5 0.0 collective-permute-done
  31.6 9.9 %all_to_all.11.average_ref = bf16[8,16,2048]{2,1,0:T(8,128)(2,1)S(1)} all-to-all(bf16[8,16,2048]{2,1,0:T(8,128)(2,1)S(1)} %broadcast_in_dim.2), channel_id=1, replica_groups=mesh['zh'=4,'zl'=2,'y'=4,'x'=4,'core'=2] {'zl','y'}, dimensions={0} | all-to-all | bytes 1048576 | tf_op jit(solution)/shard_map/all_to_all | solution.py:271
  41.5 0.3 update_base.1
  41.8 1.3 %collective-permute-start.3 = (bf16[16,8192]{1,0:T(8,128)(2,1)S(1)}, bf16[16,8192]{1,0:T(8,128)(2,1)S(1)}, u32[]{:S(2)}, u32[]{:S(2)}) collective-permute-start(bf16[16,8192]{1,0:T(8,128)(2,1)S(1)} %get-tuple-element.8.refs_0_), channel_id=1, source_target_pairs={{0,2},{2,4},{4,6},{6,0},{1,3},{3,5},{5,7},{7,1},{8,10},{10,12},{12... | collective-permute-start | bytes 786440 | tf_op jit(solution)/shard_map/ppermute | solution.py:282
  43.1 1.5 %collective-permute-start.5 = (bf16[16,8192]{1,0:T(8,128)(2,1)S(1)}, bf16[16,8192]{1,0:T(8,128)(2,1)S(1)}, u32[]{:S(2)}, u32[]{:S(2)}) collective-permute-start(bf16[16,8192]{1,0:T(8,128)(2,1)S(1)} %get-tuple-element.10.refs_1_), channel_id=1, source_target_pairs={{0,6},{2,0},{4,2},{6,4},{1,7},{3,1},{5,3},{7,5},{8,14},{10,8},{12,... | collective-permute-start | bytes 786440 | tf_op jit(solution)/shard_map/ppermute | solution.py:283
  44.6 0.0 collective-permute-start.9
  44.6 2.7 %collective-permute-start.10 = (bf16[16,8192]{1,0:T(8,128)(2,1)S(1)}, bf16[16,8192]{1,0:T(8,128)(2,1)S(1)}, u32[]{:S(2)}, u32[]{:S(2)}) collective-permute-start(bf16[16,8192]{1,0:T(8,128)(2,1)S(1)} %get-tuple-element.8.refs_0_), channel_id=1, source_target_pairs={{0,6},{2,0},{4,2},{6,4},{1,7},{3,1},{5,3},{7,5},{8,14},{10,8},{12,... | collective-permute-start | bytes 786440 | tf_op jit(solution)/shard_map/ppermute | solution.py:283
  47.2 5.6 %collective-permute-start.7 = (bf16[16,8192]{1,0:T(8,128)(2,1)S(1)}, bf16[16,8192]{1,0:T(8,128)(2,1)S(1)}, u32[]{:S(2)}, u32[]{:S(2)}) collective-permute-start(bf16[16,8192]{1,0:T(8,128)(2,1)S(1)} %get-tuple-element.8.refs_0_), channel_id=1, source_target_pairs={{0,1},{1,0},{2,3},{3,2},{4,5},{5,4},{6,7},{7,6},{8,9},{9,8},{10,11... | collective-permute-start | bytes 786440 | tf_op jit(solution)/shard_map/ppermute | solution.py:279
  52.8 2.1 %update_momentum.1.refs_1_ = f32[32,8192]{1,0:T(8,128)} custom-call(bf16[8,16,2048]{2,1,0:T(8,128)(2,1)S(1)} %all_to_all.11.average_ref, f32[32,8192]{1,0:T(8,128)} %momentum_hbm.1), custom_call_target="tpu_custom_call" | custom-call | tf_op jit(solution)/shard_map/update_momentum/pallas_call | solution.py:152
  54.9 0.0 collective-permute-done.3.refs_0_
  55.0 0.1 collective-permute-start.8
  55.1 0.8 %collective-permute-start.6 = (bf16[16,8192]{1,0:T(8,128)(2,1)S(1)}, bf16[16,8192]{1,0:T(8,128)(2,1)S(1)}, u32[]{:S(2)}, u32[]{:S(2)}) collective-permute-start(bf16[16,8192]{1,0:T(8,128)(2,1)S(1)} %collective-permute-done.5.two_ref), channel_id=1, source_target_pairs={{0,6},{2,0},{4,2},{6,4},{1,7},{3,1},{5,3},{7,5},{8,14},{10,8},{12,... | collective-permute-start | bytes 786440 | tf_op jit(solution)/shard_map/ppermute | solution.py:285
  55.9 0.7 %collective-permute-start.4 = (bf16[16,8192]{1,0:T(8,128)(2,1)S(1)}, bf16[16,8192]{1,0:T(8,128)(2,1)S(1)}, u32[]{:S(2)}, u32[]{:S(2)}) collective-permute-start(bf16[16,8192]{1,0:T(8,128)(2,1)S(1)} %get-tuple-element.9.one_ref), channel_id=1, source_target_pairs={{0,2},{2,4},{4,6},{6,0},{1,3},{3,5},{5,7},{7,1},{8,10},{10,12},{12... | collective-permute-start | bytes 786440 | tf_op jit(solution)/shard_map/ppermute | solution.py:285
  56.6 0.1 pad_add_fusion.spot_ref
  56.7 0.0 collective-permute-done.10.one_ref
  56.7 1.2 %collective-permute-start.12 = (bf16[32,8192]{1,0:T(8,128)(2,1)S(1)}, bf16[32,8192]{1,0:T(8,128)(2,1)S(1)}, u32[]{:S(2)}, u32[]{:S(2)}) collective-permute-start(bf16[32,8192]{1,0:T(8,128)(2,1)S(1)} %join.2.refs_4_), channel_id=1, source_target_pairs={{0,1},{1,0},{2,3},{3,2},{4,5},{5,4},{6,7},{7,6},{8,9},{9,8},{10,11... | collective-permute-start | bytes 1572872 | tf_op jit(solution)/shard_map/ppermute | solution.py:279
  58.0 0.1 collective-permute-start.13
  58.1 1.9 %place.3.refs_0_ = bf16[256,8192]{1,0:T(8,128)(2,1)} custom-call(s32[2]{0:T(128)S(1)} %pad_add_fusion.spot_ref, bf16[16,8192]{1,0:T(8,128)(2,1)S(1)} %get-tuple-element.8.refs_0_, bf16[16,8192]{1,0:T(8,128)(2,1)S(1)} %get-tuple-element.10.refs_1_, bf16[16,8192]{1,0:T(8,128)(2,1)S(1)} %collective-permute-done.7.refs_2_, ...), custom_call_target="tpu_custom_call" | custom-call | bytes 4194304 | tf_op jit(solution)/shard_map/place/pallas_call | solution.py:236
  60.0 2.6 %collective-permute-done.6.two_ref = bf16[16,8192]{1,0:T(8,128)(2,1)S(1)} collective-permute-done((bf16[16,8192]{1,0:T(8,128)(2,1)S(1)}, bf16[16,8192]{1,0:T(8,128)(2,1)S(1)}, u32[]{:S(2)}, u32[]{:S(2)}) %collective-permute-start.6) | collective-permute-done | bytes 262176 | tf_op jit(solution)/shard_map/ppermute | solution.py:285
  62.6 0.6 collective-permute-done.4.one_ref
  63.3 2.7 %collective-permute-start.11 = (bf16[32,8192]{1,0:T(8,128)(2,1)S(1)}, bf16[32,8192]{1,0:T(8,128)(2,1)S(1)}, u32[]{:S(2)}, u32[]{:S(2)}) collective-permute-start(bf16[32,8192]{1,0:T(8,128)(2,1)S(1)} %get-tuple-element.11.refs_2_), channel_id=1, source_target_pairs={{0,1},{1,0},{2,3},{3,2},{4,5},{5,4},{6,7},{7,6},{8,9},{9,8},{10,11... | collective-permute-start | bytes 1572872 | tf_op jit(solution)/shard_map/ppermute | solution.py:279
  66.0 1.7 %place.4.refs_1_ = bf16[256,8192]{1,0:T(8,128)(2,1)} custom-call(s32[2]{0:T(128)S(1)} %pad_add_fusion.spot_ref, bf16[32,8192]{1,0:T(8,128)(2,1)S(1)} %collective-permute-done.12.refs_0_, bf16[32,8192]{1,0:T(8,128)(2,1)S(1)} %collective-permute-done.13.refs_1_, bf16[32,8192]{1,0:T(8,128)(2,1)S(1)} %get-tuple-element.11.refs_2_, ...), custom_call_target="tpu_custom_call", output_to_operand_aliasing={{}: (4, {})} | custom-call | bytes 3145728 | tf_op jit(solution)/shard_map/place/pallas_call | solution.py:236
  67.7 1.4 %place.5 = bf16[256,8192]{1,0:T(8,128)(2,1)} custom-call(s32[2]{0:T(128)S(1)} %pad_add_fusion.spot_ref, bf16[32,8192]{1,0:T(8,128)(2,1)S(1)} %collective-permute-done.11.refs_0_, bf16[256,8192]{1,0:T(8,128)(2,1)} %place.4.refs_1_), custom_call_target="tpu_custom_call", output_to_operand_aliasing={{}: (2, {})} | custom-call | bytes 1048576 | tf_op jit(solution)/shard_map/place/pallas_call | solution.py:236
  (16 shorter events, 0.2 us)
Async XLA Ops:
  0.6 40.9 %copy-start.1 = (bf16[32,8192]{1,0:T(8,128)(2,1)S(1)}, bf16[32,8192]{1,0:T(8,128)(2,1)}, u32[]{:S(2)}) copy-start(bf16[32,8192]{1,0:T(8,128)(2,1)} %base_ref.1) | copy-start | bytes 1572868
  0.6 40.9 %copy-start = (f32[32,8192]{1,0:T(8,128)S(1)}, f32[32,8192]{1,0:T(8,128)}, u32[]{:S(2)}) copy-start(f32[32,8192]{1,0:T(8,128)} %momentum_hbm.1) | copy-start | bytes 3145732
  18.0 7.4 %collective-permute-start.2 = (bf16[16,2048]{1,0:T(8,128)(2,1)S(1)}, bf16[16,2048]{1,0:T(8,128)(2,1)S(1)}, u32[]{:S(2)}, u32[]{:S(2)}) collective-permute-start(bf16[16,2048]{1,0:T(8,128)(2,1)S(1)} %reduce_sum.12), channel_id=1, source_target_pairs={{0,192},{64,128},{128,64},{192,0},{1,193},{65,129},{129,65},{193,1... | collective-permute-start | bytes 196616 | tf_op jit(solution)/shard_map/ppermute | solution.py:265
  23.3 8.3 %collective-permute-start.1 = (bf16[16,2048]{1,0:T(8,128)(2,1)S(1)}, bf16[16,2048]{1,0:T(8,128)(2,1)S(1)}, u32[]{:S(2)}, u32[]{:S(2)}) collective-permute-start(bf16[16,2048]{1,0:T(8,128)(2,1)S(1)} %reduce_sum.12), channel_id=1, source_target_pairs={{0,128},{64,192},{128,0},{192,64},{1,129},{65,193},{129,1},{193,65... | collective-permute-start | bytes 196616 | tf_op jit(solution)/shard_map/ppermute | solution.py:265
  24.4 7.1 %collective-permute-start = (bf16[16,2048]{1,0:T(8,128)(2,1)S(1)}, bf16[16,2048]{1,0:T(8,128)(2,1)S(1)}, u32[]{:S(2)}, u32[]{:S(2)}) collective-permute-start(bf16[16,2048]{1,0:T(8,128)(2,1)S(1)} %reduce_sum.12), channel_id=1, source_target_pairs={{0,64},{64,0},{128,192},{192,128},{1,65},{65,1},{129,193},{193,129... | collective-permute-start | bytes 196616 | tf_op jit(solution)/shard_map/ppermute | solution.py:265
  41.8 13.1 %collective-permute-start.3 = (bf16[16,8192]{1,0:T(8,128)(2,1)S(1)}, bf16[16,8192]{1,0:T(8,128)(2,1)S(1)}, u32[]{:S(2)}, u32[]{:S(2)}) collective-permute-start(bf16[16,8192]{1,0:T(8,128)(2,1)S(1)} %get-tuple-element.8.refs_0_), channel_id=1, source_target_pairs={{0,2},{2,4},{4,6},{6,0},{1,3},{3,5},{5,7},{7,1},{8,10},{10,12},{12... | collective-permute-start | bytes 786440 | tf_op jit(solution)/shard_map/ppermute | solution.py:282
  43.1 12.0 %collective-permute-start.5 = (bf16[16,8192]{1,0:T(8,128)(2,1)S(1)}, bf16[16,8192]{1,0:T(8,128)(2,1)S(1)}, u32[]{:S(2)}, u32[]{:S(2)}) collective-permute-start(bf16[16,8192]{1,0:T(8,128)(2,1)S(1)} %get-tuple-element.10.refs_1_), channel_id=1, source_target_pairs={{0,6},{2,0},{4,2},{6,4},{1,7},{3,1},{5,3},{7,5},{8,14},{10,8},{12,... | collective-permute-start | bytes 786440 | tf_op jit(solution)/shard_map/ppermute | solution.py:283
  44.6 11.3 %collective-permute-start.9 = (bf16[16,8192]{1,0:T(8,128)(2,1)S(1)}, bf16[16,8192]{1,0:T(8,128)(2,1)S(1)}, u32[]{:S(2)}, u32[]{:S(2)}) collective-permute-start(bf16[16,8192]{1,0:T(8,128)(2,1)S(1)} %get-tuple-element.10.refs_1_), channel_id=1, source_target_pairs={{0,2},{2,4},{4,6},{6,0},{1,3},{3,5},{5,7},{7,1},{8,10},{10,12},{12... | collective-permute-start | bytes 786440 | tf_op jit(solution)/shard_map/ppermute | solution.py:282
  44.6 12.2 %collective-permute-start.10 = (bf16[16,8192]{1,0:T(8,128)(2,1)S(1)}, bf16[16,8192]{1,0:T(8,128)(2,1)S(1)}, u32[]{:S(2)}, u32[]{:S(2)}) collective-permute-start(bf16[16,8192]{1,0:T(8,128)(2,1)S(1)} %get-tuple-element.8.refs_0_), channel_id=1, source_target_pairs={{0,6},{2,0},{4,2},{6,4},{1,7},{3,1},{5,3},{7,5},{8,14},{10,8},{12,... | collective-permute-start | bytes 786440 | tf_op jit(solution)/shard_map/ppermute | solution.py:283
  47.2 10.7 %collective-permute-start.7 = (bf16[16,8192]{1,0:T(8,128)(2,1)S(1)}, bf16[16,8192]{1,0:T(8,128)(2,1)S(1)}, u32[]{:S(2)}, u32[]{:S(2)}) collective-permute-start(bf16[16,8192]{1,0:T(8,128)(2,1)S(1)} %get-tuple-element.8.refs_0_), channel_id=1, source_target_pairs={{0,1},{1,0},{2,3},{3,2},{4,5},{5,4},{6,7},{7,6},{8,9},{9,8},{10,11... | collective-permute-start | bytes 786440 | tf_op jit(solution)/shard_map/ppermute | solution.py:279
  55.0 3.1 %collective-permute-start.8 = (bf16[16,8192]{1,0:T(8,128)(2,1)S(1)}, bf16[16,8192]{1,0:T(8,128)(2,1)S(1)}, u32[]{:S(2)}, u32[]{:S(2)}) collective-permute-start(bf16[16,8192]{1,0:T(8,128)(2,1)S(1)} %get-tuple-element.10.refs_1_), channel_id=1, source_target_pairs={{0,1},{1,0},{2,3},{3,2},{4,5},{5,4},{6,7},{7,6},{8,9},{9,8},{10,11... | collective-permute-start | bytes 786440 | tf_op jit(solution)/shard_map/ppermute | solution.py:279
  55.1 7.5 %collective-permute-start.6 = (bf16[16,8192]{1,0:T(8,128)(2,1)S(1)}, bf16[16,8192]{1,0:T(8,128)(2,1)S(1)}, u32[]{:S(2)}, u32[]{:S(2)}) collective-permute-start(bf16[16,8192]{1,0:T(8,128)(2,1)S(1)} %collective-permute-done.5.two_ref), channel_id=1, source_target_pairs={{0,6},{2,0},{4,2},{6,4},{1,7},{3,1},{5,3},{7,5},{8,14},{10,8},{12,... | collective-permute-start | bytes 786440 | tf_op jit(solution)/shard_map/ppermute | solution.py:285
  55.9 7.3 %collective-permute-start.4 = (bf16[16,8192]{1,0:T(8,128)(2,1)S(1)}, bf16[16,8192]{1,0:T(8,128)(2,1)S(1)}, u32[]{:S(2)}, u32[]{:S(2)}) collective-permute-start(bf16[16,8192]{1,0:T(8,128)(2,1)S(1)} %get-tuple-element.9.one_ref), channel_id=1, source_target_pairs={{0,2},{2,4},{4,6},{6,0},{1,3},{3,5},{5,7},{7,1},{8,10},{10,12},{12... | collective-permute-start | bytes 786440 | tf_op jit(solution)/shard_map/ppermute | solution.py:285
  56.7 9.2 %collective-permute-start.12 = (bf16[32,8192]{1,0:T(8,128)(2,1)S(1)}, bf16[32,8192]{1,0:T(8,128)(2,1)S(1)}, u32[]{:S(2)}, u32[]{:S(2)}) collective-permute-start(bf16[32,8192]{1,0:T(8,128)(2,1)S(1)} %join.2.refs_4_), channel_id=1, source_target_pairs={{0,1},{1,0},{2,3},{3,2},{4,5},{5,4},{6,7},{7,6},{8,9},{9,8},{10,11... | collective-permute-start | bytes 1572872 | tf_op jit(solution)/shard_map/ppermute | solution.py:279
  58.0 8.0 %collective-permute-start.13 = (bf16[32,8192]{1,0:T(8,128)(2,1)S(1)}, bf16[32,8192]{1,0:T(8,128)(2,1)S(1)}, u32[]{:S(2)}, u32[]{:S(2)}) collective-permute-start(bf16[32,8192]{1,0:T(8,128)(2,1)S(1)} %join.3.refs_5_), channel_id=1, source_target_pairs={{0,1},{1,0},{2,3},{3,2},{4,5},{5,4},{6,7},{7,6},{8,9},{9,8},{10,11... | collective-permute-start | bytes 1572872 | tf_op jit(solution)/shard_map/ppermute | solution.py:279
  63.3 4.4 %collective-permute-start.11 = (bf16[32,8192]{1,0:T(8,128)(2,1)S(1)}, bf16[32,8192]{1,0:T(8,128)(2,1)S(1)}, u32[]{:S(2)}, u32[]{:S(2)}) collective-permute-start(bf16[32,8192]{1,0:T(8,128)(2,1)S(1)} %get-tuple-element.11.refs_2_), channel_id=1, source_target_pairs={{0,1},{1,0},{2,3},{3,2},{4,5},{5,4},{6,7},{7,6},{8,9},{9,8},{10,11... | collective-permute-start | bytes 1572872 | tf_op jit(solution)/shard_map/ppermute | solution.py:279

commit v5 on v4

--- a/solution.py
+++ b/solution.py
@@ -218,7 +218,7 @@
     parts, out_ref, sems = refs[: len(steps)], refs[-2], refs[-1]
     copies = []
     for k, (ref, (step, other, half)) in enumerate(zip(parts, steps)):
-        x, core = lax.rem(spot_ref[0] + step, 4), lax.rem(spot_ref[1] + other, 2)
+        x, core = spot_ref[0] ^ step, spot_ref[1] ^ other
         start = pl.multiple_of((x * 2 + core) * ROWS + half * HALF, HALF)
         copies.append(
             pltpu.make_async_copy(ref, out_ref.at[pl.ds(start, ref.shape[0]), :], sems.at[k])
@@ -250,8 +250,8 @@
     )(spot, *[in_vmem(part) for part in parts.values()], *[in_hbm(w) for w in keep])
 
 
-def ring(n, step):
-    return [(i, (i + step) % n) for i in range(n)]
+def pairs(k, n=4):
+    return [(i, i ^ k) for i in range(n)]
 
 
 def shards(local_params, base_params, momentum):
@@ -261,11 +261,10 @@
     received = lax.all_to_all(decoded, near, 0, 0, tiled=True)
     partial = jnp.sum(received.astype(jnp.float32), axis=0).astype(jnp.bfloat16)
 
-    one, two, three = [
-        lax.ppermute(partial, "zh", [(i, i ^ k) for i in range(4)]).astype(jnp.float32)
-        for k in (1, 2, 3)
-    ]
-    total = (partial.astype(jnp.float32) + one) + (two + three)
+    for k in (1, 3):
+        other = lax.ppermute(partial, "zh", pairs(k))
+        total = partial.astype(jnp.float32) + other.astype(jnp.float32)
+        partial = total.astype(jnp.bfloat16)
     average = (total / 32).astype(jnp.bfloat16)
 
     gathered = lax.all_to_all(
@@ -276,13 +275,13 @@
     new_momentum = update_momentum(gathered, momentum)
 
     def swap(part):
-        return lax.ppermute(part, "core", ring(2, 1))
+        return lax.ppermute(part, "core", pairs(1, 2))
 
     spot = jnp.stack([lax.axis_index("x"), lax.axis_index("core")]).astype(jnp.int32)
-    left = [lax.ppermute(half, "x", ring(4, 1)) for half in (first, second)]
-    right = [lax.ppermute(half, "x", ring(4, 3)) for half in (second, first)]
+    left = [lax.ppermute(half, "x", pairs(1)) for half in (first, second)]
+    right = [lax.ppermute(half, "x", pairs(3)) for half in (second, first)]
     left[0], new_momentum = after(left[0], new_momentum)
-    far = [lax.ppermute(left[0], "x", ring(4, 1)), lax.ppermute(right[0], "x", ring(4, 3))]
+    far = [lax.ppermute(left[0], "x", pairs(3)), lax.ppermute(right[0], "x", pairs(1))]
     from_left = join(left[0], left[1])
     from_right = join(right[1], right[0])
     new_base = place(
@@ -292,16 +291,16 @@
             (0, 0, 1): second,
             (0, 1, 0): swap(first),
             (0, 1, 1): swap(second),
-            (3, 0, 0): from_left,
-            (1, 0, 0): from_right,
+            (1, 0, 0): from_left,
+            (3, 0, 0): from_right,
         },
     )
     from_far, new_base = join_after(far[0], far[1], new_base)
     new_base = place(
         spot,
         {
-            (3, 1, 0): swap(from_left),
-            (1, 1, 0): swap(from_right),
+            (1, 1, 0): swap(from_left),
+            (3, 1, 0): swap(from_right),
             (2, 0, 0): from_far,
         },
         new_base,

time: 69.3 us -> 67.7 us (0.977)
  waiting for transfers between devices: 9.32 us -> 5.88 us
  starting transfers between devices: 24.1 us -> 25.1 us
  blocking collectives: 24.7 us -> 25.5 us
    ppermute x14 -> x13, waiting for transfers between devices: 9.32 us -> 5.88 us  [the longest x2 4.67 us: shards(): other = lax.ppermute(partial, 'zh', pairs(k))]
    ppermute x14 -> x13, starting transfers between devices: 24.1 us -> 25.1 us  [the longest x5 11 us: swap(): return lax.ppermute(part, 'core', pairs(1, 2))]
    all_to_all x1, blocking collectives: 9.89 us -> 10.7 us  [shards(): lax.all_to_all(jnp.broadcast_to(average[None], (8,) + average.shape), nea...]
  transfers between devices with their start and end apart: 14 -> 13, of which waited for: 3 -> 3; matrix products, arithmetic and copies ran while one was open for 0% -> 0% of each run, Pallas kernels for 8% -> 9%
where the time goes in v5:
time: 67.7 us; the launch traced here: 67.5 us
  blocking collectives  25.5 us (38%)
  starting transfers between devices  25.1 us (37%)
  Pallas kernels  9.97 us (15%)
  waiting for transfers between devices  5.88 us (9%)
  between operations  0.78 us (1%)
    all_to_all x1, blocking collectives, shards(): received = lax.all_to_all(decoded, near, 0, 0, tiled=True)  14.8 us
    ppermute x5, starting transfers between devices, swap(): return lax.ppermute(part, 'core', pairs(1, 2))  11 us
    all_to_all x1, blocking collectives, shards(): lax.all_to_all(jnp.broadcast_to(average[None], (8,) + average.shape), nea...  10.7 us
    ppermute x2, starting transfers between devices, shards(): other = lax.ppermute(partial, 'zh', pairs(k))  7.06 us
    pallas_call x3, Pallas kernels, place(): pl.pallas_call(functools.partial(place_kernel, steps), out_shape=pltpu.HB...  4.97 us
    ppermute x2, waiting for transfers between devices, shards(): other = lax.ppermute(partial, 'zh', pairs(k))  4.67 us
    pallas_call x1, Pallas kernels, encode(): pl.pallas_call(encode_kernel, out_shape=pltpu.VMEM((2 * PIECES, HALF, WID...  2.51 us
    ppermute x2, starting transfers between devices, shards(): right = [lax.ppermute(half, 'x', pairs(3)) for half in (second, first)]  2.42 us
  transfers between devices with their start and end apart: 13, of which 3 were waited for; matrix products, arithmetic and copies ran while one was open for 0% of the time, Pallas kernels for 9%

profile of v5, /device:TPU:1, one launch (start us, length us, event | category | flops | bytes accessed | tf_op | source)
XLA Modules:
  0.0 67.5 jit_solution(16564457741882846591)
XLA Ops:
  0.6 0.0 copy-start
  0.7 2.5 %encode.1 = bf16[8,16,2048]{2,1,0:T(8,128)(2,1)S(1)} custom-call(bf16[1,32,8192]{2,1,0:T(8,128)(2,1)} %local_hbm.1, bf16[32,8192]{1,0:T(8,128)(2,1)} %base_ref.1), custom_call_target="tpu_custom_call" | custom-call | tf_op jit(solution)/shard_map/encode/pallas_call | solution.py:83
  3.2 14.8 %all_to_all.10 = bf16[8,16,2048]{2,1,0:T(8,128)(2,1)S(1)} all-to-all(bf16[8,16,2048]{2,1,0:T(8,128)(2,1)S(1)} %encode.1), channel_id=1, replica_groups=mesh['zh'=4,'zl'=2,'y'=4,'x'=4,'core'=2] {'zl','y'}, dimensions={0} | all-to-all | bytes 1048576 | tf_op jit(solution)/shard_map/all_to_all | solution.py:261
  18.0 0.1 reduce_sum.12
  18.0 3.1 %collective-permute-start = (bf16[16,2048]{1,0:T(8,128)(2,1)S(1)}, bf16[16,2048]{1,0:T(8,128)(2,1)S(1)}, u32[]{:S(2)}, u32[]{:S(2)}) collective-permute-start(bf16[16,2048]{1,0:T(8,128)(2,1)S(1)} %reduce_sum.12), channel_id=1, source_target_pairs={{0,64},{64,0},{128,192},{192,128},{1,65},{65,1},{129,193},{193,129... | collective-permute-start | bytes 196616 | tf_op jit(solution)/shard_map/ppermute | solution.py:265
  21.1 2.4 %collective-permute-done = bf16[16,2048]{1,0:T(8,128)(2,1)S(1)} collective-permute-done((bf16[16,2048]{1,0:T(8,128)(2,1)S(1)}, bf16[16,2048]{1,0:T(8,128)(2,1)S(1)}, u32[]{:S(2)}, u32[]{:S(2)}) %collective-permute-start) | collective-permute-done | bytes 65568 | tf_op jit(solution)/shard_map/ppermute | solution.py:265
  23.5 4.0 %collective-permute-start.1 = (bf16[16,2048]{1,0:T(8,128)(2,1)S(1)}, bf16[16,2048]{1,0:T(8,128)(2,1)S(1)}, u32[]{:S(2)}, u32[]{:S(2)}) collective-permute-start(bf16[16,2048]{1,0:T(8,128)(2,1)S(1)} %add_convert_fusion), channel_id=1, source_target_pairs={{0,192},{64,128},{128,64},{192,0},{1,193},{65,129},{129,65},{193,1... | collective-permute-start | bytes 196616 | tf_op jit(solution)/shard_map/ppermute | solution.py:265
  27.5 2.3 %collective-permute-done.1 = bf16[16,2048]{1,0:T(8,128)(2,1)S(1)} collective-permute-done((bf16[16,2048]{1,0:T(8,128)(2,1)S(1)}, bf16[16,2048]{1,0:T(8,128)(2,1)S(1)}, u32[]{:S(2)}, u32[]{:S(2)}) %collective-permute-start.1) | collective-permute-done | bytes 65568 | tf_op jit(solution)/shard_map/ppermute | solution.py:265
  29.9 10.7 %all_to_all.11.average_ref = bf16[8,16,2048]{2,1,0:T(8,128)(2,1)S(1)} all-to-all(bf16[8,16,2048]{2,1,0:T(8,128)(2,1)S(1)} %broadcast_in_dim.2), channel_id=1, replica_groups=mesh['zh'=4,'zl'=2,'y'=4,'x'=4,'core'=2] {'zl','y'}, dimensions={0} | all-to-all | bytes 1048576 | tf_op jit(solution)/shard_map/all_to_all | solution.py:270
  40.6 0.3 update_base.1
  40.9 1.3 %collective-permute-start.2 = (bf16[16,8192]{1,0:T(8,128)(2,1)S(1)}, bf16[16,8192]{1,0:T(8,128)(2,1)S(1)}, u32[]{:S(2)}, u32[]{:S(2)}) collective-permute-start(bf16[16,8192]{1,0:T(8,128)(2,1)S(1)} %get-tuple-element.8.refs_0_), channel_id=1, source_target_pairs={{0,2},{2,0},{4,6},{6,4},{1,3},{3,1},{5,7},{7,5},{8,10},{10,8},{12,... | collective-permute-start | bytes 786440 | tf_op jit(solution)/shard_map/ppermute | solution.py:281
  42.2 1.8 %collective-permute-start.4 = (bf16[16,8192]{1,0:T(8,128)(2,1)S(1)}, bf16[16,8192]{1,0:T(8,128)(2,1)S(1)}, u32[]{:S(2)}, u32[]{:S(2)}) collective-permute-start(bf16[16,8192]{1,0:T(8,128)(2,1)S(1)} %get-tuple-element.10.refs_1_), channel_id=1, source_target_pairs={{0,6},{2,4},{4,2},{6,0},{1,7},{3,5},{5,3},{7,1},{8,14},{10,12},{12... | collective-permute-start | bytes 786440 | tf_op jit(solution)/shard_map/ppermute | solution.py:282
  44.0 0.3 collective-permute-start.8
  44.3 0.6 collective-permute-start.9
  44.9 6.0 %collective-permute-start.6 = (bf16[16,8192]{1,0:T(8,128)(2,1)S(1)}, bf16[16,8192]{1,0:T(8,128)(2,1)S(1)}, u32[]{:S(2)}, u32[]{:S(2)}) collective-permute-start(bf16[16,8192]{1,0:T(8,128)(2,1)S(1)} %get-tuple-element.8.refs_0_), channel_id=1, source_target_pairs={{0,1},{1,0},{2,3},{3,2},{4,5},{5,4},{6,7},{7,6},{8,9},{9,8},{10,11... | collective-permute-start | bytes 786440 | tf_op jit(solution)/shard_map/ppermute | solution.py:278
  50.9 2.1 %update_momentum.1.refs_1_ = f32[32,8192]{1,0:T(8,128)} custom-call(bf16[8,16,2048]{2,1,0:T(8,128)(2,1)S(1)} %all_to_all.11.average_ref, f32[32,8192]{1,0:T(8,128)} %momentum_hbm.1), custom_call_target="tpu_custom_call" | custom-call | tf_op jit(solution)/shard_map/update_momentum/pallas_call | solution.py:152
  53.0 0.0 collective-permute-done.2.refs_0_
  53.0 0.1 collective-permute-start.7
  53.2 1.2 %collective-permute-start.5 = (bf16[16,8192]{1,0:T(8,128)(2,1)S(1)}, bf16[16,8192]{1,0:T(8,128)(2,1)S(1)}, u32[]{:S(2)}, u32[]{:S(2)}) collective-permute-start(bf16[16,8192]{1,0:T(8,128)(2,1)S(1)} %collective-permute-done.4.two_ref), channel_id=1, source_target_pairs={{0,2},{2,0},{4,6},{6,4},{1,3},{3,1},{5,7},{7,5},{8,10},{10,8},{12,... | collective-permute-start | bytes 786440 | tf_op jit(solution)/shard_map/ppermute | solution.py:284
  54.3 0.0 collective-permute-done.8.two_ref
  54.3 1.8 %collective-permute-start.3 = (bf16[16,8192]{1,0:T(8,128)(2,1)S(1)}, bf16[16,8192]{1,0:T(8,128)(2,1)S(1)}, u32[]{:S(2)}, u32[]{:S(2)}) collective-permute-start(bf16[16,8192]{1,0:T(8,128)(2,1)S(1)} %get-tuple-element.9.one_ref), channel_id=1, source_target_pairs={{0,6},{2,4},{4,2},{6,0},{1,7},{3,5},{5,3},{7,1},{8,14},{10,12},{12... | collective-permute-start | bytes 786440 | tf_op jit(solution)/shard_map/ppermute | solution.py:284
  56.1 0.1 pad_add_fusion.spot_ref
  56.3 0.0 collective-permute-done.9.one_ref
  56.3 2.0 %collective-permute-start.11 = (bf16[32,8192]{1,0:T(8,128)(2,1)S(1)}, bf16[32,8192]{1,0:T(8,128)(2,1)S(1)}, u32[]{:S(2)}, u32[]{:S(2)}) collective-permute-start(bf16[32,8192]{1,0:T(8,128)(2,1)S(1)} %join.2.refs_4_), channel_id=1, source_target_pairs={{0,1},{1,0},{2,3},{3,2},{4,5},{5,4},{6,7},{7,6},{8,9},{9,8},{10,11... | collective-permute-start | bytes 1572872 | tf_op jit(solution)/shard_map/ppermute | solution.py:278
  58.3 0.0 collective-permute-done.6.refs_2_
  58.3 0.1 collective-permute-start.12
  58.5 1.9 %place.3.refs_0_ = bf16[256,8192]{1,0:T(8,128)(2,1)} custom-call(s32[2]{0:T(128)S(1)} %pad_add_fusion.spot_ref, bf16[16,8192]{1,0:T(8,128)(2,1)S(1)} %get-tuple-element.8.refs_0_, bf16[16,8192]{1,0:T(8,128)(2,1)S(1)} %get-tuple-element.10.refs_1_, bf16[16,8192]{1,0:T(8,128)(2,1)S(1)} %collective-permute-done.6.refs_2_, ...), custom_call_target="tpu_custom_call" | custom-call | bytes 4194304 | tf_op jit(solution)/shard_map/place/pallas_call | solution.py:236
  60.4 0.0 collective-permute-done.5.two_ref
  60.4 1.2 %collective-permute-done.3.one_ref = bf16[16,8192]{1,0:T(8,128)(2,1)S(1)} collective-permute-done((bf16[16,8192]{1,0:T(8,128)(2,1)S(1)}, bf16[16,8192]{1,0:T(8,128)(2,1)S(1)}, u32[]{:S(2)}, u32[]{:S(2)}) %collective-permute-start.3) | collective-permute-done | bytes 262176 | tf_op jit(solution)/shard_map/ppermute | solution.py:284
  61.6 2.8 %collective-permute-start.10 = (bf16[32,8192]{1,0:T(8,128)(2,1)S(1)}, bf16[32,8192]{1,0:T(8,128)(2,1)S(1)}, u32[]{:S(2)}, u32[]{:S(2)}) collective-permute-start(bf16[32,8192]{1,0:T(8,128)(2,1)S(1)} %get-tuple-element.11.refs_2_), channel_id=1, source_target_pairs={{0,1},{1,0},{2,3},{3,2},{4,5},{5,4},{6,7},{7,6},{8,9},{9,8},{10,11... | collective-permute-start | bytes 1572872 | tf_op jit(solution)/shard_map/ppermute | solution.py:278
  64.4 1.7 %place.4.refs_1_ = bf16[256,8192]{1,0:T(8,128)(2,1)} custom-call(s32[2]{0:T(128)S(1)} %pad_add_fusion.spot_ref, bf16[32,8192]{1,0:T(8,128)(2,1)S(1)} %collective-permute-done.11.refs_0_, bf16[32,8192]{1,0:T(8,128)(2,1)S(1)} %collective-permute-done.12.refs_1_, bf16[32,8192]{1,0:T(8,128)(2,1)S(1)} %get-tuple-element.11.refs_2_, ...), custom_call_target="tpu_custom_call", output_to_operand_aliasing={{}: (4, {})} | custom-call | bytes 3145728 | tf_op jit(solution)/shard_map/place/pallas_call | solution.py:236
  66.1 1.4 %place.5 = bf16[256,8192]{1,0:T(8,128)(2,1)} custom-call(s32[2]{0:T(128)S(1)} %pad_add_fusion.spot_ref, bf16[32,8192]{1,0:T(8,128)(2,1)S(1)} %collective-permute-done.10.refs_0_, bf16[256,8192]{1,0:T(8,128)(2,1)} %place.4.refs_1_), custom_call_target="tpu_custom_call", output_to_operand_aliasing={{}: (2, {})} | custom-call | bytes 1048576 | tf_op jit(solution)/shard_map/place/pallas_call | solution.py:236
  (15 shorter events, 0.2 us)
Async XLA Ops:
  0.6 40.0 %copy-start.1 = (bf16[32,8192]{1,0:T(8,128)(2,1)S(1)}, bf16[32,8192]{1,0:T(8,128)(2,1)}, u32[]{:S(2)}) copy-start(bf16[32,8192]{1,0:T(8,128)(2,1)} %base_ref.1) | copy-start | bytes 1572868
  0.6 39.9 %copy-start = (f32[32,8192]{1,0:T(8,128)S(1)}, f32[32,8192]{1,0:T(8,128)}, u32[]{:S(2)}) copy-start(f32[32,8192]{1,0:T(8,128)} %momentum_hbm.1) | copy-start | bytes 3145732
  18.0 5.4 %collective-permute-start = (bf16[16,2048]{1,0:T(8,128)(2,1)S(1)}, bf16[16,2048]{1,0:T(8,128)(2,1)S(1)}, u32[]{:S(2)}, u32[]{:S(2)}) collective-permute-start(bf16[16,2048]{1,0:T(8,128)(2,1)S(1)} %reduce_sum.12), channel_id=1, source_target_pairs={{0,64},{64,0},{128,192},{192,128},{1,65},{65,1},{129,193},{193,129... | collective-permute-start | bytes 196616 | tf_op jit(solution)/shard_map/ppermute | solution.py:265
  23.5 6.3 %collective-permute-start.1 = (bf16[16,2048]{1,0:T(8,128)(2,1)S(1)}, bf16[16,2048]{1,0:T(8,128)(2,1)S(1)}, u32[]{:S(2)}, u32[]{:S(2)}) collective-permute-start(bf16[16,2048]{1,0:T(8,128)(2,1)S(1)} %add_convert_fusion), channel_id=1, source_target_pairs={{0,192},{64,128},{128,64},{192,0},{1,193},{65,129},{129,65},{193,1... | collective-permute-start | bytes 196616 | tf_op jit(solution)/shard_map/ppermute | solution.py:265
  40.9 12.2 %collective-permute-start.2 = (bf16[16,8192]{1,0:T(8,128)(2,1)S(1)}, bf16[16,8192]{1,0:T(8,128)(2,1)S(1)}, u32[]{:S(2)}, u32[]{:S(2)}) collective-permute-start(bf16[16,8192]{1,0:T(8,128)(2,1)S(1)} %get-tuple-element.8.refs_0_), channel_id=1, source_target_pairs={{0,2},{2,0},{4,6},{6,4},{1,3},{3,1},{5,7},{7,5},{8,10},{10,8},{12,... | collective-permute-start | bytes 786440 | tf_op jit(solution)/shard_map/ppermute | solution.py:281
  42.2 11.0 %collective-permute-start.4 = (bf16[16,8192]{1,0:T(8,128)(2,1)S(1)}, bf16[16,8192]{1,0:T(8,128)(2,1)S(1)}, u32[]{:S(2)}, u32[]{:S(2)}) collective-permute-start(bf16[16,8192]{1,0:T(8,128)(2,1)S(1)} %get-tuple-element.10.refs_1_), channel_id=1, source_target_pairs={{0,6},{2,4},{4,2},{6,0},{1,7},{3,5},{5,3},{7,1},{8,14},{10,12},{12... | collective-permute-start | bytes 786440 | tf_op jit(solution)/shard_map/ppermute | solution.py:282
  44.0 10.3 %collective-permute-start.8 = (bf16[16,8192]{1,0:T(8,128)(2,1)S(1)}, bf16[16,8192]{1,0:T(8,128)(2,1)S(1)}, u32[]{:S(2)}, u32[]{:S(2)}) collective-permute-start(bf16[16,8192]{1,0:T(8,128)(2,1)S(1)} %get-tuple-element.10.refs_1_), channel_id=1, source_target_pairs={{0,2},{2,0},{4,6},{6,4},{1,3},{3,1},{5,7},{7,5},{8,10},{10,8},{12,... | collective-permute-start | bytes 786440 | tf_op jit(solution)/shard_map/ppermute | solution.py:281
  44.3 11.9 %collective-permute-start.9 = (bf16[16,8192]{1,0:T(8,128)(2,1)S(1)}, bf16[16,8192]{1,0:T(8,128)(2,1)S(1)}, u32[]{:S(2)}, u32[]{:S(2)}) collective-permute-start(bf16[16,8192]{1,0:T(8,128)(2,1)S(1)} %get-tuple-element.8.refs_0_), channel_id=1, source_target_pairs={{0,6},{2,4},{4,2},{6,0},{1,7},{3,5},{5,3},{7,1},{8,14},{10,12},{12... | collective-permute-start | bytes 786440 | tf_op jit(solution)/shard_map/ppermute | solution.py:282
  44.9 13.4 %collective-permute-start.6 = (bf16[16,8192]{1,0:T(8,128)(2,1)S(1)}, bf16[16,8192]{1,0:T(8,128)(2,1)S(1)}, u32[]{:S(2)}, u32[]{:S(2)}) collective-permute-start(bf16[16,8192]{1,0:T(8,128)(2,1)S(1)} %get-tuple-element.8.refs_0_), channel_id=1, source_target_pairs={{0,1},{1,0},{2,3},{3,2},{4,5},{5,4},{6,7},{7,6},{8,9},{9,8},{10,11... | collective-permute-start | bytes 786440 | tf_op jit(solution)/shard_map/ppermute | solution.py:278
  53.0 5.4 %collective-permute-start.7 = (bf16[16,8192]{1,0:T(8,128)(2,1)S(1)}, bf16[16,8192]{1,0:T(8,128)(2,1)S(1)}, u32[]{:S(2)}, u32[]{:S(2)}) collective-permute-start(bf16[16,8192]{1,0:T(8,128)(2,1)S(1)} %get-tuple-element.10.refs_1_), channel_id=1, source_target_pairs={{0,1},{1,0},{2,3},{3,2},{4,5},{5,4},{6,7},{7,6},{8,9},{9,8},{10,11... | collective-permute-start | bytes 786440 | tf_op jit(solution)/shard_map/ppermute | solution.py:278
  53.2 7.2 %collective-permute-start.5 = (bf16[16,8192]{1,0:T(8,128)(2,1)S(1)}, bf16[16,8192]{1,0:T(8,128)(2,1)S(1)}, u32[]{:S(2)}, u32[]{:S(2)}) collective-permute-start(bf16[16,8192]{1,0:T(8,128)(2,1)S(1)} %collective-permute-done.4.two_ref), channel_id=1, source_target_pairs={{0,2},{2,0},{4,6},{6,4},{1,3},{3,1},{5,7},{7,5},{8,10},{10,8},{12,... | collective-permute-start | bytes 786440 | tf_op jit(solution)/shard_map/ppermute | solution.py:284
  54.3 7.2 %collective-permute-start.3 = (bf16[16,8192]{1,0:T(8,128)(2,1)S(1)}, bf16[16,8192]{1,0:T(8,128)(2,1)S(1)}, u32[]{:S(2)}, u32[]{:S(2)}) collective-permute-start(bf16[16,8192]{1,0:T(8,128)(2,1)S(1)} %get-tuple-element.9.one_ref), channel_id=1, source_target_pairs={{0,6},{2,4},{4,2},{6,0},{1,7},{3,5},{5,3},{7,1},{8,14},{10,12},{12... | collective-permute-start | bytes 786440 | tf_op jit(solution)/shard_map/ppermute | solution.py:284
  56.3 8.1 %collective-permute-start.11 = (bf16[32,8192]{1,0:T(8,128)(2,1)S(1)}, bf16[32,8192]{1,0:T(8,128)(2,1)S(1)}, u32[]{:S(2)}, u32[]{:S(2)}) collective-permute-start(bf16[32,8192]{1,0:T(8,128)(2,1)S(1)} %join.2.refs_4_), channel_id=1, source_target_pairs={{0,1},{1,0},{2,3},{3,2},{4,5},{5,4},{6,7},{7,6},{8,9},{9,8},{10,11... | collective-permute-start | bytes 1572872 | tf_op jit(solution)/shard_map/ppermute | solution.py:278
  58.3 6.0 %collective-permute-start.12 = (bf16[32,8192]{1,0:T(8,128)(2,1)S(1)}, bf16[32,8192]{1,0:T(8,128)(2,1)S(1)}, u32[]{:S(2)}, u32[]{:S(2)}) collective-permute-start(bf16[32,8192]{1,0:T(8,128)(2,1)S(1)} %join.3.refs_5_), channel_id=1, source_target_pairs={{0,1},{1,0},{2,3},{3,2},{4,5},{5,4},{6,7},{7,6},{8,9},{9,8},{10,11... | collective-permute-start | bytes 1572872 | tf_op jit(solution)/shard_map/ppermute | solution.py:278
  61.6 4.5 %collective-permute-start.10 = (bf16[32,8192]{1,0:T(8,128)(2,1)S(1)}, bf16[32,8192]{1,0:T(8,128)(2,1)S(1)}, u32[]{:S(2)}, u32[]{:S(2)}) collective-permute-start(bf16[32,8192]{1,0:T(8,128)(2,1)S(1)} %get-tuple-element.11.refs_2_), channel_id=1, source_target_pairs={{0,1},{1,0},{2,3},{3,2},{4,5},{5,4},{6,7},{7,6},{8,9},{9,8},{10,11... | collective-permute-start | bytes 1572872 | tf_op jit(solution)/shard_map/ppermute | solution.py:278

commit v6 on v5

--- a/solution.py
+++ b/solution.py
@@ -43,7 +43,7 @@
             copy.start()
     block = lax.broadcasted_iota(jnp.int32, (LANES, LANES), 0) // BLOCK
     block_t = lax.broadcasted_iota(jnp.int32, (LANES, LANES), 1) // BLOCK
-    same_block = jnp.where(block == block_t, 1.0 / BLOCK, 0.0).astype(jnp.float32)
+    same_block = jnp.where(block == block_t, 1.0 / BLOCK, 0.0).astype(jnp.bfloat16)
     for k in range(2 * PIECES):
         half, piece = k // PIECES, k % PIECES
         if piece == 0:
@@ -56,12 +56,11 @@
         tall = jnp.concatenate(
             [grad[:, i * LANES : (i + 1) * LANES] for i in range(WIDE // LANES)], axis=0
         )
-        mean_square = jnp.dot(
-            tall * tall,
-            same_block,
-            precision=lax.Precision.HIGHEST,
-            preferred_element_type=jnp.float32,
-        )
+        rest, mean_square = tall * tall, 0.0
+        for _ in range(3):
+            part = rest.astype(jnp.bfloat16)
+            rest = rest - part.astype(jnp.float32)
+            mean_square += jnp.dot(part, same_block, preferred_element_type=jnp.float32)
         floored = jnp.maximum(mean_square, floor_value * floor_value)
         scale = (floored * lax.rsqrt(floored) * (1.0 / spread_ratio)).astype(jnp.bfloat16)
         limit = code_peak * scale.astype(jnp.float32)
@@ -127,22 +126,23 @@
 
 def momentum_kernel(average_ref, momentum_hbm, new_hbm, momentum_ref, new_ref, sems):
     reads, writes = [], []
-    for half in range(2):
-        rows = pl.ds(half * HALF, HALF)
+    for part in range(4):
+        rows = pl.ds(part * 8, 8)
         reads.append(
-            pltpu.make_async_copy(momentum_hbm.at[rows, :], momentum_ref.at[half], sems.at[0, half])
-        )
-        writes.append(pltpu.make_async_copy(new_ref.at[half], new_hbm.at[rows, :], sems.at[1, half]))
+            pltpu.make_async_copy(momentum_hbm.at[rows, :], momentum_ref.at[part], sems.at[0, part])
+        )
+        writes.append(pltpu.make_async_copy(new_ref.at[part], new_hbm.at[rows, :], sems.at[1, part]))
     for copy in reads:
         copy.start()
-    for half in range(2):
-        reads[half].wait()
+    for part in range(4):
+        reads[part].wait()
         for piece in range(PIECES):
             cols = pl.ds(piece * WIDE, WIDE)
-            new_ref[half, :, cols] = step_momentum(
-                average_ref[half * PIECES + piece].astype(jnp.float32), momentum_ref[half, :, cols]
+            average = average_ref[part // 2 * PIECES + piece].astype(jnp.float32)
+            new_ref[part, :, cols] = step_momentum(
+                average[part % 2 * 8 : part % 2 * 8 + 8], momentum_ref[part, :, cols]
             )
-        writes[half].start()
+        writes[part].start()
     for copy in writes:
         copy.wait()
 
@@ -155,9 +155,9 @@
         in_specs=[pl.BlockSpec(memory_space=pltpu.VMEM), hbm],
         out_specs=hbm,
         scratch_shapes=[
-            pltpu.VMEM((2, HALF, COLS), jnp.float32),
-            pltpu.VMEM((2, HALF, COLS), jnp.float32),
-            pltpu.SemaphoreType.DMA((2, 2)),
+            pltpu.VMEM((4, 8, COLS), jnp.float32),
+            pltpu.VMEM((4, 8, COLS), jnp.float32),
+            pltpu.SemaphoreType.DMA((2, 4)),
         ],
         compiler_params=SMALL,
         name="update_momentum",
@@ -214,11 +214,12 @@
     )(in_vmem(one), in_vmem(two), *[in_hbm(array) for array in ready])
 
 
-def place_kernel(steps, spot_ref, *refs):
+def place_kernel(steps, *refs):
     parts, out_ref, sems = refs[: len(steps)], refs[-2], refs[-1]
+    own_x, own_core = lax.axis_index("x"), lax.axis_index("core")
     copies = []
     for k, (ref, (step, other, half)) in enumerate(zip(parts, steps)):
-        x, core = spot_ref[0] ^ step, spot_ref[1] ^ other
+        x, core = own_x ^ step, own_core ^ other
         start = pl.multiple_of((x * 2 + core) * ROWS + half * HALF, HALF)
         copies.append(
             pltpu.make_async_copy(ref, out_ref.at[pl.ds(start, ref.shape[0]), :], sems.at[k])
@@ -229,25 +230,23 @@
         copy.wait()
 
 
-def place(spot, parts, whole=None):
+def place(parts, whole=None):
     steps, count = tuple(parts), len(parts)
     keep = [] if whole is None else [whole]
     hbm = pl.BlockSpec(memory_space=pltpu.HBM)
     return pl.pallas_call(
         functools.partial(place_kernel, steps),
         out_shape=pltpu.HBM((8 * ROWS, COLS), jnp.bfloat16),
-        in_specs=[pl.BlockSpec(memory_space=pltpu.SMEM)]
-        + [pl.BlockSpec(memory_space=pltpu.VMEM)] * count
-        + [hbm] * len(keep),
+        in_specs=[pl.BlockSpec(memory_space=pltpu.VMEM)] * count + [hbm] * len(keep),
         out_specs=hbm,
         scratch_shapes=[pltpu.SemaphoreType.DMA((count,))],
-        input_output_aliases={count + 1: 0} if keep else {},
+        input_output_aliases={count: 0} if keep else {},
         compiler_params=TINY,
         cost_estimate=pl.CostEstimate(
             flops=0, transcendentals=0, bytes_accessed=sum(part.size for part in parts.values()) * 4
         ),
         name="place",
-    )(spot, *[in_vmem(part) for part in parts.values()], *[in_hbm(w) for w in keep])
+    )(*[in_vmem(part) for part in parts.values()], *[in_hbm(w) for w in keep])
 
 
 def pairs(k, n=4):
@@ -277,7 +276,6 @@
     def swap(part):
         return lax.ppermute(part, "core", pairs(1, 2))
 
-    spot = jnp.stack([lax.axis_index("x"), lax.axis_index("core")]).astype(jnp.int32)
     left = [lax.ppermute(half, "x", pairs(1)) for half in (first, second)]
     right = [lax.ppermute(half, "x", pairs(3)) for half in (second, first)]
     left[0], new_momentum = after(left[0], new_momentum)
@@ -285,7 +283,6 @@
     from_left = join(left[0], left[1])
     from_right = join(right[1], right[0])
     new_base = place(
-        spot,
         {
             (0, 0, 0): first,
             (0, 0, 1): second,
@@ -297,7 +294,6 @@
     )
     from_far, new_base = join_after(far[0], far[1], new_base)
     new_base = place(
-        spot,
         {
             (1, 1, 0): swap(from_left),
             (3, 1, 0): swap(from_right),
@@ -305,7 +301,7 @@
         },
         new_base,
     )
-    new_base = place(spot, {(2, 1, 0): swap(from_far)}, new_base)
+    new_base = place({(2, 1, 0): swap(from_far)}, new_base)
     return (new_base, new_momentum)
 
 

time: 67.7 us -> 66.4 us (0.981)
  Pallas kernels: 9.97 us -> 7.8 us
  waiting for transfers between devices: 5.88 us -> 6.67 us
    pallas_call x3, Pallas kernels: 4.97 us -> 3.34 us  [place(): pl.pallas_call(functools.partial(place_kernel, steps), out_shape=pltpu.HB...]
  transfers between devices with their start and end apart: 13 -> 13, of which waited for: 3 -> 4; matrix products, arithmetic and copies ran while one was open for 0% -> 0% of each run, Pallas kernels for 9% -> 7%
where the time goes in v6:
time: 66.4 us; the launch traced here: 66.2 us
  blocking collectives  25.5 us (38%)
  starting transfers between devices  25.3 us (38%)
  Pallas kernels  7.8 us (12%)
  waiting for transfers between devices  6.67 us (10%)
  between operations  0.77 us (1%)
    all_to_all x1, blocking collectives, shards(): received = lax.all_to_all(decoded, near, 0, 0, tiled=True)  14.8 us
    ppermute x5, starting transfers between devices, swap(): return lax.ppermute(part, 'core', pairs(1, 2))  11.2 us
    all_to_all x1, blocking collectives, shards(): lax.all_to_all(jnp.broadcast_to(average[None], (8,) + average.shape), nea...  10.7 us
    ppermute x2, starting transfers between devices, shards(): other = lax.ppermute(partial, 'zh', pairs(k))  7.05 us
    ppermute x2, waiting for transfers between devices, shards(): other = lax.ppermute(partial, 'zh', pairs(k))  4.67 us
    pallas_call x3, Pallas kernels, place(): pl.pallas_call(functools.partial(place_kernel, steps), out_shape=pltpu.HB...  3.34 us
    ppermute x2, starting transfers between devices, shards(): right = [lax.ppermute(half, 'x', pairs(3)) for half in (second, first)]  2.43 us
    pallas_call x1, Pallas kernels, encode(): pl.pallas_call(encode_kernel, out_shape=pltpu.VMEM((2 * PIECES, HALF, WID...  2.06 us
  transfers between devices with their start and end apart: 13, of which 4 were waited for; matrix products, arithmetic and copies ran while one was open for 0% of the time, Pallas kernels for 7%

profile of v6, /device:TPU:1, one launch (start us, length us, event | category | flops | bytes accessed | tf_op | source)
XLA Modules:
  0.0 66.2 jit_solution(16098346395725381719)
XLA Ops:
  0.6 0.0 copy-start
  0.7 2.1 %encode.1 = bf16[8,16,2048]{2,1,0:T(8,128)(2,1)S(1)} custom-call(bf16[1,32,8192]{2,1,0:T(8,128)(2,1)} %local_hbm.1, bf16[32,8192]{1,0:T(8,128)(2,1)} %base_ref.1), custom_call_target="tpu_custom_call" | custom-call | tf_op jit(solution)/shard_map/encode/pallas_call | solution.py:82
  2.7 14.8 %all_to_all.10 = bf16[8,16,2048]{2,1,0:T(8,128)(2,1)S(1)} all-to-all(bf16[8,16,2048]{2,1,0:T(8,128)(2,1)S(1)} %encode.1), channel_id=1, replica_groups=mesh['zh'=4,'zl'=2,'y'=4,'x'=4,'core'=2] {'zl','y'}, dimensions={0} | all-to-all | bytes 1048576 | tf_op jit(solution)/shard_map/all_to_all | solution.py:260
  17.5 0.1 reduce_sum.12
  17.6 3.1 %collective-permute-start = (bf16[16,2048]{1,0:T(8,128)(2,1)S(1)}, bf16[16,2048]{1,0:T(8,128)(2,1)S(1)}, u32[]{:S(2)}, u32[]{:S(2)}) collective-permute-start(bf16[16,2048]{1,0:T(8,128)(2,1)S(1)} %reduce_sum.12), channel_id=1, source_target_pairs={{0,64},{64,0},{128,192},{192,128},{1,65},{65,1},{129,193},{193,129... | collective-permute-start | bytes 196616 | tf_op jit(solution)/shard_map/ppermute | solution.py:264
  20.7 2.4 %collective-permute-done = bf16[16,2048]{1,0:T(8,128)(2,1)S(1)} collective-permute-done((bf16[16,2048]{1,0:T(8,128)(2,1)S(1)}, bf16[16,2048]{1,0:T(8,128)(2,1)S(1)}, u32[]{:S(2)}, u32[]{:S(2)}) %collective-permute-start) | collective-permute-done | bytes 65568 | tf_op jit(solution)/shard_map/ppermute | solution.py:264
  23.1 4.0 %collective-permute-start.1 = (bf16[16,2048]{1,0:T(8,128)(2,1)S(1)}, bf16[16,2048]{1,0:T(8,128)(2,1)S(1)}, u32[]{:S(2)}, u32[]{:S(2)}) collective-permute-start(bf16[16,2048]{1,0:T(8,128)(2,1)S(1)} %add_convert_fusion), channel_id=1, source_target_pairs={{0,192},{64,128},{128,64},{192,0},{1,193},{65,129},{129,65},{193,1... | collective-permute-start | bytes 196616 | tf_op jit(solution)/shard_map/ppermute | solution.py:264
  27.0 2.3 %collective-permute-done.1 = bf16[16,2048]{1,0:T(8,128)(2,1)S(1)} collective-permute-done((bf16[16,2048]{1,0:T(8,128)(2,1)S(1)}, bf16[16,2048]{1,0:T(8,128)(2,1)S(1)}, u32[]{:S(2)}, u32[]{:S(2)}) %collective-permute-start.1) | collective-permute-done | bytes 65568 | tf_op jit(solution)/shard_map/ppermute | solution.py:264
  29.4 10.7 %all_to_all.11.average_ref = bf16[8,16,2048]{2,1,0:T(8,128)(2,1)S(1)} all-to-all(bf16[8,16,2048]{2,1,0:T(8,128)(2,1)S(1)} %broadcast_in_dim.2), channel_id=1, replica_groups=mesh['zh'=4,'zl'=2,'y'=4,'x'=4,'core'=2] {'zl','y'}, dimensions={0} | all-to-all | bytes 1048576 | tf_op jit(solution)/shard_map/all_to_all | solution.py:269
  40.1 0.3 update_base.1
  40.4 1.3 %collective-permute-start.2 = (bf16[16,8192]{1,0:T(8,128)(2,1)S(1)}, bf16[16,8192]{1,0:T(8,128)(2,1)S(1)}, u32[]{:S(2)}, u32[]{:S(2)}) collective-permute-start(bf16[16,8192]{1,0:T(8,128)(2,1)S(1)} %get-tuple-element.8.refs_0_), channel_id=1, source_target_pairs={{0,2},{2,0},{4,6},{6,4},{1,3},{3,1},{5,7},{7,5},{8,10},{10,8},{12,... | collective-permute-start | bytes 786440 | tf_op jit(solution)/shard_map/ppermute | solution.py:279
  41.7 1.8 %collective-permute-start.4 = (bf16[16,8192]{1,0:T(8,128)(2,1)S(1)}, bf16[16,8192]{1,0:T(8,128)(2,1)S(1)}, u32[]{:S(2)}, u32[]{:S(2)}) collective-permute-start(bf16[16,8192]{1,0:T(8,128)(2,1)S(1)} %get-tuple-element.10.refs_1_), channel_id=1, source_target_pairs={{0,6},{2,4},{4,2},{6,0},{1,7},{3,5},{5,3},{7,1},{8,14},{10,12},{12... | collective-permute-start | bytes 786440 | tf_op jit(solution)/shard_map/ppermute | solution.py:280
  43.5 0.3 collective-permute-start.8
  43.9 0.6 collective-permute-start.9
  44.5 6.0 %collective-permute-start.6 = (bf16[16,8192]{1,0:T(8,128)(2,1)S(1)}, bf16[16,8192]{1,0:T(8,128)(2,1)S(1)}, u32[]{:S(2)}, u32[]{:S(2)}) collective-permute-start(bf16[16,8192]{1,0:T(8,128)(2,1)S(1)} %get-tuple-element.8.refs_0_), channel_id=1, source_target_pairs={{0,1},{1,0},{2,3},{3,2},{4,5},{5,4},{6,7},{7,6},{8,9},{9,8},{10,11... | collective-permute-start | bytes 786440 | tf_op jit(solution)/shard_map/ppermute | solution.py:277
  50.5 2.0 %update_momentum.1.refs_1_ = f32[32,8192]{1,0:T(8,128)} custom-call(bf16[8,16,2048]{2,1,0:T(8,128)(2,1)S(1)} %all_to_all.11.average_ref, f32[32,8192]{1,0:T(8,128)} %momentum_hbm.1), custom_call_target="tpu_custom_call" | custom-call | tf_op jit(solution)/shard_map/update_momentum/pallas_call | solution.py:152
  52.5 0.1 collective-permute-start.7
  52.6 0.0 collective-permute-done.4.two_ref
  52.6 1.2 %collective-permute-start.5 = (bf16[16,8192]{1,0:T(8,128)(2,1)S(1)}, bf16[16,8192]{1,0:T(8,128)(2,1)S(1)}, u32[]{:S(2)}, u32[]{:S(2)}) collective-permute-start(bf16[16,8192]{1,0:T(8,128)(2,1)S(1)} %collective-permute-done.4.two_ref), channel_id=1, source_target_pairs={{0,2},{2,0},{4,6},{6,4},{1,3},{3,1},{5,7},{7,5},{8,10},{10,8},{12,... | collective-permute-start | bytes 786440 | tf_op jit(solution)/shard_map/ppermute | solution.py:282
  53.8 0.0 collective-permute-done.8.two_ref
  53.8 1.8 %collective-permute-start.3 = (bf16[16,8192]{1,0:T(8,128)(2,1)S(1)}, bf16[16,8192]{1,0:T(8,128)(2,1)S(1)}, u32[]{:S(2)}, u32[]{:S(2)}) collective-permute-start(bf16[16,8192]{1,0:T(8,128)(2,1)S(1)} %get-tuple-element.9.one_ref), channel_id=1, source_target_pairs={{0,6},{2,4},{4,2},{6,0},{1,7},{3,5},{5,3},{7,1},{8,14},{10,12},{12... | collective-permute-start | bytes 786440 | tf_op jit(solution)/shard_map/ppermute | solution.py:282
  55.7 2.1 %collective-permute-start.11 = (bf16[32,8192]{1,0:T(8,128)(2,1)S(1)}, bf16[32,8192]{1,0:T(8,128)(2,1)S(1)}, u32[]{:S(2)}, u32[]{:S(2)}) collective-permute-start(bf16[32,8192]{1,0:T(8,128)(2,1)S(1)} %join.2.refs_4_), channel_id=1, source_target_pairs={{0,1},{1,0},{2,3},{3,2},{4,5},{5,4},{6,7},{7,6},{8,9},{9,8},{10,11... | collective-permute-start | bytes 1572872 | tf_op jit(solution)/shard_map/ppermute | solution.py:277
  57.8 0.1 collective-permute-start.12
  57.9 0.0 collective-permute-done.7.refs_3_
  57.9 1.4 %place.3.refs_0_ = bf16[256,8192]{1,0:T(8,128)(2,1)} custom-call(bf16[16,8192]{1,0:T(8,128)(2,1)S(1)} %get-tuple-element.8.refs_0_, bf16[16,8192]{1,0:T(8,128)(2,1)S(1)} %get-tuple-element.10.refs_1_, bf16[16,8192]{1,0:T(8,128)(2,1)S(1)} %collective-permute-done.6.refs_2_, bf16[16,8192]{1,0:T(8,128)(2,1)S(1)} %collective-permute-done.7.refs_3_, ...), custom_call_target="tpu_custom_call" | custom-call | bytes 4194304 | tf_op jit(solution)/shard_map/place/pallas_call | solution.py:237
  59.3 1.6 %collective-permute-done.3.one_ref = bf16[16,8192]{1,0:T(8,128)(2,1)S(1)} collective-permute-done((bf16[16,8192]{1,0:T(8,128)(2,1)S(1)}, bf16[16,8192]{1,0:T(8,128)(2,1)S(1)}, u32[]{:S(2)}, u32[]{:S(2)}) %collective-permute-start.3) | collective-permute-done | bytes 262176 | tf_op jit(solution)/shard_map/ppermute | solution.py:282
  61.0 2.9 %collective-permute-start.10 = (bf16[32,8192]{1,0:T(8,128)(2,1)S(1)}, bf16[32,8192]{1,0:T(8,128)(2,1)S(1)}, u32[]{:S(2)}, u32[]{:S(2)}) collective-permute-start(bf16[32,8192]{1,0:T(8,128)(2,1)S(1)} %get-tuple-element.11.refs_2_), channel_id=1, source_target_pairs={{0,1},{1,0},{2,3},{3,2},{4,5},{5,4},{6,7},{7,6},{8,9},{9,8},{10,11... | collective-permute-start | bytes 1572872 | tf_op jit(solution)/shard_map/ppermute | solution.py:277
  63.8 0.0 collective-permute-done.11.refs_0_
  63.9 0.0 collective-permute-done.12.refs_1_
  63.9 1.2 %place.4.refs_1_ = bf16[256,8192]{1,0:T(8,128)(2,1)} custom-call(bf16[32,8192]{1,0:T(8,128)(2,1)S(1)} %collective-permute-done.11.refs_0_, bf16[32,8192]{1,0:T(8,128)(2,1)S(1)} %collective-permute-done.12.refs_1_, bf16[32,8192]{1,0:T(8,128)(2,1)S(1)} %get-tuple-element.11.refs_2_, ...), custom_call_target="tpu_custom_call", output_to_operand_aliasing={{}: (3, {})} | custom-call | bytes 3145728 | tf_op jit(solution)/shard_map/place/pallas_call | solution.py:237
  65.0 0.4 collective-permute-done.10.refs_0_
  65.4 0.8 %place.5 = bf16[256,8192]{1,0:T(8,128)(2,1)} custom-call(bf16[32,8192]{1,0:T(8,128)(2,1)S(1)} %collective-permute-done.10.refs_0_, bf16[256,8192]{1,0:T(8,128)(2,1)} %place.4.refs_1_), custom_call_target="tpu_custom_call", output_to_operand_aliasing={{}: (1, {})} | custom-call | bytes 1048576 | tf_op jit(solution)/shard_map/place/pallas_call | solution.py:237
  (14 shorter events, 0.2 us)
Async XLA Ops:
  0.6 39.5 %copy-start.1 = (bf16[32,8192]{1,0:T(8,128)(2,1)S(1)}, bf16[32,8192]{1,0:T(8,128)(2,1)}, u32[]{:S(2)}) copy-start(bf16[32,8192]{1,0:T(8,128)(2,1)} %base_ref.1) | copy-start | bytes 1572868
  0.6 39.5 %copy-start = (f32[32,8192]{1,0:T(8,128)S(1)}, f32[32,8192]{1,0:T(8,128)}, u32[]{:S(2)}) copy-start(f32[32,8192]{1,0:T(8,128)} %momentum_hbm.1) | copy-start | bytes 3145732
  17.6 5.4 %collective-permute-start = (bf16[16,2048]{1,0:T(8,128)(2,1)S(1)}, bf16[16,2048]{1,0:T(8,128)(2,1)S(1)}, u32[]{:S(2)}, u32[]{:S(2)}) collective-permute-start(bf16[16,2048]{1,0:T(8,128)(2,1)S(1)} %reduce_sum.12), channel_id=1, source_target_pairs={{0,64},{64,0},{128,192},{192,128},{1,65},{65,1},{129,193},{193,129... | collective-permute-start | bytes 196616 | tf_op jit(solution)/shard_map/ppermute | solution.py:264
  23.1 6.3 %collective-permute-start.1 = (bf16[16,2048]{1,0:T(8,128)(2,1)S(1)}, bf16[16,2048]{1,0:T(8,128)(2,1)S(1)}, u32[]{:S(2)}, u32[]{:S(2)}) collective-permute-start(bf16[16,2048]{1,0:T(8,128)(2,1)S(1)} %add_convert_fusion), channel_id=1, source_target_pairs={{0,192},{64,128},{128,64},{192,0},{1,193},{65,129},{129,65},{193,1... | collective-permute-start | bytes 196616 | tf_op jit(solution)/shard_map/ppermute | solution.py:264
  40.4 12.1 %collective-permute-start.2 = (bf16[16,8192]{1,0:T(8,128)(2,1)S(1)}, bf16[16,8192]{1,0:T(8,128)(2,1)S(1)}, u32[]{:S(2)}, u32[]{:S(2)}) collective-permute-start(bf16[16,8192]{1,0:T(8,128)(2,1)S(1)} %get-tuple-element.8.refs_0_), channel_id=1, source_target_pairs={{0,2},{2,0},{4,6},{6,4},{1,3},{3,1},{5,7},{7,5},{8,10},{10,8},{12,... | collective-permute-start | bytes 786440 | tf_op jit(solution)/shard_map/ppermute | solution.py:279
  41.7 10.9 %collective-permute-start.4 = (bf16[16,8192]{1,0:T(8,128)(2,1)S(1)}, bf16[16,8192]{1,0:T(8,128)(2,1)S(1)}, u32[]{:S(2)}, u32[]{:S(2)}) collective-permute-start(bf16[16,8192]{1,0:T(8,128)(2,1)S(1)} %get-tuple-element.10.refs_1_), channel_id=1, source_target_pairs={{0,6},{2,4},{4,2},{6,0},{1,7},{3,5},{5,3},{7,1},{8,14},{10,12},{12... | collective-permute-start | bytes 786440 | tf_op jit(solution)/shard_map/ppermute | solution.py:280
  43.5 10.2 %collective-permute-start.8 = (bf16[16,8192]{1,0:T(8,128)(2,1)S(1)}, bf16[16,8192]{1,0:T(8,128)(2,1)S(1)}, u32[]{:S(2)}, u32[]{:S(2)}) collective-permute-start(bf16[16,8192]{1,0:T(8,128)(2,1)S(1)} %get-tuple-element.10.refs_1_), channel_id=1, source_target_pairs={{0,2},{2,0},{4,6},{6,4},{1,3},{3,1},{5,7},{7,5},{8,10},{10,8},{12,... | collective-permute-start | bytes 786440 | tf_op jit(solution)/shard_map/ppermute | solution.py:279
  43.9 11.8 %collective-permute-start.9 = (bf16[16,8192]{1,0:T(8,128)(2,1)S(1)}, bf16[16,8192]{1,0:T(8,128)(2,1)S(1)}, u32[]{:S(2)}, u32[]{:S(2)}) collective-permute-start(bf16[16,8192]{1,0:T(8,128)(2,1)S(1)} %get-tuple-element.8.refs_0_), channel_id=1, source_target_pairs={{0,6},{2,4},{4,2},{6,0},{1,7},{3,5},{5,3},{7,1},{8,14},{10,12},{12... | collective-permute-start | bytes 786440 | tf_op jit(solution)/shard_map/ppermute | solution.py:280
  44.5 13.3 %collective-permute-start.6 = (bf16[16,8192]{1,0:T(8,128)(2,1)S(1)}, bf16[16,8192]{1,0:T(8,128)(2,1)S(1)}, u32[]{:S(2)}, u32[]{:S(2)}) collective-permute-start(bf16[16,8192]{1,0:T(8,128)(2,1)S(1)} %get-tuple-element.8.refs_0_), channel_id=1, source_target_pairs={{0,1},{1,0},{2,3},{3,2},{4,5},{5,4},{6,7},{7,6},{8,9},{9,8},{10,11... | collective-permute-start | bytes 786440 | tf_op jit(solution)/shard_map/ppermute | solution.py:277
  52.5 5.4 %collective-permute-start.7 = (bf16[16,8192]{1,0:T(8,128)(2,1)S(1)}, bf16[16,8192]{1,0:T(8,128)(2,1)S(1)}, u32[]{:S(2)}, u32[]{:S(2)}) collective-permute-start(bf16[16,8192]{1,0:T(8,128)(2,1)S(1)} %get-tuple-element.10.refs_1_), channel_id=1, source_target_pairs={{0,1},{1,0},{2,3},{3,2},{4,5},{5,4},{6,7},{7,6},{8,9},{9,8},{10,11... | collective-permute-start | bytes 786440 | tf_op jit(solution)/shard_map/ppermute | solution.py:277
  52.6 6.7 %collective-permute-start.5 = (bf16[16,8192]{1,0:T(8,128)(2,1)S(1)}, bf16[16,8192]{1,0:T(8,128)(2,1)S(1)}, u32[]{:S(2)}, u32[]{:S(2)}) collective-permute-start(bf16[16,8192]{1,0:T(8,128)(2,1)S(1)} %collective-permute-done.4.two_ref), channel_id=1, source_target_pairs={{0,2},{2,0},{4,6},{6,4},{1,3},{3,1},{5,7},{7,5},{8,10},{10,8},{12,... | collective-permute-start | bytes 786440 | tf_op jit(solution)/shard_map/ppermute | solution.py:282
  53.8 7.1 %collective-permute-start.3 = (bf16[16,8192]{1,0:T(8,128)(2,1)S(1)}, bf16[16,8192]{1,0:T(8,128)(2,1)S(1)}, u32[]{:S(2)}, u32[]{:S(2)}) collective-permute-start(bf16[16,8192]{1,0:T(8,128)(2,1)S(1)} %get-tuple-element.9.one_ref), channel_id=1, source_target_pairs={{0,6},{2,4},{4,2},{6,0},{1,7},{3,5},{5,3},{7,1},{8,14},{10,12},{12... | collective-permute-start | bytes 786440 | tf_op jit(solution)/shard_map/ppermute | solution.py:282
  55.7 8.2 %collective-permute-start.11 = (bf16[32,8192]{1,0:T(8,128)(2,1)S(1)}, bf16[32,8192]{1,0:T(8,128)(2,1)S(1)}, u32[]{:S(2)}, u32[]{:S(2)}) collective-permute-start(bf16[32,8192]{1,0:T(8,128)(2,1)S(1)} %join.2.refs_4_), channel_id=1, source_target_pairs={{0,1},{1,0},{2,3},{3,2},{4,5},{5,4},{6,7},{7,6},{8,9},{9,8},{10,11... | collective-permute-start | bytes 1572872 | tf_op jit(solution)/shard_map/ppermute | solution.py:277
  57.8 6.0 %collective-permute-start.12 = (bf16[32,8192]{1,0:T(8,128)(2,1)S(1)}, bf16[32,8192]{1,0:T(8,128)(2,1)S(1)}, u32[]{:S(2)}, u32[]{:S(2)}) collective-permute-start(bf16[32,8192]{1,0:T(8,128)(2,1)S(1)} %join.3.refs_5_), channel_id=1, source_target_pairs={{0,1},{1,0},{2,3},{3,2},{4,5},{5,4},{6,7},{7,6},{8,9},{9,8},{10,11... | collective-permute-start | bytes 1572872 | tf_op jit(solution)/shard_map/ppermute | solution.py:277
  61.0 4.4 %collective-permute-start.10 = (bf16[32,8192]{1,0:T(8,128)(2,1)S(1)}, bf16[32,8192]{1,0:T(8,128)(2,1)S(1)}, u32[]{:S(2)}, u32[]{:S(2)}) collective-permute-start(bf16[32,8192]{1,0:T(8,128)(2,1)S(1)} %get-tuple-element.11.refs_2_), channel_id=1, source_target_pairs={{0,1},{1,0},{2,3},{3,2},{4,5},{5,4},{6,7},{7,6},{8,9},{9,8},{10,11... | collective-permute-start | bytes 1572872 | tf_op jit(solution)/shard_map/ppermute | solution.py:277

commit v7 on v6

--- a/solution.py
+++ b/solution.py
@@ -210,6 +210,7 @@
         out_specs=(vmem,) + (hbm,) * count,
         input_output_aliases={2 + k: 1 + k for k in range(count)},
         compiler_params=TINY,
+        cost_estimate=pl.CostEstimate(flops=15000000000, transcendentals=0, bytes_accessed=0),
         name="join_after",
     )(in_vmem(one), in_vmem(two), *[in_hbm(array) for array in ready])
 
@@ -242,9 +243,7 @@
         scratch_shapes=[pltpu.SemaphoreType.DMA((count,))],
         input_output_aliases={count: 0} if keep else {},
         compiler_params=TINY,
-        cost_estimate=pl.CostEstimate(
-            flops=0, transcendentals=0, bytes_accessed=sum(part.size for part in parts.values()) * 4
-        ),
+        cost_estimate=pl.CostEstimate(flops=0, transcendentals=0, bytes_accessed=0),
         name="place",
     )(*[in_vmem(part) for part in parts.values()], *[in_hbm(w) for w in keep])
 
@@ -260,7 +259,7 @@
     received = lax.all_to_all(decoded, near, 0, 0, tiled=True)
     partial = jnp.sum(received.astype(jnp.float32), axis=0).astype(jnp.bfloat16)
 
-    for k in (1, 3):
+    for k in (3, 1):
         other = lax.ppermute(partial, "zh", pairs(k))
         total = partial.astype(jnp.float32) + other.astype(jnp.float32)
         partial = total.astype(jnp.bfloat16)

time: 66.4 us -> 66 us (level)
  waiting for transfers between devices: 6.67 us -> 5.73 us
    ppermute x2, waiting for transfers between devices: 4.67 us -> 3.73 us  [shards(): other = lax.ppermute(partial, 'zh', pairs(k))]
where the time goes in v7:
time: 66 us; the launch traced here: 65.8 us
  blocking collectives  25.7 us (39%)
  starting transfers between devices  25.7 us (39%)
  Pallas kernels  7.8 us (12%)
  waiting for transfers between devices  5.73 us (9%)
  between operations  0.77 us (1%)
    all_to_all x1, blocking collectives, shards(): received = lax.all_to_all(decoded, near, 0, 0, tiled=True)  14.8 us
    ppermute x5, starting transfers between devices, swap(): return lax.ppermute(part, 'core', pairs(1, 2))  11.3 us
    all_to_all x1, blocking collectives, shards(): lax.all_to_all(jnp.broadcast_to(average[None], (8,) + average.shape), nea...  10.9 us
    ppermute x2, starting transfers between devices, shards(): other = lax.ppermute(partial, 'zh', pairs(k))  7.33 us
    ppermute x2, waiting for transfers between devices, shards(): other = lax.ppermute(partial, 'zh', pairs(k))  3.73 us
    pallas_call x3, Pallas kernels, place(): pl.pallas_call(functools.partial(place_kernel, steps), out_shape=pltpu.HB...  3.34 us
    ppermute x2, starting transfers between devices, shards(): right = [lax.ppermute(half, 'x', pairs(3)) for half in (second, first)]  2.43 us
    pallas_call x1, Pallas kernels, encode(): pl.pallas_call(encode_kernel, out_shape=pltpu.VMEM((2 * PIECES, HALF, WID...  2.06 us
  transfers between devices with their start and end apart: 13, of which 4 were waited for; matrix products, arithmetic and copies ran while one was open for 0% of the time, Pallas kernels for 7%

profile of v7, /device:TPU:1, one launch (start us, length us, event | category | flops | bytes accessed | tf_op | source)
XLA Modules:
  0.0 65.8 jit_solution(12592594479648538573)
XLA Ops:
  0.6 0.0 copy-start
  0.7 2.1 %encode.1 = bf16[8,16,2048]{2,1,0:T(8,128)(2,1)S(1)} custom-call(bf16[1,32,8192]{2,1,0:T(8,128)(2,1)} %local_hbm.1, bf16[32,8192]{1,0:T(8,128)(2,1)} %base_ref.1), custom_call_target="tpu_custom_call" | custom-call | tf_op jit(solution)/shard_map/encode/pallas_call | solution.py:82
  2.7 14.8 %all_to_all.10 = bf16[8,16,2048]{2,1,0:T(8,128)(2,1)S(1)} all-to-all(bf16[8,16,2048]{2,1,0:T(8,128)(2,1)S(1)} %encode.1), channel_id=1, replica_groups=mesh['zh'=4,'zl'=2,'y'=4,'x'=4,'core'=2] {'zl','y'}, dimensions={0} | all-to-all | bytes 1048576 | tf_op jit(solution)/shard_map/all_to_all | solution.py:259
  17.5 0.1 reduce_sum.12
  17.6 5.2 %collective-permute-start = (bf16[16,2048]{1,0:T(8,128)(2,1)S(1)}, bf16[16,2048]{1,0:T(8,128)(2,1)S(1)}, u32[]{:S(2)}, u32[]{:S(2)}) collective-permute-start(bf16[16,2048]{1,0:T(8,128)(2,1)S(1)} %reduce_sum.12), channel_id=1, source_target_pairs={{0,192},{64,128},{128,64},{192,0},{1,193},{65,129},{129,65},{193,1... | collective-permute-start | bytes 196616 | tf_op jit(solution)/shard_map/ppermute | solution.py:263
  22.8 1.8 %collective-permute-done = bf16[16,2048]{1,0:T(8,128)(2,1)S(1)} collective-permute-done((bf16[16,2048]{1,0:T(8,128)(2,1)S(1)}, bf16[16,2048]{1,0:T(8,128)(2,1)S(1)}, u32[]{:S(2)}, u32[]{:S(2)}) %collective-permute-start) | collective-permute-done | bytes 65568 | tf_op jit(solution)/shard_map/ppermute | solution.py:263
  24.6 2.1 %collective-permute-start.1 = (bf16[16,2048]{1,0:T(8,128)(2,1)S(1)}, bf16[16,2048]{1,0:T(8,128)(2,1)S(1)}, u32[]{:S(2)}, u32[]{:S(2)}) collective-permute-start(bf16[16,2048]{1,0:T(8,128)(2,1)S(1)} %add_convert_fusion), channel_id=1, source_target_pairs={{0,64},{64,0},{128,192},{192,128},{1,65},{65,1},{129,193},{193,129... | collective-permute-start | bytes 196616 | tf_op jit(solution)/shard_map/ppermute | solution.py:263
  26.7 2.0 %collective-permute-done.1 = bf16[16,2048]{1,0:T(8,128)(2,1)S(1)} collective-permute-done((bf16[16,2048]{1,0:T(8,128)(2,1)S(1)}, bf16[16,2048]{1,0:T(8,128)(2,1)S(1)}, u32[]{:S(2)}, u32[]{:S(2)}) %collective-permute-start.1) | collective-permute-done | bytes 65568 | tf_op jit(solution)/shard_map/ppermute | solution.py:263
  28.8 10.9 %all_to_all.11.average_ref = bf16[8,16,2048]{2,1,0:T(8,128)(2,1)S(1)} all-to-all(bf16[8,16,2048]{2,1,0:T(8,128)(2,1)S(1)} %broadcast_in_dim.2), channel_id=1, replica_groups=mesh['zh'=4,'zl'=2,'y'=4,'x'=4,'core'=2] {'zl','y'}, dimensions={0} | all-to-all | bytes 1048576 | tf_op jit(solution)/shard_map/all_to_all | solution.py:268
  39.7 0.3 update_base.1
  40.0 1.3 %collective-permute-start.2 = (bf16[16,8192]{1,0:T(8,128)(2,1)S(1)}, bf16[16,8192]{1,0:T(8,128)(2,1)S(1)}, u32[]{:S(2)}, u32[]{:S(2)}) collective-permute-start(bf16[16,8192]{1,0:T(8,128)(2,1)S(1)} %get-tuple-element.8.refs_0_), channel_id=1, source_target_pairs={{0,2},{2,0},{4,6},{6,4},{1,3},{3,1},{5,7},{7,5},{8,10},{10,8},{12,... | collective-permute-start | bytes 786440 | tf_op jit(solution)/shard_map/ppermute | solution.py:278
  41.3 1.8 %collective-permute-start.4 = (bf16[16,8192]{1,0:T(8,128)(2,1)S(1)}, bf16[16,8192]{1,0:T(8,128)(2,1)S(1)}, u32[]{:S(2)}, u32[]{:S(2)}) collective-permute-start(bf16[16,8192]{1,0:T(8,128)(2,1)S(1)} %get-tuple-element.10.refs_1_), channel_id=1, source_target_pairs={{0,6},{2,4},{4,2},{6,0},{1,7},{3,5},{5,3},{7,1},{8,14},{10,12},{12... | collective-permute-start | bytes 786440 | tf_op jit(solution)/shard_map/ppermute | solution.py:279
  43.1 0.3 collective-permute-start.8
  43.4 0.6 collective-permute-start.9
  44.0 6.1 %collective-permute-start.6 = (bf16[16,8192]{1,0:T(8,128)(2,1)S(1)}, bf16[16,8192]{1,0:T(8,128)(2,1)S(1)}, u32[]{:S(2)}, u32[]{:S(2)}) collective-permute-start(bf16[16,8192]{1,0:T(8,128)(2,1)S(1)} %get-tuple-element.8.refs_0_), channel_id=1, source_target_pairs={{0,1},{1,0},{2,3},{3,2},{4,5},{5,4},{6,7},{7,6},{8,9},{9,8},{10,11... | collective-permute-start | bytes 786440 | tf_op jit(solution)/shard_map/ppermute | solution.py:276
  50.1 2.0 %update_momentum.1.refs_1_ = f32[32,8192]{1,0:T(8,128)} custom-call(bf16[8,16,2048]{2,1,0:T(8,128)(2,1)S(1)} %all_to_all.11.average_ref, f32[32,8192]{1,0:T(8,128)} %momentum_hbm.1), custom_call_target="tpu_custom_call" | custom-call | tf_op jit(solution)/shard_map/update_momentum/pallas_call | solution.py:152
  52.2 0.1 collective-permute-start.7
  52.3 0.0 collective-permute-done.4.two_ref
  52.3 1.2 %collective-permute-start.5 = (bf16[16,8192]{1,0:T(8,128)(2,1)S(1)}, bf16[16,8192]{1,0:T(8,128)(2,1)S(1)}, u32[]{:S(2)}, u32[]{:S(2)}) collective-permute-start(bf16[16,8192]{1,0:T(8,128)(2,1)S(1)} %collective-permute-done.4.two_ref), channel_id=1, source_target_pairs={{0,2},{2,0},{4,6},{6,4},{1,3},{3,1},{5,7},{7,5},{8,10},{10,8},{12,... | collective-permute-start | bytes 786440 | tf_op jit(solution)/shard_map/ppermute | solution.py:281
  53.4 0.0 collective-permute-done.8.two_ref
  53.4 1.8 %collective-permute-start.3 = (bf16[16,8192]{1,0:T(8,128)(2,1)S(1)}, bf16[16,8192]{1,0:T(8,128)(2,1)S(1)}, u32[]{:S(2)}, u32[]{:S(2)}) collective-permute-start(bf16[16,8192]{1,0:T(8,128)(2,1)S(1)} %get-tuple-element.9.one_ref), channel_id=1, source_target_pairs={{0,6},{2,4},{4,2},{6,0},{1,7},{3,5},{5,3},{7,1},{8,14},{10,12},{12... | collective-permute-start | bytes 786440 | tf_op jit(solution)/shard_map/ppermute | solution.py:281
  55.3 0.0 collective-permute-done.9.one_ref
  55.3 2.1 %collective-permute-start.11 = (bf16[32,8192]{1,0:T(8,128)(2,1)S(1)}, bf16[32,8192]{1,0:T(8,128)(2,1)S(1)}, u32[]{:S(2)}, u32[]{:S(2)}) collective-permute-start(bf16[32,8192]{1,0:T(8,128)(2,1)S(1)} %join.2.refs_4_), channel_id=1, source_target_pairs={{0,1},{1,0},{2,3},{3,2},{4,5},{5,4},{6,7},{7,6},{8,9},{9,8},{10,11... | collective-permute-start | bytes 1572872 | tf_op jit(solution)/shard_map/ppermute | solution.py:276
  57.5 0.0 collective-permute-done.6.refs_2_
  57.5 0.1 collective-permute-start.12
  57.6 1.4 %place.3.refs_0_ = bf16[256,8192]{1,0:T(8,128)(2,1)} custom-call(bf16[16,8192]{1,0:T(8,128)(2,1)S(1)} %get-tuple-element.8.refs_0_, bf16[16,8192]{1,0:T(8,128)(2,1)S(1)} %get-tuple-element.10.refs_1_, bf16[16,8192]{1,0:T(8,128)(2,1)S(1)} %collective-permute-done.6.refs_2_, bf16[16,8192]{1,0:T(8,128)(2,1)S(1)} %collective-permute-done.7.refs_3_, ...), custom_call_target="tpu_custom_call" | custom-call | tf_op jit(solution)/shard_map/place/pallas_call | solution.py:238
  59.0 0.0 collective-permute-done.5.two_ref
  59.0 1.6 %collective-permute-done.3.one_ref = bf16[16,8192]{1,0:T(8,128)(2,1)S(1)} collective-permute-done((bf16[16,8192]{1,0:T(8,128)(2,1)S(1)}, bf16[16,8192]{1,0:T(8,128)(2,1)S(1)}, u32[]{:S(2)}, u32[]{:S(2)}) %collective-permute-start.3) | collective-permute-done | bytes 262176 | tf_op jit(solution)/shard_map/ppermute | solution.py:281
  60.6 2.9 %collective-permute-start.10 = (bf16[32,8192]{1,0:T(8,128)(2,1)S(1)}, bf16[32,8192]{1,0:T(8,128)(2,1)S(1)}, u32[]{:S(2)}, u32[]{:S(2)}) collective-permute-start(bf16[32,8192]{1,0:T(8,128)(2,1)S(1)} %get-tuple-element.11.refs_2_), channel_id=1, source_target_pairs={{0,1},{1,0},{2,3},{3,2},{4,5},{5,4},{6,7},{7,6},{8,9},{9,8},{10,11... | collective-permute-start | bytes 1572872 | tf_op jit(solution)/shard_map/ppermute | solution.py:276
  63.5 1.2 %place.4.refs_1_ = bf16[256,8192]{1,0:T(8,128)(2,1)} custom-call(bf16[32,8192]{1,0:T(8,128)(2,1)S(1)} %collective-permute-done.11.refs_0_, bf16[32,8192]{1,0:T(8,128)(2,1)S(1)} %collective-permute-done.12.refs_1_, bf16[32,8192]{1,0:T(8,128)(2,1)S(1)} %get-tuple-element.11.refs_2_, ...), custom_call_target="tpu_custom_call", output_to_operand_aliasing={{}: (3, {})} | custom-call | tf_op jit(solution)/shard_map/place/pallas_call | solution.py:238
  64.7 0.4 collective-permute-done.10.refs_0_
  65.0 0.8 %place.5 = bf16[256,8192]{1,0:T(8,128)(2,1)} custom-call(bf16[32,8192]{1,0:T(8,128)(2,1)S(1)} %collective-permute-done.10.refs_0_, bf16[256,8192]{1,0:T(8,128)(2,1)} %place.4.refs_1_), custom_call_target="tpu_custom_call", output_to_operand_aliasing={{}: (1, {})} | custom-call | tf_op jit(solution)/shard_map/place/pallas_call | solution.py:238
  (14 shorter events, 0.2 us)
Async XLA Ops:
  0.6 39.0 %copy-start.1 = (bf16[32,8192]{1,0:T(8,128)(2,1)S(1)}, bf16[32,8192]{1,0:T(8,128)(2,1)}, u32[]{:S(2)}) copy-start(bf16[32,8192]{1,0:T(8,128)(2,1)} %base_ref.1) | copy-start | bytes 1572868
  0.6 39.0 %copy-start = (f32[32,8192]{1,0:T(8,128)S(1)}, f32[32,8192]{1,0:T(8,128)}, u32[]{:S(2)}) copy-start(f32[32,8192]{1,0:T(8,128)} %momentum_hbm.1) | copy-start | bytes 3145732
  17.6 7.0 %collective-permute-start = (bf16[16,2048]{1,0:T(8,128)(2,1)S(1)}, bf16[16,2048]{1,0:T(8,128)(2,1)S(1)}, u32[]{:S(2)}, u32[]{:S(2)}) collective-permute-start(bf16[16,2048]{1,0:T(8,128)(2,1)S(1)} %reduce_sum.12), channel_id=1, source_target_pairs={{0,192},{64,128},{128,64},{192,0},{1,193},{65,129},{129,65},{193,1... | collective-permute-start | bytes 196616 | tf_op jit(solution)/shard_map/ppermute | solution.py:263
  24.6 4.1 %collective-permute-start.1 = (bf16[16,2048]{1,0:T(8,128)(2,1)S(1)}, bf16[16,2048]{1,0:T(8,128)(2,1)S(1)}, u32[]{:S(2)}, u32[]{:S(2)}) collective-permute-start(bf16[16,2048]{1,0:T(8,128)(2,1)S(1)} %add_convert_fusion), channel_id=1, source_target_pairs={{0,64},{64,0},{128,192},{192,128},{1,65},{65,1},{129,193},{193,129... | collective-permute-start | bytes 196616 | tf_op jit(solution)/shard_map/ppermute | solution.py:263
  40.0 12.2 %collective-permute-start.2 = (bf16[16,8192]{1,0:T(8,128)(2,1)S(1)}, bf16[16,8192]{1,0:T(8,128)(2,1)S(1)}, u32[]{:S(2)}, u32[]{:S(2)}) collective-permute-start(bf16[16,8192]{1,0:T(8,128)(2,1)S(1)} %get-tuple-element.8.refs_0_), channel_id=1, source_target_pairs={{0,2},{2,0},{4,6},{6,4},{1,3},{3,1},{5,7},{7,5},{8,10},{10,8},{12,... | collective-permute-start | bytes 786440 | tf_op jit(solution)/shard_map/ppermute | solution.py:278
  41.3 11.0 %collective-permute-start.4 = (bf16[16,8192]{1,0:T(8,128)(2,1)S(1)}, bf16[16,8192]{1,0:T(8,128)(2,1)S(1)}, u32[]{:S(2)}, u32[]{:S(2)}) collective-permute-start(bf16[16,8192]{1,0:T(8,128)(2,1)S(1)} %get-tuple-element.10.refs_1_), channel_id=1, source_target_pairs={{0,6},{2,4},{4,2},{6,0},{1,7},{3,5},{5,3},{7,1},{8,14},{10,12},{12... | collective-permute-start | bytes 786440 | tf_op jit(solution)/shard_map/ppermute | solution.py:279
  43.1 10.4 %collective-permute-start.8 = (bf16[16,8192]{1,0:T(8,128)(2,1)S(1)}, bf16[16,8192]{1,0:T(8,128)(2,1)S(1)}, u32[]{:S(2)}, u32[]{:S(2)}) collective-permute-start(bf16[16,8192]{1,0:T(8,128)(2,1)S(1)} %get-tuple-element.10.refs_1_), channel_id=1, source_target_pairs={{0,2},{2,0},{4,6},{6,4},{1,3},{3,1},{5,7},{7,5},{8,10},{10,8},{12,... | collective-permute-start | bytes 786440 | tf_op jit(solution)/shard_map/ppermute | solution.py:278
  43.4 11.9 %collective-permute-start.9 = (bf16[16,8192]{1,0:T(8,128)(2,1)S(1)}, bf16[16,8192]{1,0:T(8,128)(2,1)S(1)}, u32[]{:S(2)}, u32[]{:S(2)}) collective-permute-start(bf16[16,8192]{1,0:T(8,128)(2,1)S(1)} %get-tuple-element.8.refs_0_), channel_id=1, source_target_pairs={{0,6},{2,4},{4,2},{6,0},{1,7},{3,5},{5,3},{7,1},{8,14},{10,12},{12... | collective-permute-start | bytes 786440 | tf_op jit(solution)/shard_map/ppermute | solution.py:279
  44.0 13.5 %collective-permute-start.6 = (bf16[16,8192]{1,0:T(8,128)(2,1)S(1)}, bf16[16,8192]{1,0:T(8,128)(2,1)S(1)}, u32[]{:S(2)}, u32[]{:S(2)}) collective-permute-start(bf16[16,8192]{1,0:T(8,128)(2,1)S(1)} %get-tuple-element.8.refs_0_), channel_id=1, source_target_pairs={{0,1},{1,0},{2,3},{3,2},{4,5},{5,4},{6,7},{7,6},{8,9},{9,8},{10,11... | collective-permute-start | bytes 786440 | tf_op jit(solution)/shard_map/ppermute | solution.py:276
  52.2 5.4 %collective-permute-start.7 = (bf16[16,8192]{1,0:T(8,128)(2,1)S(1)}, bf16[16,8192]{1,0:T(8,128)(2,1)S(1)}, u32[]{:S(2)}, u32[]{:S(2)}) collective-permute-start(bf16[16,8192]{1,0:T(8,128)(2,1)S(1)} %get-tuple-element.10.refs_1_), channel_id=1, source_target_pairs={{0,1},{1,0},{2,3},{3,2},{4,5},{5,4},{6,7},{7,6},{8,9},{9,8},{10,11... | collective-permute-start | bytes 786440 | tf_op jit(solution)/shard_map/ppermute | solution.py:276
  52.3 6.7 %collective-permute-start.5 = (bf16[16,8192]{1,0:T(8,128)(2,1)S(1)}, bf16[16,8192]{1,0:T(8,128)(2,1)S(1)}, u32[]{:S(2)}, u32[]{:S(2)}) collective-permute-start(bf16[16,8192]{1,0:T(8,128)(2,1)S(1)} %collective-permute-done.4.two_ref), channel_id=1, source_target_pairs={{0,2},{2,0},{4,6},{6,4},{1,3},{3,1},{5,7},{7,5},{8,10},{10,8},{12,... | collective-permute-start | bytes 786440 | tf_op jit(solution)/shard_map/ppermute | solution.py:281
  53.4 7.1 %collective-permute-start.3 = (bf16[16,8192]{1,0:T(8,128)(2,1)S(1)}, bf16[16,8192]{1,0:T(8,128)(2,1)S(1)}, u32[]{:S(2)}, u32[]{:S(2)}) collective-permute-start(bf16[16,8192]{1,0:T(8,128)(2,1)S(1)} %get-tuple-element.9.one_ref), channel_id=1, source_target_pairs={{0,6},{2,4},{4,2},{6,0},{1,7},{3,5},{5,3},{7,1},{8,14},{10,12},{12... | collective-permute-start | bytes 786440 | tf_op jit(solution)/shard_map/ppermute | solution.py:281
  55.3 8.2 %collective-permute-start.11 = (bf16[32,8192]{1,0:T(8,128)(2,1)S(1)}, bf16[32,8192]{1,0:T(8,128)(2,1)S(1)}, u32[]{:S(2)}, u32[]{:S(2)}) collective-permute-start(bf16[32,8192]{1,0:T(8,128)(2,1)S(1)} %join.2.refs_4_), channel_id=1, source_target_pairs={{0,1},{1,0},{2,3},{3,2},{4,5},{5,4},{6,7},{7,6},{8,9},{9,8},{10,11... | collective-permute-start | bytes 1572872 | tf_op jit(solution)/shard_map/ppermute | solution.py:276
  57.5 6.0 %collective-permute-start.12 = (bf16[32,8192]{1,0:T(8,128)(2,1)S(1)}, bf16[32,8192]{1,0:T(8,128)(2,1)S(1)}, u32[]{:S(2)}, u32[]{:S(2)}) collective-permute-start(bf16[32,8192]{1,0:T(8,128)(2,1)S(1)} %join.3.refs_5_), channel_id=1, source_target_pairs={{0,1},{1,0},{2,3},{3,2},{4,5},{5,4},{6,7},{7,6},{8,9},{9,8},{10,11... | collective-permute-start | bytes 1572872 | tf_op jit(solution)/shard_map/ppermute | solution.py:276
  60.6 4.4 %collective-permute-start.10 = (bf16[32,8192]{1,0:T(8,128)(2,1)S(1)}, bf16[32,8192]{1,0:T(8,128)(2,1)S(1)}, u32[]{:S(2)}, u32[]{:S(2)}) collective-permute-start(bf16[32,8192]{1,0:T(8,128)(2,1)S(1)} %get-tuple-element.11.refs_2_), channel_id=1, source_target_pairs={{0,1},{1,0},{2,3},{3,2},{4,5},{5,4},{6,7},{7,6},{8,9},{9,8},{10,11... | collective-permute-start | bytes 1572872 | tf_op jit(solution)/shard_map/ppermute | solution.py:276

commit v8 on v7

--- a/solution.py
+++ b/solution.py
@@ -41,8 +41,8 @@
     for pair in copies:
         for copy in pair:
             copy.start()
-    block = lax.broadcasted_iota(jnp.int32, (LANES, LANES), 0) // BLOCK
-    block_t = lax.broadcasted_iota(jnp.int32, (LANES, LANES), 1) // BLOCK
+    block = lax.broadcasted_iota(jnp.int32, (3 * LANES, LANES), 0) % LANES // BLOCK
+    block_t = lax.broadcasted_iota(jnp.int32, (3 * LANES, LANES), 1) // BLOCK
     same_block = jnp.where(block == block_t, 1.0 / BLOCK, 0.0).astype(jnp.bfloat16)
     for k in range(2 * PIECES):
         half, piece = k // PIECES, k % PIECES
@@ -56,11 +56,13 @@
         tall = jnp.concatenate(
             [grad[:, i * LANES : (i + 1) * LANES] for i in range(WIDE // LANES)], axis=0
         )
-        rest, mean_square = tall * tall, 0.0
+        rest, parts = tall * tall, []
         for _ in range(3):
-            part = rest.astype(jnp.bfloat16)
-            rest = rest - part.astype(jnp.float32)
-            mean_square += jnp.dot(part, same_block, preferred_element_type=jnp.float32)
+            parts.append(rest.astype(jnp.bfloat16))
+            rest = rest - parts[-1].astype(jnp.float32)
+        mean_square = jnp.dot(
+            jnp.concatenate(parts, axis=1), same_block, preferred_element_type=jnp.float32
+        )
         floored = jnp.maximum(mean_square, floor_value * floor_value)
         scale = (floored * lax.rsqrt(floored) * (1.0 / spread_ratio)).astype(jnp.bfloat16)
         limit = code_peak * scale.astype(jnp.float32)

time: 66 us -> 66 us (level)
  no operation moved by 1% of the time
where the time goes in v8:
time: 66 us; the launch traced here: 65.8 us
  starting transfers between devices  25.7 us (39%)
  blocking collectives  25.6 us (39%)
  Pallas kernels  7.79 us (12%)
  waiting for transfers between devices  5.73 us (9%)
  between operations  0.77 us (1%)
    all_to_all x1, blocking collectives, shards(): received = lax.all_to_all(decoded, near, 0, 0, tiled=True)  14.8 us
    ppermute x5, starting transfers between devices, swap(): return lax.ppermute(part, 'core', pairs(1, 2))  11.3 us
    all_to_all x1, blocking collectives, shards(): lax.all_to_all(jnp.broadcast_to(average[None], (8,) + average.shape), nea...  10.9 us
    ppermute x2, starting transfers between devices, shards(): other = lax.ppermute(partial, 'zh', pairs(k))  7.35 us
    ppermute x2, waiting for transfers between devices, shards(): other = lax.ppermute(partial, 'zh', pairs(k))  3.74 us
    pallas_call x3, Pallas kernels, place(): pl.pallas_call(functools.partial(place_kernel, steps), out_shape=pltpu.HB...  3.34 us
    ppermute x2, starting transfers between devices, shards(): right = [lax.ppermute(half, 'x', pairs(3)) for half in (second, first)]  2.43 us
    pallas_call x1, Pallas kernels, encode(): pl.pallas_call(encode_kernel, out_shape=pltpu.VMEM((2 * PIECES, HALF, WID...  2.05 us
  transfers between devices with their start and end apart: 13, of which 4 were waited for; matrix products, arithmetic and copies ran while one was open for 0% of the time, Pallas kernels for 7%

profile of v8, /device:TPU:1, one launch (start us, length us, event | category | flops | bytes accessed | tf_op | source)
XLA Modules:
  0.0 65.8 jit_solution(14840511341541361661)
XLA Ops:
  0.6 0.0 copy-start
  0.7 2.0 %encode.1 = bf16[8,16,2048]{2,1,0:T(8,128)(2,1)S(1)} custom-call(bf16[1,32,8192]{2,1,0:T(8,128)(2,1)} %local_hbm.1, bf16[32,8192]{1,0:T(8,128)(2,1)} %base_ref.1), custom_call_target="tpu_custom_call" | custom-call | tf_op jit(solution)/shard_map/encode/pallas_call | solution.py:84
  2.7 14.8 %all_to_all.10 = bf16[8,16,2048]{2,1,0:T(8,128)(2,1)S(1)} all-to-all(bf16[8,16,2048]{2,1,0:T(8,128)(2,1)S(1)} %encode.1), channel_id=1, replica_groups=mesh['zh'=4,'zl'=2,'y'=4,'x'=4,'core'=2] {'zl','y'}, dimensions={0} | all-to-all | bytes 1048576 | tf_op jit(solution)/shard_map/all_to_all | solution.py:261
  17.5 0.1 reduce_sum.12
  17.5 5.2 %collective-permute-start = (bf16[16,2048]{1,0:T(8,128)(2,1)S(1)}, bf16[16,2048]{1,0:T(8,128)(2,1)S(1)}, u32[]{:S(2)}, u32[]{:S(2)}) collective-permute-start(bf16[16,2048]{1,0:T(8,128)(2,1)S(1)} %reduce_sum.12), channel_id=1, source_target_pairs={{0,192},{64,128},{128,64},{192,0},{1,193},{65,129},{129,65},{193,1... | collective-permute-start | bytes 196616 | tf_op jit(solution)/shard_map/ppermute | solution.py:265
  22.8 1.8 %collective-permute-done = bf16[16,2048]{1,0:T(8,128)(2,1)S(1)} collective-permute-done((bf16[16,2048]{1,0:T(8,128)(2,1)S(1)}, bf16[16,2048]{1,0:T(8,128)(2,1)S(1)}, u32[]{:S(2)}, u32[]{:S(2)}) %collective-permute-start) | collective-permute-done | bytes 65568 | tf_op jit(solution)/shard_map/ppermute | solution.py:265
  24.5 2.1 %collective-permute-start.1 = (bf16[16,2048]{1,0:T(8,128)(2,1)S(1)}, bf16[16,2048]{1,0:T(8,128)(2,1)S(1)}, u32[]{:S(2)}, u32[]{:S(2)}) collective-permute-start(bf16[16,2048]{1,0:T(8,128)(2,1)S(1)} %add_convert_fusion), channel_id=1, source_target_pairs={{0,64},{64,0},{128,192},{192,128},{1,65},{65,1},{129,193},{193,129... | collective-permute-start | bytes 196616 | tf_op jit(solution)/shard_map/ppermute | solution.py:265
  26.7 2.0 %collective-permute-done.1 = bf16[16,2048]{1,0:T(8,128)(2,1)S(1)} collective-permute-done((bf16[16,2048]{1,0:T(8,128)(2,1)S(1)}, bf16[16,2048]{1,0:T(8,128)(2,1)S(1)}, u32[]{:S(2)}, u32[]{:S(2)}) %collective-permute-start.1) | collective-permute-done | bytes 65568 | tf_op jit(solution)/shard_map/ppermute | solution.py:265
  28.7 10.9 %all_to_all.11.average_ref = bf16[8,16,2048]{2,1,0:T(8,128)(2,1)S(1)} all-to-all(bf16[8,16,2048]{2,1,0:T(8,128)(2,1)S(1)} %broadcast_in_dim.2), channel_id=1, replica_groups=mesh['zh'=4,'zl'=2,'y'=4,'x'=4,'core'=2] {'zl','y'}, dimensions={0} | all-to-all | bytes 1048576 | tf_op jit(solution)/shard_map/all_to_all | solution.py:270
  39.6 0.3 update_base.1
  39.9 1.3 %collective-permute-start.2 = (bf16[16,8192]{1,0:T(8,128)(2,1)S(1)}, bf16[16,8192]{1,0:T(8,128)(2,1)S(1)}, u32[]{:S(2)}, u32[]{:S(2)}) collective-permute-start(bf16[16,8192]{1,0:T(8,128)(2,1)S(1)} %get-tuple-element.8.refs_0_), channel_id=1, source_target_pairs={{0,2},{2,0},{4,6},{6,4},{1,3},{3,1},{5,7},{7,5},{8,10},{10,8},{12,... | collective-permute-start | bytes 786440 | tf_op jit(solution)/shard_map/ppermute | solution.py:280
  41.2 1.8 %collective-permute-start.4 = (bf16[16,8192]{1,0:T(8,128)(2,1)S(1)}, bf16[16,8192]{1,0:T(8,128)(2,1)S(1)}, u32[]{:S(2)}, u32[]{:S(2)}) collective-permute-start(bf16[16,8192]{1,0:T(8,128)(2,1)S(1)} %get-tuple-element.10.refs_1_), channel_id=1, source_target_pairs={{0,6},{2,4},{4,2},{6,0},{1,7},{3,5},{5,3},{7,1},{8,14},{10,12},{12... | collective-permute-start | bytes 786440 | tf_op jit(solution)/shard_map/ppermute | solution.py:281
  43.1 0.3 collective-permute-start.8
  43.3 0.6 collective-permute-start.9
  44.0 6.2 %collective-permute-start.6 = (bf16[16,8192]{1,0:T(8,128)(2,1)S(1)}, bf16[16,8192]{1,0:T(8,128)(2,1)S(1)}, u32[]{:S(2)}, u32[]{:S(2)}) collective-permute-start(bf16[16,8192]{1,0:T(8,128)(2,1)S(1)} %get-tuple-element.8.refs_0_), channel_id=1, source_target_pairs={{0,1},{1,0},{2,3},{3,2},{4,5},{5,4},{6,7},{7,6},{8,9},{9,8},{10,11... | collective-permute-start | bytes 786440 | tf_op jit(solution)/shard_map/ppermute | solution.py:278
  50.1 2.0 %update_momentum.1.refs_1_ = f32[32,8192]{1,0:T(8,128)} custom-call(bf16[8,16,2048]{2,1,0:T(8,128)(2,1)S(1)} %all_to_all.11.average_ref, f32[32,8192]{1,0:T(8,128)} %momentum_hbm.1), custom_call_target="tpu_custom_call" | custom-call | tf_op jit(solution)/shard_map/update_momentum/pallas_call | solution.py:154
  52.1 0.0 collective-permute-done.2.refs_0_
  52.1 0.1 collective-permute-start.7
  52.2 1.2 %collective-permute-start.5 = (bf16[16,8192]{1,0:T(8,128)(2,1)S(1)}, bf16[16,8192]{1,0:T(8,128)(2,1)S(1)}, u32[]{:S(2)}, u32[]{:S(2)}) collective-permute-start(bf16[16,8192]{1,0:T(8,128)(2,1)S(1)} %collective-permute-done.4.two_ref), channel_id=1, source_target_pairs={{0,2},{2,0},{4,6},{6,4},{1,3},{3,1},{5,7},{7,5},{8,10},{10,8},{12,... | collective-permute-start | bytes 786440 | tf_op jit(solution)/shard_map/ppermute | solution.py:283
  53.4 0.0 collective-permute-done.8.two_ref
  53.4 1.8 %collective-permute-start.3 = (bf16[16,8192]{1,0:T(8,128)(2,1)S(1)}, bf16[16,8192]{1,0:T(8,128)(2,1)S(1)}, u32[]{:S(2)}, u32[]{:S(2)}) collective-permute-start(bf16[16,8192]{1,0:T(8,128)(2,1)S(1)} %get-tuple-element.9.one_ref), channel_id=1, source_target_pairs={{0,6},{2,4},{4,2},{6,0},{1,7},{3,5},{5,3},{7,1},{8,14},{10,12},{12... | collective-permute-start | bytes 786440 | tf_op jit(solution)/shard_map/ppermute | solution.py:283
  55.3 2.1 %collective-permute-start.11 = (bf16[32,8192]{1,0:T(8,128)(2,1)S(1)}, bf16[32,8192]{1,0:T(8,128)(2,1)S(1)}, u32[]{:S(2)}, u32[]{:S(2)}) collective-permute-start(bf16[32,8192]{1,0:T(8,128)(2,1)S(1)} %join.2.refs_4_), channel_id=1, source_target_pairs={{0,1},{1,0},{2,3},{3,2},{4,5},{5,4},{6,7},{7,6},{8,9},{9,8},{10,11... | collective-permute-start | bytes 1572872 | tf_op jit(solution)/shard_map/ppermute | solution.py:278
  57.4 0.0 collective-permute-done.6.refs_2_
  57.4 0.1 collective-permute-start.12
  57.6 0.0 collective-permute-done.7.refs_3_
  57.6 1.4 %place.3.refs_0_ = bf16[256,8192]{1,0:T(8,128)(2,1)} custom-call(bf16[16,8192]{1,0:T(8,128)(2,1)S(1)} %get-tuple-element.8.refs_0_, bf16[16,8192]{1,0:T(8,128)(2,1)S(1)} %get-tuple-element.10.refs_1_, bf16[16,8192]{1,0:T(8,128)(2,1)S(1)} %collective-permute-done.6.refs_2_, bf16[16,8192]{1,0:T(8,128)(2,1)S(1)} %collective-permute-done.7.refs_3_, ...), custom_call_target="tpu_custom_call" | custom-call | tf_op jit(solution)/shard_map/place/pallas_call | solution.py:240
  58.9 1.6 %collective-permute-done.3.one_ref = bf16[16,8192]{1,0:T(8,128)(2,1)S(1)} collective-permute-done((bf16[16,8192]{1,0:T(8,128)(2,1)S(1)}, bf16[16,8192]{1,0:T(8,128)(2,1)S(1)}, u32[]{:S(2)}, u32[]{:S(2)}) %collective-permute-start.3) | collective-permute-done | bytes 262176 | tf_op jit(solution)/shard_map/ppermute | solution.py:283
  60.6 2.9 %collective-permute-start.10 = (bf16[32,8192]{1,0:T(8,128)(2,1)S(1)}, bf16[32,8192]{1,0:T(8,128)(2,1)S(1)}, u32[]{:S(2)}, u32[]{:S(2)}) collective-permute-start(bf16[32,8192]{1,0:T(8,128)(2,1)S(1)} %get-tuple-element.11.refs_2_), channel_id=1, source_target_pairs={{0,1},{1,0},{2,3},{3,2},{4,5},{5,4},{6,7},{7,6},{8,9},{9,8},{10,11... | collective-permute-start | bytes 1572872 | tf_op jit(solution)/shard_map/ppermute | solution.py:278
  63.5 0.0 collective-permute-done.11.refs_0_
  63.5 1.2 %place.4.refs_1_ = bf16[256,8192]{1,0:T(8,128)(2,1)} custom-call(bf16[32,8192]{1,0:T(8,128)(2,1)S(1)} %collective-permute-done.11.refs_0_, bf16[32,8192]{1,0:T(8,128)(2,1)S(1)} %collective-permute-done.12.refs_1_, bf16[32,8192]{1,0:T(8,128)(2,1)S(1)} %get-tuple-element.11.refs_2_, ...), custom_call_target="tpu_custom_call", output_to_operand_aliasing={{}: (3, {})} | custom-call | tf_op jit(solution)/shard_map/place/pallas_call | solution.py:240
  64.7 0.4 collective-permute-done.10.refs_0_
  65.0 0.8 %place.5 = bf16[256,8192]{1,0:T(8,128)(2,1)} custom-call(bf16[32,8192]{1,0:T(8,128)(2,1)S(1)} %collective-permute-done.10.refs_0_, bf16[256,8192]{1,0:T(8,128)(2,1)} %place.4.refs_1_), custom_call_target="tpu_custom_call", output_to_operand_aliasing={{}: (1, {})} | custom-call | tf_op jit(solution)/shard_map/place/pallas_call | solution.py:240
  (14 shorter events, 0.2 us)
Async XLA Ops:
  0.6 39.0 %copy-start.1 = (bf16[32,8192]{1,0:T(8,128)(2,1)S(1)}, bf16[32,8192]{1,0:T(8,128)(2,1)}, u32[]{:S(2)}) copy-start(bf16[32,8192]{1,0:T(8,128)(2,1)} %base_ref.1) | copy-start | bytes 1572868
  0.6 39.0 %copy-start = (f32[32,8192]{1,0:T(8,128)S(1)}, f32[32,8192]{1,0:T(8,128)}, u32[]{:S(2)}) copy-start(f32[32,8192]{1,0:T(8,128)} %momentum_hbm.1) | copy-start | bytes 3145732
  17.5 7.0 %collective-permute-start = (bf16[16,2048]{1,0:T(8,128)(2,1)S(1)}, bf16[16,2048]{1,0:T(8,128)(2,1)S(1)}, u32[]{:S(2)}, u32[]{:S(2)}) collective-permute-start(bf16[16,2048]{1,0:T(8,128)(2,1)S(1)} %reduce_sum.12), channel_id=1, source_target_pairs={{0,192},{64,128},{128,64},{192,0},{1,193},{65,129},{129,65},{193,1... | collective-permute-start | bytes 196616 | tf_op jit(solution)/shard_map/ppermute | solution.py:265
  24.5 4.1 %collective-permute-start.1 = (bf16[16,2048]{1,0:T(8,128)(2,1)S(1)}, bf16[16,2048]{1,0:T(8,128)(2,1)S(1)}, u32[]{:S(2)}, u32[]{:S(2)}) collective-permute-start(bf16[16,2048]{1,0:T(8,128)(2,1)S(1)} %add_convert_fusion), channel_id=1, source_target_pairs={{0,64},{64,0},{128,192},{192,128},{1,65},{65,1},{129,193},{193,129... | collective-permute-start | bytes 196616 | tf_op jit(solution)/shard_map/ppermute | solution.py:265
  39.9 12.2 %collective-permute-start.2 = (bf16[16,8192]{1,0:T(8,128)(2,1)S(1)}, bf16[16,8192]{1,0:T(8,128)(2,1)S(1)}, u32[]{:S(2)}, u32[]{:S(2)}) collective-permute-start(bf16[16,8192]{1,0:T(8,128)(2,1)S(1)} %get-tuple-element.8.refs_0_), channel_id=1, source_target_pairs={{0,2},{2,0},{4,6},{6,4},{1,3},{3,1},{5,7},{7,5},{8,10},{10,8},{12,... | collective-permute-start | bytes 786440 | tf_op jit(solution)/shard_map/ppermute | solution.py:280
  41.2 11.0 %collective-permute-start.4 = (bf16[16,8192]{1,0:T(8,128)(2,1)S(1)}, bf16[16,8192]{1,0:T(8,128)(2,1)S(1)}, u32[]{:S(2)}, u32[]{:S(2)}) collective-permute-start(bf16[16,8192]{1,0:T(8,128)(2,1)S(1)} %get-tuple-element.10.refs_1_), channel_id=1, source_target_pairs={{0,6},{2,4},{4,2},{6,0},{1,7},{3,5},{5,3},{7,1},{8,14},{10,12},{12... | collective-permute-start | bytes 786440 | tf_op jit(solution)/shard_map/ppermute | solution.py:281
  43.1 10.4 %collective-permute-start.8 = (bf16[16,8192]{1,0:T(8,128)(2,1)S(1)}, bf16[16,8192]{1,0:T(8,128)(2,1)S(1)}, u32[]{:S(2)}, u32[]{:S(2)}) collective-permute-start(bf16[16,8192]{1,0:T(8,128)(2,1)S(1)} %get-tuple-element.10.refs_1_), channel_id=1, source_target_pairs={{0,2},{2,0},{4,6},{6,4},{1,3},{3,1},{5,7},{7,5},{8,10},{10,8},{12,... | collective-permute-start | bytes 786440 | tf_op jit(solution)/shard_map/ppermute | solution.py:280
  43.3 11.9 %collective-permute-start.9 = (bf16[16,8192]{1,0:T(8,128)(2,1)S(1)}, bf16[16,8192]{1,0:T(8,128)(2,1)S(1)}, u32[]{:S(2)}, u32[]{:S(2)}) collective-permute-start(bf16[16,8192]{1,0:T(8,128)(2,1)S(1)} %get-tuple-element.8.refs_0_), channel_id=1, source_target_pairs={{0,6},{2,4},{4,2},{6,0},{1,7},{3,5},{5,3},{7,1},{8,14},{10,12},{12... | collective-permute-start | bytes 786440 | tf_op jit(solution)/shard_map/ppermute | solution.py:281
  44.0 13.5 %collective-permute-start.6 = (bf16[16,8192]{1,0:T(8,128)(2,1)S(1)}, bf16[16,8192]{1,0:T(8,128)(2,1)S(1)}, u32[]{:S(2)}, u32[]{:S(2)}) collective-permute-start(bf16[16,8192]{1,0:T(8,128)(2,1)S(1)} %get-tuple-element.8.refs_0_), channel_id=1, source_target_pairs={{0,1},{1,0},{2,3},{3,2},{4,5},{5,4},{6,7},{7,6},{8,9},{9,8},{10,11... | collective-permute-start | bytes 786440 | tf_op jit(solution)/shard_map/ppermute | solution.py:278
  52.1 5.4 %collective-permute-start.7 = (bf16[16,8192]{1,0:T(8,128)(2,1)S(1)}, bf16[16,8192]{1,0:T(8,128)(2,1)S(1)}, u32[]{:S(2)}, u32[]{:S(2)}) collective-permute-start(bf16[16,8192]{1,0:T(8,128)(2,1)S(1)} %get-tuple-element.10.refs_1_), channel_id=1, source_target_pairs={{0,1},{1,0},{2,3},{3,2},{4,5},{5,4},{6,7},{7,6},{8,9},{9,8},{10,11... | collective-permute-start | bytes 786440 | tf_op jit(solution)/shard_map/ppermute | solution.py:278
  52.2 6.7 %collective-permute-start.5 = (bf16[16,8192]{1,0:T(8,128)(2,1)S(1)}, bf16[16,8192]{1,0:T(8,128)(2,1)S(1)}, u32[]{:S(2)}, u32[]{:S(2)}) collective-permute-start(bf16[16,8192]{1,0:T(8,128)(2,1)S(1)} %collective-permute-done.4.two_ref), channel_id=1, source_target_pairs={{0,2},{2,0},{4,6},{6,4},{1,3},{3,1},{5,7},{7,5},{8,10},{10,8},{12,... | collective-permute-start | bytes 786440 | tf_op jit(solution)/shard_map/ppermute | solution.py:283
  53.4 7.1 %collective-permute-start.3 = (bf16[16,8192]{1,0:T(8,128)(2,1)S(1)}, bf16[16,8192]{1,0:T(8,128)(2,1)S(1)}, u32[]{:S(2)}, u32[]{:S(2)}) collective-permute-start(bf16[16,8192]{1,0:T(8,128)(2,1)S(1)} %get-tuple-element.9.one_ref), channel_id=1, source_target_pairs={{0,6},{2,4},{4,2},{6,0},{1,7},{3,5},{5,3},{7,1},{8,14},{10,12},{12... | collective-permute-start | bytes 786440 | tf_op jit(solution)/shard_map/ppermute | solution.py:283
  55.3 8.2 %collective-permute-start.11 = (bf16[32,8192]{1,0:T(8,128)(2,1)S(1)}, bf16[32,8192]{1,0:T(8,128)(2,1)S(1)}, u32[]{:S(2)}, u32[]{:S(2)}) collective-permute-start(bf16[32,8192]{1,0:T(8,128)(2,1)S(1)} %join.2.refs_4_), channel_id=1, source_target_pairs={{0,1},{1,0},{2,3},{3,2},{4,5},{5,4},{6,7},{7,6},{8,9},{9,8},{10,11... | collective-permute-start | bytes 1572872 | tf_op jit(solution)/shard_map/ppermute | solution.py:278
  57.4 6.0 %collective-permute-start.12 = (bf16[32,8192]{1,0:T(8,128)(2,1)S(1)}, bf16[32,8192]{1,0:T(8,128)(2,1)S(1)}, u32[]{:S(2)}, u32[]{:S(2)}) collective-permute-start(bf16[32,8192]{1,0:T(8,128)(2,1)S(1)} %join.3.refs_5_), channel_id=1, source_target_pairs={{0,1},{1,0},{2,3},{3,2},{4,5},{5,4},{6,7},{7,6},{8,9},{9,8},{10,11... | collective-permute-start | bytes 1572872 | tf_op jit(solution)/shard_map/ppermute | solution.py:278
  60.6 4.4 %collective-permute-start.10 = (bf16[32,8192]{1,0:T(8,128)(2,1)S(1)}, bf16[32,8192]{1,0:T(8,128)(2,1)S(1)}, u32[]{:S(2)}, u32[]{:S(2)}) collective-permute-start(bf16[32,8192]{1,0:T(8,128)(2,1)S(1)} %get-tuple-element.11.refs_2_), channel_id=1, source_target_pairs={{0,1},{1,0},{2,3},{3,2},{4,5},{5,4},{6,7},{7,6},{8,9},{9,8},{10,11... | collective-permute-start | bytes 1572872 | tf_op jit(solution)/shard_map/ppermute | solution.py:278
